TPU v7x, 32 devices: a whole 2x2x4 slice. The times are simulated.
32 devices in a mesh: seg: 4 (over y, x), seq: 2 (over core), chan: 4 (over z).
Axes of the slice: x: 2, y: 2, z: 4, core: 2. Of those that a mesh axis runs over, the one named last changes fastest.
Arguments:
- sequence_elements: bfloat16 [4, 1024, 2048], P('seg', ('seq', 'chan')), may hold values from -6 to 6
- segment_predecessor_entries: float32 [4, 2, 2048], P('seg'), may hold values from -6 to 6
- opening_recurrences: float32 [4, 64, 2048], P('seg'), may hold values from -12 to 12
- first_layernorm_gain: float32 [2048], replicated, may hold values from 0.5 to 1.5
- first_layernorm_shift_term: float32 [2048], replicated, may hold values from -2 to 2
- lag_blend_coefficients: float32 [2048, 6], replicated, may hold values from 0 to 1
- lag_narrowing_factor: bfloat16 [2048, 160], replicated, may hold values from -0.125 to 0.125
- lag_widening_factors: bfloat16 [2048, 160], replicated, may hold values from -1 to 1
- fading_exponent_baseline: float32 [2048], replicated, as said below
- fading_narrowing_factor: bfloat16 [2048, 64], replicated, may hold values from -0.125 to 0.125
- fading_widening_factor: bfloat16 [2048, 64], replicated, may hold values from -0.75 to 0.75
- present_reward: float32 [2048], replicated, may hold values from -3 to 3
- acceptor_projection: bfloat16 [2048, 2048], P('seg'), may hold values from -0.125 to 0.125
- address_projection: bfloat16 [2048, 2048], P('seg'), may hold values from -0.125 to 0.125
- content_projection: bfloat16 [2048, 2048], P('seg'), may hold values from -0.125 to 0.125
- valve_projection: bfloat16 [2048, 2048], P('seg'), may hold values from -0.125 to 0.125
- timemix_result_projection: bfloat16 [2048, 2048], P('seg'), may hold values from -0.25 to 0.25
- subspace_cluster_gain: float32 [2048], replicated, may hold values from 0.5 to 1.5
- subspace_cluster_shift_term: float32 [2048], replicated, may hold values from -2 to 2
- second_layernorm_gain: float32 [2048], replicated, may hold values from 0.5 to 1.5
- second_layernorm_shift_term: float32 [2048], replicated, may hold values from -2 to 2
- feedforward_lag_blends: float32 [2048, 2], replicated, may hold values from 0 to 1
- feedforward_address_projection: bfloat16 [2048, 7168], P('seg', 'chan'), may hold values from -0.125 to 0.125
- feedforward_acceptor_projection: bfloat16 [2048, 2048], P('seg'), may hold values from -0.125 to 0.125
- feedforward_content_projection: bfloat16 [2048, 7168], P('seg', 'chan'), may hold values from -0.0625 to 0.0625
- result_adjoint: bfloat16 [4, 1024, 2048], P('seg', ('seq', 'chan')), may hold values from -6 to 6
- final_recurrence_adjoint: float32 [4, 8, 64, 2048], P('seg', ('seq', 'chan')), may hold values from -0.8 to 0.8
Outputs:
- output: bfloat16 [4, 1024, 2048], P('seg', ('seq', 'chan'))
- end_states: float32 [4, 8, 64, 2048], P('seg', ('seq', 'chan'))
- input_grad: float32 [4, 1024, 2048], P('seg', ('seq', 'chan'))
- grad_att_norm_gain: float32 [2048], P(('seg', 'seq', 'chan'))
- grad_att_norm_bias: float32 [2048], P(('seg', 'seq', 'chan'))
- grad_token_shift_mix: float32 [2048, 6], P(('seg', 'seq', 'chan'))
- shift_down_gradient: float32 [2048, 160], P(('seg', 'seq', 'chan'))
- shift_up_gradient: float32 [2048, 160], P(('seg', 'seq', 'chan'))
- grad_decay_base: float32 [2048], P(('seg', 'seq', 'chan'))
- grad_decay_down: float32 [2048, 64], P(('seg', 'seq', 'chan'))
- grad_decay_up: float32 [2048, 64], P(('seg', 'seq', 'chan'))
- reward_coefficient_sensitivity: float32 [2048], P(('seg', 'seq', 'chan'))
- grad_w_recept: float32 [2048, 2048], P(('seg', 'seq', 'chan'))
- grad_w_key: float32 [2048, 2048], P(('seg', 'seq', 'chan'))
- grad_w_value: float32 [2048, 2048], P(('seg', 'seq', 'chan'))
- grad_w_gate: float32 [2048, 2048], P(('seg', 'seq', 'chan'))
- grad_w_output: float32 [2048, 2048], P(('seg', 'seq', 'chan'))
- grad_group_gain: float32 [2048], P(('seg', 'seq', 'chan'))
- grad_group_bias: float32 [2048], P(('seg', 'seq', 'chan'))
- grad_ffn_norm_gain: float32 [2048], P(('seg', 'seq', 'chan'))
- grad_ffn_norm_bias: float32 [2048], P(('seg', 'seq', 'chan'))
- grad_ffn_shift_mix: float32 [2048, 2], P(('seg', 'seq', 'chan'))
- grad_ffn_key: float32 [2048, 7168], P(('seg', 'seq'), 'chan')
- grad_ffn_recept: float32 [2048, 2048], P(('seg', 'seq', 'chan'))
- grad_ffn_value: float32 [2048, 7168], P(('seg', 'seq'), 'chan')
Inputs may be any that keep to these rules, and one draw needn't show every extreme that they name: `fading_exponent_baseline`: offsets of the decay's inner exponent lie between ln 0.1 - ln 1024 and ln 0.1.
All inputs are finite; a program needn't handle non-finite values.
Results may differ from a plain program's by a relative error of at most 0.03.
Values may be sent and summed in bfloat16 or wider, within the bound.
No kernel may reach another device: no remote copies, remote signals or barrier semaphores. Data moves between devices by JAX's collectives and lax.ppermute only.
A program may use at most 384 MiB of HBM per device.

v0:
```python
import math

import jax
import jax.numpy as jnp
from jax import lax
from jax.sharding import PartitionSpec as P

SUBSPACE_SIZE = 64


EXACT_ARITHMETIC = lax.Precision.HIGHEST
LAYER_EPSILON = 1e-05
GROUP_EPSILON = 0.00064


def from_behind(block, axis, distance):
    devices = range(lax.axis_size(axis))
    route = [(i - distance, i) for i in devices if i - distance in devices]
    return lax.ppermute(block, axis, route)


def entering(value, axis, join, neutral):
    count, mine = (lax.axis_size(axis), lax.axis_index(axis))
    pieces = jax.tree.map(lambda part: lax.all_gather(part, axis), value)
    running = jax.tree.map(
        lambda part, zero: jnp.full_like(part, 0) + jnp.asarray(zero, part.dtype), value, neutral
    )

    def entering_hop(position, running):
        longer = join(running, jax.tree.map(lambda part: part[position], pieces))
        return jax.tree.map(lambda new, old: jnp.where(position < mine, new, old), longer, running)

    return lax.fori_loop(0, count - 1, entering_hop, running)


def carried_in(x, axis, combine, identity):
    peers, here = (lax.axis_size(axis), lax.axis_index(axis))
    everything = jax.tree.map(
        lambda part, kind: lax.all_gather(part.astype(kind), axis),
        x,
        jax.tree.map(lambda a: jnp.bfloat16 if a.dtype == jnp.float32 else a.dtype, x),
    )
    start = jax.tree.map(
        lambda part, zero: jnp.broadcast_to(jnp.asarray(zero, part.dtype), part.shape), x, identity
    )

    def carried_hop(k, before):
        at = peers - 1 - k
        reached = at > here
        new = combine(
            before, jax.tree.map(lambda part, own: part[at].astype(own.dtype), everything, x)
        )
        return jax.tree.map(lambda a, b: jnp.where(reached, a, b), new, before)

    return lax.fori_loop(0, peers, carried_hop, start)


def rounded_value(values):
    return values + lax.stop_gradient(values.astype(jnp.bfloat16).astype(jnp.float32) - values)


def product_in(left_side, right_side):
    return jnp.dot(left_side, right_side, preferred_element_type=jnp.float32)


def product_out(left_side, right_side):
    return lax.dot_general(
        left_side, right_side, (((1,), (1,)), ((), ())), preferred_element_type=jnp.float32
    )


def product_left(left_side, right_side):
    return lax.dot_general(
        left_side, right_side, (((0,), (0,)), ((), ())), preferred_element_type=jnp.float32
    )


def layer_norm(values, scale_gain, shift_bias):
    center = values - jnp.mean(values, -1, keepdims=True)
    spread = jnp.mean(center * center, -1, keepdims=True)
    return center * lax.rsqrt(spread + LAYER_EPSILON) * scale_gain + shift_bias


def token_mixing(
    normed_input,
    previous_row,
    shift_mixing,
    lag_narrowing_factor,
    lag_widening_factors,
    fading_exponent_baseline,
    fading_narrowing_factor,
    fading_widening_factor,
):
    number_tokens, embedding_breadth = normed_input.shape
    rank_dimension = lag_widening_factors.shape[1] // 5
    shift_difference = jnp.concatenate([previous_row[None, :], normed_input[:-1]], 0) - normed_input
    shift_low_input = rounded_value(normed_input + shift_difference * shift_mixing[:, 0])
    shift_low_middle = rounded_value(
        jnp.tanh(jnp.dot(shift_low_input, lag_narrowing_factor, precision=EXACT_ARITHMETIC))
    )
    shift_modifiers = jnp.einsum(
        "phy,shy->hps",
        shift_low_middle.reshape(number_tokens, 5, rank_dimension),
        lag_widening_factors.reshape(embedding_breadth, 5, rank_dimension),
        precision=EXACT_ARITHMETIC,
    )
    mixed_rows = [
        normed_input + shift_difference * (shift_mixing[:, column + 1] + shift_modifiers[column])
        for column in range(5)
    ]
    decay_mid = rounded_value(
        jnp.tanh(
            jnp.dot(
                rounded_value(mixed_rows[0]), fading_narrowing_factor, precision=EXACT_ARITHMETIC
            )
        )
    )
    fading_exponent_level = -jnp.exp(
        fading_exponent_baseline
        + lax.dot_general(
            decay_mid, fading_widening_factor, (((1,), (1,)), ((), ())), precision=EXACT_ARITHMETIC
        )
    )
    return (mixed_rows[1], mixed_rows[2], mixed_rows[3], mixed_rows[4], fading_exponent_level)


def channel_mix(normed_input, previous_row, shift_mixing):
    shift_difference = jnp.concatenate([previous_row[None, :], normed_input[:-1]], 0) - normed_input
    return (
        normed_input + shift_difference * shift_mixing[:, 0],
        normed_input + shift_difference * shift_mixing[:, 1],
    )


def group_gate(wkv_rows, gate_raw, scale_gain, shift_bias):
    number_tokens, subspace_count, head_size = wkv_rows.shape
    center = wkv_rows - jnp.mean(wkv_rows, -1, keepdims=True)
    spread = jnp.mean(center * center, -1, keepdims=True)
    grouped = (center * lax.rsqrt(spread + GROUP_EPSILON)).reshape(
        number_tokens, subspace_count * head_size
    )
    return (grouped * scale_gain + shift_bias) * jax.nn.silu(gate_raw)


def block_step(handed_recurrence, block_items):
    recurrence_content, subspace_reward = handed_recurrence
    acceptor_entries, address_entries, content_entries, fading_exponent_entries = block_items
    length = acceptor_entries.shape[0]
    triangle = jnp.tril(jnp.ones((length, length), jnp.float32))
    strict_mask = jnp.arange(length)[:, None] > jnp.arange(length)[None, :]
    inclusive = jnp.einsum(
        "ts,shk->thk", triangle, fading_exponent_entries, precision=EXACT_ARITHMETIC
    )
    exclusive = inclusive - fading_exponent_entries
    decay_sum = inclusive[-1]
    recurrence_feed_text = jnp.einsum(
        "thk,khj->thj",
        acceptor_entries * jnp.exp(exclusive),
        recurrence_content,
        precision=EXACT_ARITHMETIC,
    )
    spacing = jnp.minimum(exclusive[:, None] - inclusive[None, :], 0.0)
    weights = jnp.where(strict_mask[:, :, None, None], jnp.exp(spacing), 0.0)
    scores = jnp.einsum(
        "thk,tshk->tsh",
        acceptor_entries,
        weights * address_entries[None],
        precision=EXACT_ARITHMETIC,
    )
    present_content = jnp.sum(acceptor_entries * subspace_reward * address_entries, -1)
    layer_feed_text = (
        jnp.einsum("tsh,shj->thj", scores, content_entries, precision=EXACT_ARITHMETIC)
        + present_content[:, :, None] * content_entries
    )
    update = jnp.einsum(
        "shk,shj->khj",
        address_entries * jnp.exp(decay_sum[None] - inclusive),
        content_entries,
        precision=EXACT_ARITHMETIC,
    )
    revised_recurrence = jnp.transpose(jnp.exp(decay_sum))[:, :, None] * recurrence_content + update
    return ((revised_recurrence, subspace_reward), recurrence_feed_text + layer_feed_text)


def mixing_states(
    acceptor_entries,
    address_entries,
    content_entries,
    fading_exponent_entries,
    subspace_reward,
    opening_recurrence,
):
    number_tokens, subspace_count, head_size = acceptor_entries.shape
    length = math.gcd(number_tokens, 32)

    def to_blocks(values):
        return values.reshape(number_tokens // length, length, subspace_count, head_size)

    handed_recurrence, outputs = lax.scan(
        jax.checkpoint(block_step),
        (opening_recurrence, subspace_reward),
        (
            to_blocks(acceptor_entries),
            to_blocks(address_entries),
            to_blocks(content_entries),
            to_blocks(fading_exponent_entries),
        ),
    )
    return outputs.reshape(number_tokens, subspace_count, head_size)


def chain_map(address_entries, content_entries, fading_exponent_entries):
    number_tokens = address_entries.shape[0]
    triangle = jnp.tril(jnp.ones((number_tokens, number_tokens), jnp.float32))
    inclusive = jnp.einsum(
        "ts,shk->thk", triangle, fading_exponent_entries, precision=EXACT_ARITHMETIC
    )
    decay_sum = inclusive[-1]
    update = jnp.einsum(
        "shk,shj->khj",
        address_entries * jnp.exp(decay_sum[None] - inclusive),
        content_entries,
        precision=EXACT_ARITHMETIC,
    )
    return (jnp.transpose(jnp.exp(decay_sum))[:, :, None], update)


def combine_maps(earlier, later):
    return (earlier[0] * later[0], later[0] * earlier[1] + later[1])


def pass_last(last_row, first_row):
    received = from_behind(last_row, ("seq", "chan"), 1)
    return jnp.where(lax.axis_index(("seq", "chan")) == 0, first_row, received)


def pass_first(first_grad):
    return from_behind(first_grad, ("seq", "chan"), -1)


def reduce_ffn(grad_ffn_key, grad_ffn_value):
    return (
        lax.psum_scatter(
            grad_ffn_key.astype(jnp.bfloat16), ("seg", "seq"), scatter_dimension=0, tiled=True
        ).astype(jnp.float32),
        lax.psum_scatter(
            grad_ffn_value.astype(jnp.bfloat16), ("seg", "seq"), scatter_dimension=0, tiled=True
        ).astype(jnp.float32),
    )


def on_device(
    sequence_elements,
    segment_predecessor_entries,
    opening_recurrences,
    first_layernorm_gain,
    first_layernorm_shift_term,
    lag_blend_coefficients,
    lag_narrowing_factor,
    lag_widening_factors,
    fading_exponent_baseline,
    fading_narrowing_factor,
    fading_widening_factor,
    present_reward,
    acceptor_projection,
    address_projection,
    content_projection,
    valve_projection,
    timemix_result_projection,
    subspace_cluster_gain,
    subspace_cluster_shift_term,
    second_layernorm_gain,
    second_layernorm_shift_term,
    feedforward_lag_blends,
    feedforward_address_projection,
    feedforward_acceptor_projection,
    feedforward_content_projection,
    result_adjoint,
    final_recurrence_adjoint,
):
    inputs = sequence_elements[0].astype(jnp.float32)
    number_tokens, embedding_breadth = inputs.shape
    subspace_count = embedding_breadth // SUBSPACE_SIZE
    (
        full_recept,
        full_key,
        full_value,
        full_gate,
        full_output,
        full_ffn_recept,
        part_ffn_key,
        part_ffn_value,
    ) = (
        lax.all_gather(acceptor_projection, "seg", axis=0, tiled=True),
        lax.all_gather(address_projection, "seg", axis=0, tiled=True),
        lax.all_gather(content_projection, "seg", axis=0, tiled=True),
        lax.all_gather(valve_projection, "seg", axis=0, tiled=True),
        lax.all_gather(timemix_result_projection, "seg", axis=0, tiled=True),
        lax.all_gather(feedforward_acceptor_projection, "seg", axis=0, tiled=True),
        lax.all_gather(feedforward_address_projection, "seg", axis=0, tiled=True),
        lax.all_gather(feedforward_content_projection, "seg", axis=0, tiled=True),
    )
    normed_input, norm_pull = jax.vjp(
        layer_norm, inputs, first_layernorm_gain, first_layernorm_shift_term
    )
    previous_row = pass_last(normed_input[-1], segment_predecessor_entries[0, 0])
    mixed_out, mix_pull = jax.vjp(
        token_mixing,
        normed_input,
        previous_row,
        lag_blend_coefficients,
        lag_narrowing_factor.astype(jnp.float32),
        lag_widening_factors.astype(jnp.float32),
        fading_exponent_baseline,
        fading_narrowing_factor.astype(jnp.float32),
        fading_widening_factor.astype(jnp.float32),
    )
    key_in = mixed_out[0].astype(jnp.bfloat16)
    value_in = mixed_out[1].astype(jnp.bfloat16)
    recept_in = mixed_out[2].astype(jnp.bfloat16)
    gate_in = mixed_out[3].astype(jnp.bfloat16)

    def to_heads(values):
        return (
            values.astype(jnp.bfloat16)
            .astype(jnp.float32)
            .reshape(number_tokens, subspace_count, SUBSPACE_SIZE)
        )

    acceptor_entries = to_heads(product_in(recept_in, full_recept))
    address_entries = to_heads(product_in(key_in, full_key))
    content_entries = to_heads(product_in(value_in, full_value))
    gate_raw = product_in(gate_in, full_gate)
    fading_exponent_entries = mixed_out[4].reshape(number_tokens, subspace_count, SUBSPACE_SIZE)
    subspace_reward = present_reward.reshape(subspace_count, SUBSPACE_SIZE)
    local_map, chain_pull = jax.vjp(
        chain_map, address_entries, content_entries, fading_exponent_entries
    )
    identity = (jnp.ones_like(local_map[0]), jnp.zeros_like(local_map[1]))
    before = entering((local_map[0], local_map[1]), ("seq", "chan"), combine_maps, identity)
    opening_recurrence = (
        before[0] * opening_recurrences[0].reshape(SUBSPACE_SIZE, subspace_count, SUBSPACE_SIZE)
        + before[1]
    )
    end_memory = local_map[0] * opening_recurrence + local_map[1]
    wkv_rows, state_pullback = jax.vjp(
        mixing_states,
        acceptor_entries,
        address_entries,
        content_entries,
        fading_exponent_entries,
        subspace_reward,
        opening_recurrence,
    )
    gated_f32, gate_pull = jax.vjp(
        group_gate, wkv_rows, gate_raw, subspace_cluster_gain, subspace_cluster_shift_term
    )
    gated_rows = gated_f32.astype(jnp.bfloat16)
    residual = inputs + product_in(gated_rows, full_output)
    ffn_normed, ffn_norm_pull = jax.vjp(
        layer_norm, residual, second_layernorm_gain, second_layernorm_shift_term
    )
    ffn_previous = pass_last(ffn_normed[-1], segment_predecessor_entries[0, 1])
    ffn_mixed, ffn_mix_pull = jax.vjp(channel_mix, ffn_normed, ffn_previous, feedforward_lag_blends)
    ffn_key_in = ffn_mixed[0].astype(jnp.bfloat16)
    ffn_recept_in = ffn_mixed[1].astype(jnp.bfloat16)
    group_keys = lax.all_gather(ffn_key_in, "chan", axis=0, tiled=True)
    hidden = product_in(group_keys, part_ffn_key)
    squared = jnp.square(jax.nn.relu(hidden)).astype(jnp.bfloat16)
    ffn_values = lax.psum_scatter(
        product_out(squared, part_ffn_value).astype(jnp.bfloat16),
        "chan",
        scatter_dimension=0,
        tiled=True,
    ).astype(jnp.float32)
    ffn_gate = jax.nn.sigmoid(product_in(ffn_recept_in, full_ffn_recept))
    result = residual + ffn_gate * ffn_values
    cotangent = result_adjoint[0].astype(jnp.float32)
    d_values = (cotangent * ffn_gate).astype(jnp.bfloat16)
    d_ffn_gate = (cotangent * ffn_values * ffn_gate * (1.0 - ffn_gate)).astype(jnp.bfloat16)
    d_ffn_recept_in = product_out(d_ffn_gate, full_ffn_recept)
    group_dvalues = lax.all_gather(d_values, "chan", axis=0, tiled=True)
    d_hidden = (product_in(group_dvalues, part_ffn_value) * 2.0 * jax.nn.relu(hidden)).astype(
        jnp.bfloat16
    )
    grad_ffn_value = product_left(group_dvalues, squared)
    grad_ffn_key = product_left(group_keys, d_hidden)
    d_ffn_key_in = lax.psum_scatter(
        product_out(d_hidden, part_ffn_key).astype(jnp.bfloat16),
        "chan",
        scatter_dimension=0,
        tiled=True,
    ).astype(jnp.float32)
    d_ffn_normed, d_ffn_previous, grad_ffn_shift_mix = ffn_mix_pull((d_ffn_key_in, d_ffn_recept_in))
    d_ffn_normed = d_ffn_normed.at[-1].add(pass_first(d_ffn_previous))
    d_residual_norm, grad_ffn_norm_gain, grad_ffn_norm_bias = ffn_norm_pull(d_ffn_normed)
    d_residual = cotangent + d_residual_norm
    d_attention = d_residual.astype(jnp.bfloat16)
    mixture_row_gradient, d_gate_raw, grad_group_gain, grad_group_bias = gate_pull(
        product_out(d_attention, full_output)
    )
    d_gate = d_gate_raw.astype(jnp.bfloat16)
    d_gate_in = product_out(d_gate, full_gate)
    (
        received_gradient,
        local_key_gradient,
        local_value_gradient,
        local_logdecay_gradient,
        present_reward_sensitivity,
        start_gradient,
    ) = state_pullback(mixture_row_gradient)
    end_cot = final_recurrence_adjoint[0, 0].reshape(SUBSPACE_SIZE, subspace_count, SUBSPACE_SIZE)
    after = carried_in(
        (local_map[0], local_map[0] * end_cot + start_gradient),
        ("seq", "chan"),
        combine_maps,
        identity,
    )
    d_end = end_cot + after[1]
    d_key_chain, d_value_chain, d_log_chain = chain_pull(
        (jnp.sum(d_end * opening_recurrence, -1, keepdims=True), d_end)
    )

    def flatten(values):
        return values.reshape(number_tokens, embedding_breadth)

    d_recept = flatten(received_gradient).astype(jnp.bfloat16)
    d_key = flatten(local_key_gradient + d_key_chain).astype(jnp.bfloat16)
    d_value = flatten(local_value_gradient + d_value_chain).astype(jnp.bfloat16)
    (
        d_normed,
        d_previous,
        grad_shift_mix,
        shift_down_gradient,
        shift_up_gradient,
        grad_decay_base,
        grad_decay_down,
        grad_decay_up,
    ) = mix_pull(
        (
            product_out(d_key, full_key),
            product_out(d_value, full_value),
            product_out(d_recept, full_recept),
            d_gate_in,
            flatten(local_logdecay_gradient + d_log_chain),
        )
    )
    d_normed = d_normed.at[-1].add(pass_first(d_previous))
    d_inputs_norm, grad_att_norm_gain, grad_att_norm_bias = norm_pull(d_normed)
    input_grad = d_residual + d_inputs_norm
    reward_coefficient_sensitivity = present_reward_sensitivity.reshape(embedding_breadth)
    grad_ffn_recept = product_left(ffn_recept_in, d_ffn_gate)
    grad_output = product_left(gated_rows, d_attention)
    grad_gate = product_left(gate_in, d_gate)
    grad_recept = product_left(recept_in, d_recept)
    grad_key = product_left(key_in, d_key)
    grad_value = product_left(value_in, d_value)
    summed = (
        lax.psum_scatter(
            grad_att_norm_gain, ("seg", "seq", "chan"), scatter_dimension=0, tiled=True
        ),
        lax.psum_scatter(
            grad_att_norm_bias, ("seg", "seq", "chan"), scatter_dimension=0, tiled=True
        ),
        lax.psum_scatter(grad_shift_mix, ("seg", "seq", "chan"), scatter_dimension=0, tiled=True),
        lax.psum_scatter(
            shift_down_gradient, ("seg", "seq", "chan"), scatter_dimension=0, tiled=True
        ),
        lax.psum_scatter(
            shift_up_gradient, ("seg", "seq", "chan"), scatter_dimension=0, tiled=True
        ),
        lax.psum_scatter(grad_decay_base, ("seg", "seq", "chan"), scatter_dimension=0, tiled=True),
        lax.psum_scatter(grad_decay_down, ("seg", "seq", "chan"), scatter_dimension=0, tiled=True),
        lax.psum_scatter(grad_decay_up, ("seg", "seq", "chan"), scatter_dimension=0, tiled=True),
        lax.psum_scatter(
            reward_coefficient_sensitivity, ("seg", "seq", "chan"), scatter_dimension=0, tiled=True
        ),
        lax.psum_scatter(grad_recept, ("seg", "seq", "chan"), scatter_dimension=0, tiled=True),
        lax.psum_scatter(grad_key, ("seg", "seq", "chan"), scatter_dimension=0, tiled=True),
        lax.psum_scatter(grad_value, ("seg", "seq", "chan"), scatter_dimension=0, tiled=True),
        lax.psum_scatter(grad_gate, ("seg", "seq", "chan"), scatter_dimension=0, tiled=True),
        lax.psum_scatter(grad_output, ("seg", "seq", "chan"), scatter_dimension=0, tiled=True),
        lax.psum_scatter(grad_group_gain, ("seg", "seq", "chan"), scatter_dimension=0, tiled=True),
        lax.psum_scatter(grad_group_bias, ("seg", "seq", "chan"), scatter_dimension=0, tiled=True),
        lax.psum_scatter(
            grad_ffn_norm_gain, ("seg", "seq", "chan"), scatter_dimension=0, tiled=True
        ),
        lax.psum_scatter(
            grad_ffn_norm_bias, ("seg", "seq", "chan"), scatter_dimension=0, tiled=True
        ),
        lax.psum_scatter(
            grad_ffn_shift_mix, ("seg", "seq", "chan"), scatter_dimension=0, tiled=True
        ),
        lax.psum_scatter(grad_ffn_recept, ("seg", "seq", "chan"), scatter_dimension=0, tiled=True),
    )
    mixer_sums = summed[:12]
    channel_sums = summed[12:]
    ffn_pair = reduce_ffn(grad_ffn_key, grad_ffn_value)
    return (
        result.astype(jnp.bfloat16)[None],
        end_memory.reshape(SUBSPACE_SIZE, embedding_breadth)[None, None],
        input_grad[None],
        mixer_sums[0],
        mixer_sums[1],
        mixer_sums[2],
        mixer_sums[3],
        mixer_sums[4],
        mixer_sums[5],
        mixer_sums[6],
        mixer_sums[7],
        mixer_sums[8],
        mixer_sums[9],
        mixer_sums[10],
        mixer_sums[11],
        channel_sums[0],
        channel_sums[1],
        channel_sums[2],
        channel_sums[3],
        channel_sums[4],
        channel_sums[5],
        channel_sums[6],
        ffn_pair[0],
        channel_sums[7],
        ffn_pair[1],
    )


def solution(mesh):
    placed = (
        P("seg", ("seq", "chan"), None),
        P("seg", None, None),
        P("seg", None, None),
        P(),
        P(),
        P(),
        P(),
        P(),
        P(),
        P(),
        P(),
        P(),
        P("seg", None),
        P("seg", None),
        P("seg", None),
        P("seg", None),
        P("seg", None),
        P(),
        P(),
        P(),
        P(),
        P(),
        P("seg", "chan"),
        P("seg", None),
        P("seg", "chan"),
        P("seg", ("seq", "chan"), None),
        P("seg", ("seq", "chan"), None, None),
    )
    return jax.shard_map(
        on_device,
        mesh=mesh,
        in_specs=placed,
        out_specs=(
            P("seg", ("seq", "chan"), None),
            P("seg", ("seq", "chan"), None, None),
            P("seg", ("seq", "chan"), None),
            P(("seg", "seq", "chan")),
            P(("seg", "seq", "chan")),
            P(("seg", "seq", "chan"), None),
            P(("seg", "seq", "chan"), None),
            P(("seg", "seq", "chan"), None),
            P(("seg", "seq", "chan")),
            P(("seg", "seq", "chan"), None),
            P(("seg", "seq", "chan"), None),
            P(("seg", "seq", "chan")),
            P(("seg", "seq", "chan"), None),
            P(("seg", "seq", "chan"), None),
            P(("seg", "seq", "chan"), None),
            P(("seg", "seq", "chan"), None),
            P(("seg", "seq", "chan"), None),
            P(("seg", "seq", "chan")),
            P(("seg", "seq", "chan")),
            P(("seg", "seq", "chan")),
            P(("seg", "seq", "chan")),
            P(("seg", "seq", "chan"), None),
            P(("seg", "seq"), "chan"),
            P(("seg", "seq", "chan"), None),
            P(("seg", "seq"), "chan"),
        ),
        check_vma=False,
    )
```

profile of v0, /device:TPU:1, one launch (start us, length us, event | category | flops | bytes accessed | tf_op | source)
XLA Modules:
  0.0 4871.1 jit_solution(5571883972634747086)
XLA Ops:
  32.3 67.3 %all-gather.19.cloned.1.call-done = bf16[2048,2048]{1,0:T(8,128)(2,1)} async-done(((bf16[512,2048]{1,0:T(8,128)(2,1)}), bf16[2048,2048]{1,0:T(8,128)(2,1)}) %all-gather.19.cloned.1.call-update) | async-done | bytes 8388624 | tf_op jit(solution)/shard_map/all_gather | solution.py:296
  107.7 81.5 %all-gather.21.cloned.1.call-done = bf16[2048,2048]{1,0:T(8,128)(2,1)} async-done(((bf16[512,2048]{1,0:T(8,128)(2,1)}), bf16[2048,2048]{1,0:T(8,128)(2,1)}) %all-gather.21.cloned.1.call-update) | async-done | bytes 8388624 | tf_op jit(solution)/shard_map/all_gather | solution.py:295
  292.4 70.2 %all-gather.39.cloned.1.call-done = f32[512,32,64]{2,1,0:T(8,128)} async-done(((f32[64,32,64]{2,1,0:T(8,128)}), f32[512,32,64]{2,1,0:T(8,128)}) %all-gather.39.cloned.1.call-update) | async-done | bytes 4194320 | tf_op jit(solution)/shard_map/all_gather | solution.py:24
  382.9 225.5 %while.81 = (s32[]{:T(128)}, f32[64,32,64]{0,2,1:T(8,128)S(1)}, f32[4,32,32,64]{3,1,2,0:T(8,128)}, f32[4,64,32,64]{1,3,2,0:T(8,128)}, f32[4,32,64]{2,1,0:T(8,128...) while((s32[]{:T(128)}, f32[64,32,64]{0,2,1:T(8,128)S(1)}, ...), condition=%wide.region_6.7_spmd.clone.clone, body=%wide.region_4.6_spmd.clone.sunk.clone | while | flops 185404480 | bytes 35755180 | solution.py:199
  644.7 42.1 all-gather.31.cloned.1.call-done
  696.4 69.9 %all-gather.35.cloned.1.call-done = bf16[2048,1792]{1,0:T(8,128)(2,1)} async-done(((bf16[512,1792]{1,0:T(8,128)(2,1)}), bf16[2048,1792]{1,0:T(8,128)(2,1)}) %all-gather.35.cloned.1.call-update) | async-done | bytes 7340048 | tf_op jit(solution)/shard_map/all_gather | solution.py:301
  775.9 79.7 %all-gather.29.cloned.1.call-done = bf16[2048,2048]{1,0:T(8,128)(2,1)} async-done(((bf16[512,2048]{1,0:T(8,128)(2,1)}), bf16[2048,2048]{1,0:T(8,128)(2,1)}) %all-gather.29.cloned.1.call-update) | async-done | bytes 8388624 | tf_op jit(solution)/shard_map/all_gather | solution.py:299
  855.6 46.0 reduce-scatter.21.cloned.1.call-done
  908.4 45.3 all-gather.37.cloned.1.call-done
  1058.5 476.2 %while.83 = (s32[]{:T(128)}, f32[64,32,64]{0,2,1:T(8,128)}, f32[32,64]{1,0:T(8,128)S(1)}, bf16[4,32,32,64]{3,1,2,0:T(8,128)(2,1)}, f32[4,32,32,64]{3,2,1,0:T(8,1...) while((s32[]{:T(128)}, f32[64,32,64]{0,2,1:T(8,128)}, ...), condition=%wide.region_26.27_spmd.clone.clone, body=%wide.region_17.26_spmd.clone.sunk.clone | while | flops 391126080 | bytes 67733992 | solution.py:199
  1772.4 77.6 %all-reduce.28.cloned.1.call-done = (f32[2048]{0:T(1024)}, f32[2048]{0:T(1024)}, f32[2048]{0:T(1024)}, f32[2048]{0:T(1024)}, f32[2048]{0:T(1024)}, /*index=5*/f32[2048]{0:T(1024)}, f32[2048]{0:T(1024)}, f32[2048]{0:T(1024)}) async-done(((f32[2048]{0:T(1024)}, f32[2048]{0:T(1024)}, f32[2048]{0:T(1024)}, f32[2048]{0:T(1024)}, f32[2048]{0:T(1024)}, /*index=5*/f32[2048]{0:T(1024)}, f32[2048]{0:T(1024)}, ...) | async-done | bytes 65552
  1860.0 122.6 %reduce-scatter.49.cloned.1.call-done = f32[64,6]{1,0:T(8,128)} async-done(((f32[2048,6]{1,0:T(8,128)}), f32[64,6]{1,0:T(8,128)}) %reduce-scatter.49.cloned.1.call-update) | async-done | bytes 1552
  1984.1 70.5 %reduce-scatter.43.cloned.1.call-done = bf16[256,1792]{1,0:T(8,128)(2,1)} async-done(((bf16[2048,1792]{1,0:T(8,128)(2,1)}), bf16[256,1792]{1,0:T(8,128)(2,1)}) %reduce-scatter.43.cloned.1.call-update) | async-done | bytes 917520 | tf_op jit(solution)/shard_map/reduce_scatter | solution.py:243
  2057.1 67.8 %reduce-scatter.47.cloned.1.call-done = bf16[256,1792]{1,0:T(8,128)(2,1)} async-done(((bf16[2048,1792]{1,0:T(8,128)(2,1)}), bf16[256,1792]{1,0:T(8,128)(2,1)}) %reduce-scatter.47.cloned.1.call-update) | async-done | bytes 917520 | tf_op jit(solution)/shard_map/reduce_scatter | solution.py:246
  2127.4 130.9 %reduce-scatter.29.cloned.1.call-done = f32[64,64]{1,0:T(8,128)} async-done(((f32[2048,64]{1,0:T(8,128)}), f32[64,64]{1,0:T(8,128)}) %reduce-scatter.29.cloned.1.call-update) | async-done | bytes 16400 | tf_op jit(solution)/shard_map/reduce_scatter | solution.py:473
  2258.3 134.9 %reduce-scatter.31.cloned.1.call-done = f32[64,64]{1,0:T(8,128)} async-done(((f32[2048,64]{1,0:T(8,128)}), f32[64,64]{1,0:T(8,128)}) %reduce-scatter.31.cloned.1.call-update) | async-done | bytes 16400 | tf_op jit(solution)/shard_map/reduce_scatter | solution.py:474
  2393.2 138.1 %reduce-scatter.25.cloned.1.call-done = f32[64,160]{1,0:T(8,128)} async-done(((f32[2048,160]{1,0:T(8,128)}), f32[64,160]{1,0:T(8,128)}) %reduce-scatter.25.cloned.1.call-update) | async-done | bytes 40976 | tf_op jit(solution)/shard_map/reduce_scatter | solution.py:466
  2531.3 138.9 %reduce-scatter.27.cloned.1.call-done = f32[64,160]{1,0:T(8,128)} async-done(((f32[2048,160]{1,0:T(8,128)}), f32[64,160]{1,0:T(8,128)}) %reduce-scatter.27.cloned.1.call-update) | async-done | bytes 40976 | tf_op jit(solution)/shard_map/reduce_scatter | solution.py:469
  2670.2 368.4 %reduce-scatter.45.cloned.1.call-done = f32[64,2048]{1,0:T(8,128)} async-done(((f32[2048,2048]{1,0:T(8,128)}), f32[64,2048]{1,0:T(8,128)}) %reduce-scatter.45.cloned.1.call-update) | async-done | bytes 524304 | tf_op jit(solution)/shard_map/reduce_scatter | solution.py:494
  3038.6 365.1 %reduce-scatter.33.cloned.1.call-done = f32[64,2048]{1,0:T(8,128)} async-done(((f32[2048,2048]{1,0:T(8,128)}), f32[64,2048]{1,0:T(8,128)}) %reduce-scatter.33.cloned.1.call-update) | async-done | bytes 524304 | tf_op jit(solution)/shard_map/reduce_scatter | solution.py:478
  3403.8 365.0 %reduce-scatter.39.cloned.1.call-done = f32[64,2048]{1,0:T(8,128)} async-done(((f32[2048,2048]{1,0:T(8,128)}), f32[64,2048]{1,0:T(8,128)}) %reduce-scatter.39.cloned.1.call-update) | async-done | bytes 524304 | tf_op jit(solution)/shard_map/reduce_scatter | solution.py:481
  3768.8 365.0 %reduce-scatter.41.cloned.1.call-done = f32[64,2048]{1,0:T(8,128)} async-done(((f32[2048,2048]{1,0:T(8,128)}), f32[64,2048]{1,0:T(8,128)}) %reduce-scatter.41.cloned.1.call-update) | async-done | bytes 524304 | tf_op jit(solution)/shard_map/reduce_scatter | solution.py:482
  4133.8 365.2 %reduce-scatter.35.cloned.1.call-done = f32[64,2048]{1,0:T(8,128)} async-done(((f32[2048,2048]{1,0:T(8,128)}), f32[64,2048]{1,0:T(8,128)}) %reduce-scatter.35.cloned.1.call-update) | async-done | bytes 524304 | tf_op jit(solution)/shard_map/reduce_scatter | solution.py:479
  4499.0 365.2 %reduce-scatter.37.cloned.1.call-done = f32[64,2048]{1,0:T(8,128)} async-done(((f32[2048,2048]{1,0:T(8,128)}), f32[64,2048]{1,0:T(8,128)}) %reduce-scatter.37.cloned.1.call-update) | async-done | bytes 524304 | tf_op jit(solution)/shard_map/reduce_scatter | solution.py:480
  (839 shorter events, 1258.9 us)
Async XLA Ops:
  8.8 269.9 %all-gather.23.cloned.1.call-start = ((), (), s32[]{:S(2)}) async-start(), calls=%async_computation.18 | async-start | bytes 10485760 | tf_op jit(solution)/shard_map/all_gather | solution.py:294
  9.5 353.1 %all-gather.39.cloned.1.call-start = ((), (), s32[]{:S(2)}) async-start(), calls=%async_computation.40 | async-start | bytes 9437184 | tf_op jit(solution)/shard_map/all_gather | solution.py:24
  205.0 417.1 %all-gather.25.cloned.1.call-start = ((), (), s32[]{:S(2)}) async-start(), calls=%async_computation.19 | async-start | bytes 10485760 | tf_op jit(solution)/shard_map/all_gather | solution.py:297
  205.6 423.5 %all-gather.27.cloned.1.call-start = ((), (), s32[]{:S(2)}) async-start(), calls=%async_computation.20 | async-start | bytes 10485760 | tf_op jit(solution)/shard_map/all_gather | solution.py:298
  206.2 438.4 %all-gather.33.cloned.1.call-start = ((), (), s32[]{:S(2)}) async-start(), calls=%async_computation.23 | async-start | bytes 9175040 | tf_op jit(solution)/shard_map/all_gather | solution.py:300
  207.0 479.8 %all-gather.31.cloned.1.call-start = ((), (), s32[]{:S(2)}) async-start(), calls=%async_computation.22 | async-start | bytes 2621440 | tf_op jit(solution)/shard_map/all_gather | solution.py:367
  643.8 211.8 %all-gather.29.cloned.1.call-start = ((), (), s32[]{:S(2)}) async-start(), calls=%async_computation.21 | async-start | bytes 10485760 | tf_op jit(solution)/shard_map/all_gather | solution.py:299
  644.4 257.2 %reduce-scatter.21.cloned.1.call-start = ((), (), s32[]{:S(2)}) async-start(), calls=%async_computation.25 | async-start | bytes 2621440 | tf_op jit(solution)/shard_map/reduce_scatter | solution.py:370
  972.0 623.3 %all-gather.41.cloned.1.call-start = ((), (), s32[]{:S(2)}) async-start(), calls=%async_computation.41 | async-start | bytes 4718592 | tf_op jit(solution)/shard_map/all_gather | solution.py:39
  1538.2 230.2 %reduce-scatter.51.cloned.1.call-start = ((), (), s32[]{:S(2)}) async-start(), calls=%async_computation.43 | async-start | bytes 1081344
  1565.2 284.7 %all-reduce.28.cloned.1.call-start = ((), (), s32[]{:S(2)}) async-start(), calls=%async_computation.44 | async-start | bytes 131072
  1664.0 318.6 %reduce-scatter.49.cloned.1.call-start = ((), (), s32[]{:S(2)}) async-start(), calls=%async_computation.42 | async-start | bytes 1081344
  1665.6 389.0 %reduce-scatter.43.cloned.1.call-start = ((), (), s32[]{:S(2)}) async-start(), calls=%async_computation.37 | async-start | bytes 8257536 | tf_op jit(solution)/shard_map/reduce_scatter | solution.py:243
  1674.8 450.0 %reduce-scatter.47.cloned.1.call-start = ((), (), s32[]{:S(2)}) async-start(), calls=%async_computation.39 | async-start | bytes 8257536 | tf_op jit(solution)/shard_map/reduce_scatter | solution.py:246
  1684.7 573.6 %reduce-scatter.29.cloned.1.call-start = ((), (), s32[]{:S(2)}) async-start(), calls=%async_computation.30 | async-start | bytes 1081344 | tf_op jit(solution)/shard_map/reduce_scatter | solution.py:473
  1689.8 703.4 %reduce-scatter.31.cloned.1.call-start = ((), (), s32[]{:S(2)}) async-start(), calls=%async_computation.31 | async-start | bytes 1081344 | tf_op jit(solution)/shard_map/reduce_scatter | solution.py:474
  1694.0 837.3 %reduce-scatter.25.cloned.1.call-start = ((), (), s32[]{:S(2)}) async-start(), calls=%async_computation.28 | async-start | bytes 2162688 | tf_op jit(solution)/shard_map/reduce_scatter | solution.py:466
  1697.3 972.9 %reduce-scatter.27.cloned.1.call-start = ((), (), s32[]{:S(2)}) async-start(), calls=%async_computation.29 | async-start | bytes 2162688 | tf_op jit(solution)/shard_map/reduce_scatter | solution.py:469
  1706.6 1332.0 %reduce-scatter.45.cloned.1.call-start = ((), (), s32[]{:S(2)}) async-start(), calls=%async_computation.38 | async-start | bytes 17301504 | tf_op jit(solution)/shard_map/reduce_scatter | solution.py:494
  1714.9 1688.8 %reduce-scatter.33.cloned.1.call-start = ((), (), s32[]{:S(2)}) async-start(), calls=%async_computation.32 | async-start | bytes 17301504 | tf_op jit(solution)/shard_map/reduce_scatter | solution.py:478
  1725.9 2042.9 %reduce-scatter.39.cloned.1.call-start = ((), (), s32[]{:S(2)}) async-start(), calls=%async_computation.35 | async-start | bytes 17301504 | tf_op jit(solution)/shard_map/reduce_scatter | solution.py:481
  1735.3 2398.5 %reduce-scatter.41.cloned.1.call-start = ((), (), s32[]{:S(2)}) async-start(), calls=%async_computation.36 | async-start | bytes 17301504 | tf_op jit(solution)/shard_map/reduce_scatter | solution.py:482
  1744.7 2754.3 %reduce-scatter.35.cloned.1.call-start = ((), (), s32[]{:S(2)}) async-start(), calls=%async_computation.33 | async-start | bytes 17301504 | tf_op jit(solution)/shard_map/reduce_scatter | solution.py:479
  1755.3 3108.9 %reduce-scatter.37.cloned.1.call-start = ((), (), s32[]{:S(2)}) async-start(), calls=%async_computation.34 | async-start | bytes 17301504 | tf_op jit(solution)/shard_map/reduce_scatter | solution.py:480
  (167 other events, 4211.9 us)
Sparse Core Ops, SparseCore 0:
  9.9 89.6 all-gather.18
  101.5 87.5 all-gather.20
  191.0 87.5 all-gather.22
  280.1 82.4 all-gather.38
  364.3 85.7 all-gather.24
  451.8 87.5 all-gather.26
  541.3 78.8 all-gather.32
  688.6 77.5 all-gather.34
  768.0 87.5 all-gather.28
  1590.2 129.0 reduce-scatter.50
  1726.8 123.1 all-reduce.27
  1852.0 130.5 reduce-scatter.48
  1986.3 68.2 reduce-scatter.42
  2057.9 66.8 reduce-scatter.46
  2127.6 130.6 reduce-scatter.28
  2261.1 132.0 reduce-scatter.30
  2396.2 135.1 reduce-scatter.24
  2534.2 135.9 reduce-scatter.26
  2673.0 365.5 reduce-scatter.44
  3041.6 362.1 reduce-scatter.32
  3406.6 362.1 reduce-scatter.38
  3771.6 362.1 reduce-scatter.40
  4136.8 362.1 reduce-scatter.34
  4501.9 362.1 reduce-scatter.36
  (5 shorter events, 224.6 us)
where the time goes:
time: 4890 us; the launch traced here: 4870 us
  waiting for transfers between devices  3650 us (75%)
  matrix products  682 us (14%)
  local copies, waits for them, and re-layouts  230 us (5%)
  other arithmetic  179 us (4%)
  blocking collectives  50.1 us (1%)
    reduce_scatter x1, waiting for transfers between devices, on_device(): lax.psum_scatter(grad_ffn_recept, ('seg', 'seq', 'chan'), scatter_dimensi...  368 us
    reduce_scatter x1, waiting for transfers between devices, on_device(): lax.psum_scatter(grad_value, ('seg', 'seq', 'chan'), scatter_dimension=0,...  365 us
    reduce_scatter x1, waiting for transfers between devices, on_device(): lax.psum_scatter(grad_key, ('seg', 'seq', 'chan'), scatter_dimension=0, t...  365 us
    reduce_scatter x1, waiting for transfers between devices, on_device(): lax.psum_scatter(grad_recept, ('seg', 'seq', 'chan'), scatter_dimension=0...  365 us
    reduce_scatter x1, waiting for transfers between devices, on_device(): lax.psum_scatter(grad_gate, ('seg', 'seq', 'chan'), scatter_dimension=0,...  365 us
    reduce_scatter x1, waiting for transfers between devices, on_device(): lax.psum_scatter(grad_output, ('seg', 'seq', 'chan'), scatter_dimension=0...  365 us
    dot_general x12, matrix products, block_step(): jnp.einsum('thk,tshk->tsh', acceptor_entries, weights * address_entries[N...  338 us
    unnamed x32, waiting for transfers between devices  206 us
  transfers between devices with their start and end apart: 33, of which 27 were waited for; matrix products, arithmetic and copies ran while one was open for 12% of the time, Pallas kernels for 0%

commit v1 on v0

v1 whole, which is shorter than its diff:
```python
import jax
import jax.numpy as jnp
from jax import lax
from jax.experimental import pallas as pl
from jax.experimental.pallas import tpu as pltpu
from jax.sharding import PartitionSpec as P

HEAD = 64
TP = ("seq", "chan")
ALL = ("seg", "seq", "chan")
LAYER_EPSILON = 1e-05
GROUP_EPSILON = 0.00064
F32 = jnp.float32
BF16 = jnp.bfloat16
CHUNK = 256
VMEM = 56 * 2**20


def dot(a, b, dims):
    return lax.dot_general(
        a.astype(BF16), b.astype(BF16), (dims, ((), ())), preferred_element_type=F32
    )


def nn(a, b):
    return dot(a, b, ((1,), (0,)))


def nt(a, b):
    return dot(a, b, ((1,), (1,)))


def tn(a, b):
    return dot(a, b, ((0,), (0,)))


def iota(shape, axis):
    return lax.broadcasted_iota(jnp.int32, shape, axis)


def head_sum(values, ones):
    high = values.astype(BF16)
    low = (values - high.astype(F32)).astype(BF16)
    return nn(high, ones) + nn(low, ones)


def pyramid(w):
    length = w.shape[0]
    row = iota(w.shape, 0)
    before, after, total = jnp.zeros_like(w), jnp.zeros_like(w), w
    levels = []
    half = 1
    while half < length:
        upper = (row & half) != 0
        levels.append((half, upper, jnp.where(upper, before, after)))
        sibling = jnp.where(upper, pltpu.roll(total, half, 0), pltpu.roll(total, length - half, 0))
        before = jnp.where(upper, before + sibling, before)
        after = jnp.where(upper, after, after + sibling)
        total = total + sibling
        half *= 2
    return levels, before, after, total


def split_heads(values, heads):
    if heads == 1:
        return [values.astype(BF16)]
    lane = iota(values.shape, 1) // HEAD
    return [jnp.where(lane == head, values, 0.0).astype(BF16) for head in range(heads)]


def row_stats(x_ref):
    rows, width = x_ref.shape
    step = 128
    total = jnp.zeros((rows, step), F32)
    for at in range(0, width, step):
        total = total + x_ref[:, at : at + step].astype(F32)
    mean = jnp.sum(total, 1, keepdims=True) / width
    total = jnp.zeros((rows, step), F32)
    for at in range(0, width, step):
        center = x_ref[:, at : at + step].astype(F32) - mean
        total = total + center * center
    return mean, lax.rsqrt(jnp.sum(total, 1, keepdims=True) / width + LAYER_EPSILON)


def fold(values):
    rows, width = values.shape
    return jnp.sum(values.reshape(rows // 8, 8, width), 0)


def rank_blocks(values, rank):
    lane = iota(values.shape, 1) // rank
    return jnp.concatenate([jnp.where(lane == j, values, 0.0).astype(BF16) for j in range(5)], 0)


GAIN, BIAS, MIX, FIRST = 0, 1, 2, 8


def mix_forward(
    rank, x_ref, rows_ref, own_ref, wn_ref, wwt_ref, fn_ref, fwt_ref, wr_ref, wk_ref, wv_ref, wg_ref,
    ones_ref, start_ref,
    xk_ref, xv_ref, xr_ref, xg_ref, r_ref, k_ref, v_ref, w_ref, graw_ref, wkv_ref, gated_ref, lm_ref, dm_ref,
    ends_ref, normed_ref, delta_ref, carry_ref, state_ref,
):
    step = pl.program_id(0)
    length, width = x_ref.shape
    own = own_ref.shape[1]
    heads = own // HEAD

    @pl.when(step == 0)
    def _():
        carry_ref[...] = jnp.broadcast_to(rows_ref[FIRST : FIRST + 1, :], carry_ref.shape)
        state_ref[...] = start_ref[...]

    mean, scale = row_stats(x_ref)
    first = iota((length, CHUNK), 0) == 0
    narrow = jnp.zeros((length, wn_ref.shape[1]), F32)
    for at in range(0, width, CHUNK):
        c = slice(at, at + CHUNK)
        normed = (x_ref[:, c].astype(F32) - mean) * scale * rows_ref[GAIN : GAIN + 1, c] + rows_ref[BIAS : BIAS + 1, c]
        delta = jnp.where(first, carry_ref[0:1, c], pltpu.roll(normed, 1, 0)) - normed
        carry_ref[0:1, c] = normed[length - 1 : length, :]
        normed_ref[:, c] = normed
        delta_ref[:, c] = delta
        narrow = narrow + nn(normed + delta * rows_ref[MIX : MIX + 1, c], wn_ref[c, :])
    middle = jnp.tanh(narrow)
    lm_ref[...] = middle
    blocks = rank_blocks(middle, rank)
    decay_in = jnp.zeros((length, fn_ref.shape[1]), F32)
    for at in range(0, width, CHUNK):
        c = slice(at, at + CHUNK)
        normed, delta = normed_ref[:, c], delta_ref[:, c]
        modifiers = nn(blocks, wwt_ref[:, c])
        for j, ref in enumerate((None, xk_ref, xv_ref, xr_ref, xg_ref)):
            modifier = modifiers[j * length : (j + 1) * length, :]
            mixed = (normed + delta * (rows_ref[MIX + 1 + j : MIX + 2 + j, c] + modifier)).astype(BF16)
            if ref is None:
                decay_in = decay_in + nn(mixed, fn_ref[c, :])
            else:
                ref[:, c] = mixed
    decay_mid = jnp.tanh(decay_in)
    dm_ref[...] = decay_mid
    w = -jnp.exp(own_ref[0:1, :] + nn(decay_mid, fwt_ref[...]))
    w_ref[...] = w
    r = nn(xr_ref[...], wr_ref[...]).astype(BF16)
    k = nn(xk_ref[...], wk_ref[...]).astype(BF16)
    v = nn(xv_ref[...], wv_ref[...]).astype(BF16)
    graw = nn(xg_ref[...], wg_ref[...])
    r_ref[...], k_ref[...], v_ref[...], graw_ref[...] = r, k, v, graw

    rf, kf, vf = r.astype(F32), k.astype(F32), v.astype(F32)
    levels, before, after, total = pyramid(w)
    row, col = iota((length, length), 0), iota((length, length), 1)
    apart = jnp.where(row > col, row ^ col, 0)
    scores = [jnp.zeros((length, length), F32)] * heads
    for half, upper, exponent in levels:
        scaled = jnp.where(upper, rf, kf) * jnp.exp(exponent)
        flat = scaled.astype(BF16)
        here = (apart >= half) & (apart < 2 * half)
        for head, one in enumerate(split_heads(scaled, heads)):
            scores[head] = jnp.where(here, nt(one, flat), scores[head])
    ones = ones_ref[...]
    wkv = nn(jnp.concatenate([s.astype(BF16) for s in scores], 1), jnp.concatenate(split_heads(vf, heads), 0))
    state = state_ref[...]
    wkv = wkv + nt(rf * jnp.exp(before), state) + head_sum(rf * own_ref[1:2, :] * kf, ones) * vf
    wkv_ref[...] = wkv
    state = state * jnp.exp(total[0:1, :]) + tn(v, kf * jnp.exp(after)) * ones.astype(F32)
    state_ref[...] = state
    ends_ref[0] = state

    center = wkv - head_sum(wkv, ones) / HEAD
    spread = head_sum(center * center, ones) / HEAD
    grouped = center * lax.rsqrt(spread + GROUP_EPSILON) * own_ref[2:3, :] + own_ref[3:4, :]
    gated_ref[...] = (grouped * graw * jax.nn.sigmoid(graw)).astype(BF16)


def wkv_backward(
    count, d_ref, r_ref, k_ref, v_ref, w_ref, graw_ref, wkv_ref, own_ref, ones_ref, sums_ref, start_ref, ends_ref,
    adj_ref,
    dr_ref, dk_ref, dv_ref, dg_ref, dpre_ref, own_sums_ref, state_ref,
):
    step = pl.program_id(0)
    length, own = d_ref.shape
    heads = own // HEAD
    ones = ones_ref[...]

    @pl.when(step == 0)
    def _():
        state_ref[...] = jnp.zeros_like(state_ref)
        own_sums_ref[...] = jnp.zeros_like(own_sums_ref)

    reward, gain, bias = own_ref[1:2, :], own_ref[2:3, :], own_ref[3:4, :]
    wkv, graw, d_gated = wkv_ref[...], graw_ref[...], d_ref[...]
    center = wkv - head_sum(wkv, ones) / HEAD
    scale = lax.rsqrt(head_sum(center * center, ones) / HEAD + GROUP_EPSILON)
    normed = center * scale
    sigma = jax.nn.sigmoid(graw)
    d_grouped = d_gated * graw * sigma
    dg_ref[...] = (d_gated * (normed * gain + bias) * sigma * (1.0 + graw * (1.0 - sigma))).astype(BF16)
    d_normed = d_grouped * gain
    do = scale * (d_normed - head_sum(d_normed, ones) / HEAD - normed * (head_sum(d_normed * normed, ones) / HEAD))

    rb, kb, vb, dob = r_ref[...], k_ref[...], v_ref[...], do.astype(BF16)
    r, k, v, w = rb.astype(F32), kb.astype(F32), vb.astype(F32), w_ref[...]
    levels, before, after, total = pyramid(w)
    d_state = state_ref[...] + adj_ref[0]
    state = jnp.where(step == count - 1, start_ref[...], ends_ref[0])
    d_flat, flat = d_state.astype(BF16), state.astype(BF16)
    from_start, to_end, decay = jnp.exp(before), jnp.exp(after), jnp.exp(total[0:1, :])
    dr = from_start * nn(dob, flat)
    dk = to_end * nn(vb, d_flat)
    dv = nt(k * to_end, d_flat)
    through = [r * dr, k * dk]
    state_ref[...] = d_state * decay + tn(dob, r * from_start) * ones.astype(F32)
    whole = decay * jnp.sum(state * d_state, 0, keepdims=True)

    row, col = iota((length, length), 0), iota((length, length), 1)
    apart = row ^ col
    do_heads, v_heads = split_heads(do, heads), split_heads(v, heads)
    d_scores = [
        jnp.where(row > col, nt(do_heads[h], vb), jnp.where(row < col, nt(v_heads[h], dob), 0.0)).astype(BF16)
        for h in range(heads)
    ]
    scores = [jnp.zeros((length, length), F32)] * heads
    for half, upper, exponent in levels:
        factor = jnp.exp(exponent)
        scaled = jnp.where(upper, r, k) * factor
        mine = split_heads(scaled, heads)
        here = (apart >= half) & (apart < 2 * half)
        late = here & (row < col)
        for h in range(heads):
            scores[h] = jnp.where(late, nt(mine[h], scaled), scores[h])
        pulled = nn(
            jnp.concatenate([jnp.where(here, d, 0.0).astype(BF16) for d in d_scores], 1), jnp.concatenate(mine, 0)
        )
        if half > 1:
            through.append(scaled * pulled)
        pulled = pulled * factor
        dr = dr + jnp.where(upper, pulled, 0.0)
        dk = dk + jnp.where(upper, 0.0, pulled)
    dv = dv + nn(jnp.concatenate([s.astype(BF16) for s in scores], 1), jnp.concatenate(do_heads, 0))
    met = head_sum(v * do, ones)
    dr = dr + reward * k * met
    dk = dk + reward * r * met
    dv = dv + head_sum(r * reward * k, ones) * do
    d_log = whole + nn(sums_ref[...], jnp.concatenate([q.astype(BF16) for q in through], 0))
    d_pre = d_log * w
    dr_ref[...], dk_ref[...], dv_ref[...] = dr.astype(BF16), dk.astype(BF16), dv.astype(BF16)
    dpre_ref[...] = d_pre
    for i, part in enumerate((d_pre, r * k * met, d_grouped * normed, d_grouped)):
        own_sums_ref[8 * i : 8 * i + 8, :] += fold(part)


def sum_table(length):
    row, col = iota((length, length), 0), iota((length, length), 1)
    tables = [col > row, col < row]
    half = 2
    while half < length:
        inside = (row // half) == (col // half)
        upper = (row // half) % 2 == 1
        tables.append(inside & jnp.where(upper, col > row, col < row))
        half *= 2
    return jnp.concatenate(tables, 1).astype(BF16)


def mix_backward(
    rank, count, x_ref, edge_ref, rows_ref, lm_ref, dm_ref, dr_ref, dk_ref, dv_ref, dg_ref, dpre_ref,
    wn_ref, ww_ref, wwt_ref, fn_ref, fwt_ref, wr_ref, wk_ref, wv_ref, wg_ref,
    dx_ref, row_sums_ref, up_ref, down_ref, decay_down_ref, decay_up_ref,
    sum_ref, coef_ref, normed_ref, delta_ref, carry_ref,
):
    step = pl.program_id(0)
    length, width = x_ref.shape

    @pl.when(step == 0)
    def _():
        carry_ref[...] = jnp.zeros_like(carry_ref)
        for ref in (row_sums_ref, up_ref, down_ref, decay_down_ref, decay_up_ref):
            ref[...] = jnp.zeros_like(ref)

    mean, scale = row_stats(x_ref)
    edge = edge_ref.shape[0]
    edge_mean, edge_scale = row_stats(edge_ref)
    middle, decay_mid = lm_ref[...], dm_ref[...]
    blocks = rank_blocks(middle, rank)
    d_pre = dpre_ref[...]
    decay_up_ref[...] += tn(decay_mid, d_pre)
    d_decay = (nt(d_pre, fwt_ref[...]) * (1.0 - decay_mid * decay_mid)).astype(BF16)
    sources = (
        (d_decay, fn_ref), (dk_ref[...], wk_ref), (dv_ref[...], wv_ref), (dr_ref[...], wr_ref), (dg_ref[...], wg_ref),
    )
    first = iota((length, CHUNK), 0) == 0
    last = iota((length, CHUNK), 0) == length - 1
    d_mid = jnp.zeros((5 * length, wn_ref.shape[1]), F32)
    for at in range(0, width, CHUNK):
        c = slice(at, at + CHUNK)
        gain, bias = rows_ref[GAIN : GAIN + 1, c], rows_ref[BIAS : BIAS + 1, c]
        normed = (x_ref[:, c].astype(F32) - mean) * scale * gain + bias
        edge_normed = (edge_ref[:, c].astype(F32) - edge_mean) * edge_scale * gain + bias
        before = jnp.where(step == count - 1, rows_ref[FIRST : FIRST + 1, c], edge_normed[edge - 1 : edge, :])
        delta = jnp.where(first, before, pltpu.roll(normed, 1, 0)) - normed
        normed_ref[:, c] = normed
        delta_ref[:, c] = delta
        modifiers = nn(blocks, wwt_ref[:, c])
        total = jnp.zeros_like(normed)
        by_coef = jnp.zeros_like(normed)
        d_mods = []
        for j, (d, w_ref) in enumerate(sources):
            d_mixed = nt(d, w_ref[c, :])
            coef = rows_ref[MIX + 1 + j : MIX + 2 + j, c] + modifiers[j * length : (j + 1) * length, :]
            if j == 0:
                decay_down_ref[:, c] += tn(d_decay, normed + delta * coef)
            d_mod = delta * d_mixed
            row_sums_ref[8 * (MIX + 1 + j) : 8 * (MIX + 2 + j), c] += fold(d_mod)
            d_mods.append(d_mod.astype(BF16))
            total = total + d_mixed
            by_coef = by_coef + d_mixed * coef
        d_mods = jnp.concatenate(d_mods, 0)
        up_ref[:, c] += tn(blocks, d_mods)
        d_mid = d_mid + nn(d_mods, ww_ref[c, :])
        sum_ref[:, c] = total
        coef_ref[:, c] = by_coef
    lane = iota(middle.shape, 1) // rank
    d_low = jnp.zeros_like(middle)
    for j in range(5):
        d_low = jnp.where(lane == j, d_mid[j * length : (j + 1) * length, :], d_low)
    d_low = (d_low * (1.0 - middle * middle)).astype(BF16)
    sum_g = jnp.zeros((length, CHUNK), F32)
    sum_gn = jnp.zeros((length, CHUNK), F32)
    for at in range(0, width, CHUNK):
        c = slice(at, at + CHUNK)
        normed, delta = normed_ref[:, c], delta_ref[:, c]
        mix = rows_ref[MIX : MIX + 1, c]
        d_in = nt(d_low, wn_ref[c, :])
        down_ref[:, c] += tn(d_low, normed + delta * mix)
        row_sums_ref[8 * MIX : 8 * MIX + 8, c] += fold(delta * d_in)
        d_delta = coef_ref[:, c] + d_in * mix
        above = jnp.where(last, carry_ref[0:1, c], pltpu.roll(d_delta, length - 1, 0))
        carry_ref[0:1, c] = d_delta[0:1, :]
        d_normed = sum_ref[:, c] + d_in - d_delta + above
        unit = (x_ref[:, c].astype(F32) - mean) * scale
        row_sums_ref[8 * GAIN : 8 * GAIN + 8, c] += fold(d_normed * unit)
        row_sums_ref[8 * BIAS : 8 * BIAS + 8, c] += fold(d_normed)
        g = d_normed * rows_ref[GAIN : GAIN + 1, c]
        sum_g = sum_g + g
        sum_gn = sum_gn + g * unit
        sum_ref[:, c] = g
    mean_g = jnp.sum(sum_g, 1, keepdims=True) / width
    mean_gn = jnp.sum(sum_gn, 1, keepdims=True) / width
    for at in range(0, width, CHUNK):
        c = slice(at, at + CHUNK)
        unit = (x_ref[:, c].astype(F32) - mean) * scale
        dx_ref[:, c] = (scale * (sum_ref[:, c] - mean_g - unit * mean_gn)).astype(BF16)


def whole(a):
    return pl.BlockSpec(a.shape, lambda t: (0,) * a.ndim)


def params(**more):
    return pltpu.CompilerParams(
        dimension_semantics=("arbitrary",), vmem_limit_bytes=VMEM, **more
    )


def call_forward(rank, length, x, rows, own, wn, wwt, fn, fwt, wr, wk, wv, wg, ones, start):
    tokens, width = x.shape
    cw = own.shape[1]
    count = tokens // length
    tile = lambda n: pl.BlockSpec((length, n), lambda t: (t, 0))
    shape = lambda n, dtype: jax.ShapeDtypeStruct((tokens, n), dtype)
    fixed = (rows, own, wn, wwt, fn, fwt, wr, wk, wv, wg, ones, start)
    return pl.pallas_call(
        lambda *refs: mix_forward(rank, *refs),
        grid=(count,),
        in_specs=[tile(width)] + [whole(a) for a in fixed],
        out_specs=[tile(width)] * 4 + [tile(cw)] * 7 + [tile(wn.shape[1]), tile(fn.shape[1])]
        + [pl.BlockSpec((1, cw, cw), lambda t: (t, 0, 0))],
        out_shape=[shape(width, BF16)] * 4 + [shape(cw, BF16)] * 3 + [shape(cw, F32)] * 3 + [shape(cw, BF16)]
        + [shape(wn.shape[1], F32), shape(fn.shape[1], F32), jax.ShapeDtypeStruct((count, cw, cw), F32)],
        scratch_shapes=[
            pltpu.VMEM((length, width), F32), pltpu.VMEM((length, width), F32), pltpu.VMEM((8, width), F32),
            pltpu.VMEM((cw, cw), F32),
        ],
        compiler_params=params(),
        cost_estimate=pl.CostEstimate(
            flops=2 * tokens * width * (4 * cw + 5 * 256 + 384), bytes_accessed=tokens * width * 10 + width * cw * 8,
            transcendentals=0,
        ),
        name="mix_forward",
    )(x, *fixed)


def call_wkv_backward(length, d, r, k, v, w, graw, wkv, own, ones, sums, start, ends, adj):
    tokens, cw = d.shape
    count = tokens // length
    tile = pl.BlockSpec((length, cw), lambda t: (count - 1 - t, 0))
    shape = lambda dtype: jax.ShapeDtypeStruct((tokens, cw), dtype)
    return pl.pallas_call(
        lambda *refs: wkv_backward(count, *refs),
        grid=(count,),
        in_specs=[tile] * 7 + [whole(a) for a in (own, ones, sums, start)]
        + [
            pl.BlockSpec((1, cw, cw), lambda t: (jnp.maximum(count - 2 - t, 0), 0, 0)),
            pl.BlockSpec((1, cw, cw), lambda t: (count - 1 - t, 0, 0)),
        ],
        out_specs=[tile] * 5 + [pl.BlockSpec((32, cw), lambda t: (0, 0))],
        out_shape=[shape(BF16)] * 4 + [shape(F32), jax.ShapeDtypeStruct((32, cw), F32)],
        scratch_shapes=[pltpu.VMEM((cw, cw), F32)],
        compiler_params=params(),
        cost_estimate=pl.CostEstimate(
            flops=2 * tokens * cw * 128 * 50, bytes_accessed=tokens * cw * 40, transcendentals=0
        ),
        name="wkv_backward",
    )(d, r, k, v, w, graw, wkv, own, ones, sums, start, ends, adj)


def call_mix_backward(rank, length, x, rows, lm, dm, dr, dk, dv, dg, dpre, wn, ww, wwt, fn, fwt, wr, wk, wv, wg):
    tokens, width = x.shape
    cw = dr.shape[1]
    count = tokens // length
    edge = 16
    tile = lambda n: pl.BlockSpec((length, n), lambda t: (count - 1 - t, 0))
    before = pl.BlockSpec((edge, width), lambda t: (jnp.maximum((count - 1 - t) * (length // edge) - 1, 0), 0))
    fixed = (wn, ww, wwt, fn, fwt, wr, wk, wv, wg)
    sums = [(8 * 8, width), (wn.shape[1], width), (wn.shape[1], width), (fn.shape[1], width), (fn.shape[1], cw)]
    return pl.pallas_call(
        lambda *refs: mix_backward(rank, count, *refs),
        grid=(count,),
        in_specs=[tile(width), before, whole(rows), tile(lm.shape[1]), tile(dm.shape[1])] + [tile(cw)] * 5
        + [whole(a) for a in fixed],
        out_specs=[tile(width)] + [pl.BlockSpec(s, lambda t: (0, 0)) for s in sums],
        out_shape=[jax.ShapeDtypeStruct((tokens, width), BF16)] + [jax.ShapeDtypeStruct(s, F32) for s in sums],
        scratch_shapes=[pltpu.VMEM((length, width), F32)] * 4 + [pltpu.VMEM((8, width), F32)],
        compiler_params=params(),
        cost_estimate=pl.CostEstimate(
            flops=2 * tokens * width * (4 * cw + 15 * 256 + 768), bytes_accessed=tokens * width * 6 + width * cw * 8,
            transcendentals=0,
        ),
        name="mix_backward",
    )(x, x, rows, lm, dm, dr, dk, dv, dg, dpre, *fixed)


def gather_group(block):
    return lax.all_gather(block, TP, axis=0, tiled=True)


def reduce_group(parts):
    seqs, chans = lax.axis_size("seq"), lax.axis_size("chan")
    parts = parts.reshape((seqs, chans) + parts.shape[1:])
    me, at = lax.axis_index("seq"), lax.axis_index("chan")
    if seqs == 2:
        other = lax.ppermute(lax.dynamic_index_in_dim(parts, 1 - me, 0, False), "seq", [(0, 1), (1, 0)])
        mine = lax.dynamic_index_in_dim(parts, me, 0, False).astype(F32) + other.astype(F32)
    else:
        mine = lax.psum_scatter(parts, "seq", scatter_dimension=0, tiled=True)[0].astype(F32)
    sent = mine.astype(BF16)
    total = lax.dynamic_index_in_dim(mine, at, 0, False)
    for k in range(1, chans):
        block = lax.dynamic_index_in_dim(sent, (at + k) % chans, 0, False)
        total = total + lax.ppermute(block, "chan", [(i, (i + k) % chans) for i in range(chans)]).astype(F32)
    return total


def next_row(row, by):
    count = lax.axis_size(TP)
    return lax.ppermute(row, TP, [(i, i + by) for i in range(count) if 0 <= i + by < count])


def shift_down(values, first_row):
    return jnp.concatenate([first_row, values[:-1]], 0)


def unit_rows(values):
    center = values - jnp.mean(values, -1, keepdims=True)
    scale = lax.rsqrt(jnp.mean(center * center, -1, keepdims=True) + LAYER_EPSILON)
    return center * scale, scale


def on_device(
    sequence_elements,
    segment_predecessor_entries,
    opening_recurrences,
    first_layernorm_gain,
    first_layernorm_shift_term,
    lag_blend_coefficients,
    lag_narrowing_factor,
    lag_widening_factors,
    fading_exponent_baseline,
    fading_narrowing_factor,
    fading_widening_factor,
    present_reward,
    acceptor_projection,
    address_projection,
    content_projection,
    valve_projection,
    timemix_result_projection,
    subspace_cluster_gain,
    subspace_cluster_shift_term,
    second_layernorm_gain,
    second_layernorm_shift_term,
    feedforward_lag_blends,
    feedforward_address_projection,
    feedforward_acceptor_projection,
    feedforward_content_projection,
    result_adjoint,
    final_recurrence_adjoint,
):
    segs, seqs, chans = lax.axis_size("seg"), lax.axis_size("seq"), lax.axis_size("chan")
    group = seqs * chans
    p = lax.axis_index(TP)
    x = sequence_elements[0]
    length, width = x.shape
    tokens = group * length
    cw = width // group
    heads = cw // HEAD
    rank = lag_widening_factors.shape[1] // 5
    ranks, decays = 5 * rank, fading_widening_factor.shape[1]
    wide_rank, wide_decay = -(-ranks // 128) * 128, -(-decays // 128) * 128

    def columns(a, axis=-1):
        return lax.dynamic_slice_in_dim(a, p * cw, cw, axis if axis >= 0 else a.ndim + axis)

    def gather_rows(a):
        return lax.all_gather(a, "seg", axis=0, tiled=True)

    x_all = gather_group(x)
    four = gather_rows(
        jnp.concatenate(
            [columns(a) for a in (acceptor_projection, address_projection, content_projection, valve_projection)], 1
        )
    )
    wr, wk, wv, wg = (four[:, i * cw : (i + 1) * cw] for i in range(4))
    share = group // segs
    out_rows = lax.dynamic_slice_in_dim(timemix_result_projection, (p % share) * cw, cw, 0)
    w_out = lax.ppermute(
        out_rows, ALL,
        [(s * group + j, (j // share) * group + s * share + j % share) for s in range(segs) for j in range(group)],
    )
    hidden_units = feedforward_address_projection.shape[1] // seqs
    me = lax.axis_index("seq")

    def hidden_part(a):
        return lax.dynamic_slice_in_dim(a, me * hidden_units, hidden_units, 1)

    fr_columns = width // seqs
    w_recept = lax.all_gather(
        gather_rows(lax.dynamic_slice_in_dim(feedforward_acceptor_projection, me * fr_columns, fr_columns, 1)),
        "seq", axis=1, tiled=True,
    )
    w_key = gather_rows(hidden_part(feedforward_address_projection))
    w_value = gather_rows(hidden_part(feedforward_content_projection))

    zeros_row = jnp.zeros((7, width), F32)
    rows = jnp.concatenate(
        [
            first_layernorm_gain[None], first_layernorm_shift_term[None], lag_blend_coefficients.T,
            segment_predecessor_entries[0, 0][None], zeros_row,
        ]
    )
    own = jnp.stack(
        [columns(a) for a in (fading_exponent_baseline, present_reward, subspace_cluster_gain, subspace_cluster_shift_term)]
        + [jnp.zeros((cw,), F32)] * 4
    )
    wn = jnp.pad(lag_narrowing_factor, ((0, 0), (0, wide_rank - ranks)))
    ww = jnp.pad(lag_widening_factors, ((0, 0), (0, wide_rank - ranks)))
    wwt = ww.T
    fn = jnp.pad(fading_narrowing_factor, ((0, 0), (0, wide_decay - decays)))
    fwt = columns(jnp.pad(fading_widening_factor, ((0, 0), (0, wide_decay - decays))).T)
    same_head = (iota((cw, cw), 0) // HEAD) == (iota((cw, cw), 1) // HEAD)

    def spread(states):
        flat = jnp.swapaxes(states, -1, -2)
        return jnp.where(same_head, jnp.concatenate([flat] * heads, -1), 0.0)

    start = spread(columns(opening_recurrences[0]))
    adjoints = lax.all_to_all(
        final_recurrence_adjoint[0, 0].reshape(HEAD, group, cw).transpose(1, 0, 2), TP, 0, 0, tiled=True
    )
    adjoints = spread(adjoints)

    (xk, xv, xr, xg, r, k, v, w, graw, wkv, gated, lm, dm, ends) = call_forward(
        rank, length, x_all, rows, own, wn, wwt, fn, fwt, wr, wk, wv, wg, same_head.astype(BF16), start
    )
    mixed_out = nn(gated, w_out).astype(BF16).reshape(group, length, width)
    residual = x.astype(F32) + reduce_group(mixed_out)

    cot = result_adjoint[0].astype(F32)
    ffn_unit, ffn_scale = unit_rows(residual)
    ffn_normed = ffn_unit * second_layernorm_gain + second_layernorm_shift_term
    first_row = segment_predecessor_entries[0, 1][None]
    previous = jnp.where(p == 0, first_row, next_row(ffn_normed[-1:], 1))
    ffn_delta = shift_down(ffn_normed, previous) - ffn_normed
    mix_key, mix_recept = feedforward_lag_blends[:, 0], feedforward_lag_blends[:, 1]
    recept_in = (ffn_normed + ffn_delta * mix_recept).astype(BF16)
    ffn_gate = jax.nn.sigmoid(nn(recept_in, w_recept))
    d_values = (cot * ffn_gate).astype(BF16)

    normed_all = gather_group(ffn_normed.astype(BF16))
    d_values_all = gather_group(d_values)
    normed_f32 = normed_all.astype(F32)
    delta_all = shift_down(normed_f32, first_row) - normed_f32
    key_in_all = (normed_f32 + delta_all * mix_key).astype(BF16)
    recept_in_all = (normed_f32 + delta_all * mix_recept).astype(BF16)
    hidden = jax.nn.relu(nn(key_in_all, w_key))
    squared = jnp.square(hidden).astype(BF16)
    ffn_values = reduce_group(nt(squared, w_value).astype(BF16).reshape(group, length, width))
    d_hidden = (nn(d_values_all, w_value) * 2.0 * hidden).astype(BF16)
    d_fk = reduce_group(nt(d_hidden, w_key).astype(BF16).reshape(group, length, width))

    def reduce_rows(a):
        return lax.psum_scatter(a.astype(BF16), "seg", scatter_dimension=0, tiled=True)

    def join_hidden(a):
        return lax.all_to_all(a, "seq", 0, 1, tiled=True).astype(F32)

    grad_ffn_value = join_hidden(reduce_rows(tn(d_values_all, squared)))
    grad_ffn_key = join_hidden(reduce_rows(tn(key_in_all, d_hidden)))

    output = residual + ffn_gate * ffn_values
    d_ffn_gate = (cot * ffn_values * ffn_gate * (1.0 - ffn_gate)).astype(BF16)
    d_fr = nt(d_ffn_gate, w_recept)
    d_fdelta = d_fk * mix_key + d_fr * mix_recept
    d_ffn_normed = d_fk + d_fr - d_fdelta + jnp.concatenate([d_fdelta[1:], next_row(d_fdelta[:1], -1)], 0)
    g = d_ffn_normed * second_layernorm_gain
    d_residual = cot + ffn_scale * (
        g - jnp.mean(g, -1, keepdims=True) - ffn_unit * jnp.mean(g * ffn_unit, -1, keepdims=True)
    )
    ffn_sums = jnp.stack(
        [
            jnp.sum(d_ffn_normed * ffn_unit, 0), jnp.sum(d_ffn_normed, 0),
            jnp.sum(ffn_delta * d_fk, 0), jnp.sum(ffn_delta * d_fr, 0),
        ]
    )
    d_att = gather_group(d_residual.astype(BF16))
    d_gate_own = lax.all_to_all(d_ffn_gate.reshape(length, group, cw).transpose(1, 0, 2), TP, 0, 0, tiled=True)
    grad_recept_part = tn(recept_in_all, d_gate_own.reshape(tokens, cw))

    d_gated = nt(d_att, w_out)
    dr, dk, dv, dg, d_pre, own_sums = call_wkv_backward(
        length, d_gated, r, k, v, w, graw, wkv, own, same_head.astype(BF16), sum_table(length), start, ends, adjoints
    )
    grad_four = jnp.concatenate([tn(xr, dr), tn(xk, dk), tn(xv, dv), tn(xg, dg), grad_recept_part], 1)
    dx, row_sums, up, down, decay_down, decay_up = call_mix_backward(
        rank, length, x_all, rows, lm, dm, dr, dk, dv, dg, d_pre, wn, ww, wwt, fn, fwt, wr, wk, wv, wg
    )
    input_grad = d_residual + reduce_group(dx.reshape(group, length, width))

    five = reduce_rows(grad_four).reshape(group, width // (segs * group), 5 * cw)
    five = lax.all_to_all(five, TP, 0, 0, tiled=True).astype(F32)
    block = width // (segs * group)
    five = five.reshape(group, block, 5, cw).transpose(2, 1, 0, 3).reshape(5, block, width)
    grad_out = lax.psum_scatter(tn(gated, d_att).astype(BF16), "seg", scatter_dimension=0, tiled=True)
    grad_out = lax.ppermute(
        grad_out, ALL, [(i * group + j, segs * j + i) for i in range(segs) for j in range(group)]
    ).astype(F32)

    own_rows = jnp.concatenate([jnp.sum(own_sums.reshape(4, 8, cw), 1), decay_up[:decays]], 0)
    own_rows = lax.dynamic_update_slice_in_dim(jnp.zeros((4 + decays, width), F32), own_rows, p * cw, 1)
    small = jnp.concatenate(
        [jnp.sum(row_sums.reshape(8, 8, width), 1), ffn_sums, own_rows, down[:ranks], up[:ranks], decay_down[:decays]], 0
    )
    count = small.shape[0]
    small = small.astype(BF16).reshape(count, segs, group, block).transpose(2, 1, 0, 3).reshape(group, segs * count, block)
    small = reduce_group(small).astype(BF16).reshape(segs, count, block)
    small = jnp.sum(lax.all_to_all(small, "seg", 0, 0, tiled=True).astype(F32), 0)
    norm_gain, norm_bias, shift_mix = small[0], small[1], small[2:8].T
    ffn_gain, ffn_bias, ffn_shift_mix = small[8], small[9], small[10:12].T
    decay_base, reward, group_gain, group_bias = small[12], small[13], small[14], small[15]
    at = 16
    d_up, at = small[at : at + decays].T, at + decays
    shift_down_grad, at = small[at : at + ranks].T, at + ranks
    shift_up_grad, at = small[at : at + ranks].T, at + ranks
    d_down = small[at : at + decays].T

    end_states = jnp.swapaxes(jnp.sum(ends.reshape(group, cw, heads, HEAD), 2), 1, 2)
    end_states = lax.all_to_all(end_states, TP, 0, 0, tiled=True).transpose(1, 0, 2).reshape(HEAD, width)
    return (
        output.astype(BF16)[None],
        end_states[None, None],
        input_grad[None],
        norm_gain,
        norm_bias,
        shift_mix,
        shift_down_grad,
        shift_up_grad,
        decay_base,
        d_down,
        d_up,
        reward,
        five[0],
        five[1],
        five[2],
        five[3],
        grad_out,
        group_gain,
        group_bias,
        ffn_gain,
        ffn_bias,
        ffn_shift_mix,
        grad_ffn_key,
        five[4],
        grad_ffn_value,
    )


def solution(mesh):
    rows, tokens = P("seg", None), P("seg", TP, None)
    matrix = P("seg", "chan")
    vector_out, matrix_out = P(ALL), P(ALL, None)
    ffn_out = P(("seg", "seq"), "chan")
    return jax.shard_map(
        on_device,
        mesh=mesh,
        in_specs=(tokens, P("seg", None, None), P("seg", None, None)) + (P(),) * 9 + (rows,) * 5 + (P(),) * 5
        + (matrix, rows, matrix, tokens, P("seg", TP, None, None)),
        out_specs=(tokens, P("seg", TP, None, None), tokens) + (vector_out,) * 2 + (matrix_out,) * 3 + (vector_out,)
        + (matrix_out,) * 2 + (vector_out,) + (matrix_out,) * 5 + (vector_out,) * 4
        + (matrix_out, ffn_out, matrix_out, ffn_out),
        check_vma=False,
    )
```

time: 4890 us -> 976 us (0.20)
  waiting for transfers between devices: 3650 us -> 524 us
  matrix products: 682 us -> 88.6 us
  other arithmetic: 179 us -> 41.8 us
  local copies, waits for them, and re-layouts: 230 us -> 110 us
  Pallas kernels: 0 us -> 115 us
    reduce_scatter x14 -> x4, waiting for transfers between devices: 2960 us -> 0.03 us  [the longest x3 0.02 us: reduce_rows(): lax.psum_scatter(a.astype(BF16), 'seg', scatter_dimension=0, tiled=True)]
    dot_general x99 -> x16, matrix products: 679 us -> 88.6 us  [dot(): lax.dot_general(a.astype(BF16), b.astype(BF16), (dims, ((), ())), preferr...]
    ppermute x4 -> x24, waiting for transfers between devices: 7.24 us -> 220 us  [the longest x15 153 us: reduce_group(): lax.ppermute(block, 'chan', [(i, (i + k) % chans) for i in range(chans)])]
    all_gather x12 -> x9, waiting for transfers between devices: 480 us -> 270 us  [the longest x4 135 us: gather_group(): return lax.all_gather(block, TP, axis=0, tiled=True)]
    unnamed x32 -> x13, waiting for transfers between devices: 206 us -> 1.55 us
    pallas_call x0 -> x3, Pallas kernels: none -> 115 us  [the longest x1 57.2 us: call_mix_backward(): pl.pallas_call(lambda *refs: mix_backward(rank, count, *refs), grid=(coun...]
    reduce_sum x26 -> x8, other arithmetic: 81.5 us -> 5.79 us  [the longest x1 1.79 us: unit_rows(): center = values - jnp.mean(values, -1, keepdims=True)]
    all_gather x2 -> x0, blocking collectives: 50.1 us -> none  [the longest x1 25.6 us: carried_in(): lax.all_gather(part.astype(kind), axis)]
  transfers between devices with their start and end apart: 33 -> 43, of which waited for: 27 -> 22; matrix products, arithmetic and copies ran while one was open for 12% -> 19% of each run, Pallas kernels for 0% -> 12%
where the time goes in v1:
time: 976 us; the launch traced here: 961 us
  waiting for transfers between devices  524 us (54%)
  Pallas kernels  115 us (12%)
  local copies, waits for them, and re-layouts  110 us (11%)
  matrix products  88.6 us (9%)
  starting transfers between devices  60.5 us (6%)
  other arithmetic  41.8 us (4%)
  between operations  15.3 us (2%)
    ppermute x15, waiting for transfers between devices, reduce_group(): lax.ppermute(block, 'chan', [(i, (i + k) % chans) for i in range(chans)])  153 us
    all_gather x4, waiting for transfers between devices, gather_group(): return lax.all_gather(block, TP, axis=0, tiled=True)  135 us
    all_gather x4, waiting for transfers between devices, gather_rows(): return lax.all_gather(a, 'seg', axis=0, tiled=True)  135 us
    dot_general x16, matrix products, dot(): lax.dot_general(a.astype(BF16), b.astype(BF16), (dims, ((), ())), preferr...  88.6 us
    pallas_call x1, Pallas kernels, call_mix_backward(): pl.pallas_call(lambda *refs: mix_backward(rank, count, *refs), grid=(coun...  57.2 us
    pallas_call x1, Pallas kernels, call_forward(): pl.pallas_call(lambda *refs: mix_forward(rank, *refs), grid=(count,), in_...  36.9 us
    ppermute x2, waiting for transfers between devices, next_row(): lax.ppermute(row, TP, [(i, i + by) for i in range(count) if 0 <= i + by <...  33.4 us
    all_to_all x1, waiting for transfers between devices, on_device(): lax.all_to_all(final_recurrence_adjoint[0, 0].reshape(HEAD, group, cw).tr...  27.1 us
  transfers between devices with their start and end apart: 43, of which 22 were waited for; matrix products, arithmetic and copies ran while one was open for 19% of the time, Pallas kernels for 12%

profile of v1, /device:TPU:1, one launch (start us, length us, event | category | flops | bytes accessed | tf_op | source)
XLA Modules:
  0.0 960.7 jit_solution(7749167208210882119)
XLA Ops:
  32.1 55.7 %all-gather.11.cloned.1.call-done = bf16[2048,1024]{1,0:T(8,128)(2,1)} async-done(((bf16[512,1024]{1,0:T(8,128)(2,1)}), bf16[2048,1024]{1,0:T(8,128)(2,1)}) %all-gather.11.cloned.1.call-update) | async-done | bytes 4194320 | tf_op jit(solution)/shard_map/all_gather | solution.py:524
  92.1 45.1 %all-gather.27.cloned.1.call-done = bf16[1,1024,2048]{2,1,0:T(8,128)(2,1)} async-done(((bf16[1,128,2048]{2,1,0:T(8,128)(2,1)}), bf16[1,1024,2048]{2,1,0:T(8,128)(2,1)}) %all-gather.27.cloned.1.call-update) | async-done | bytes 4194320 | tf_op jit(solution)/shard_map/all_gather | solution.py:444
  137.2 36.9 %mix_forward.1 = (bf16[1024,2048]{1,0:T(8,128)(2,1)}, bf16[1024,2048]{1,0:T(8,128)(2,1)}, bf16[1024,2048]{1,0:T(8,128)(2,1)}, bf16[1024,2048]{1,0:T(8,128)(2,1)}...) custom-call(bf16[1024,2048]{1,0:T(8,128)(2,1)} %bitcast.290, ...), custom_call_target="tpu_custom_call" | custom-call | flops 11274289152 | bytes 25165824 | tf_op jit(solution)/shard_map/mix_forward/pallas_call | solution.py:372
  192.0 11.8 %collective-permute-done.4 = bf16[128,2048]{1,0:T(8,128)(2,1)S(1)} collective-permute-done((bf16[128,2048]{1,0:T(8,128)(2,1)}, bf16[128,2048]{1,0:T(8,128)(2,1)S(1)}, u32[]{:S(2)}, u32[]{:S(2)}) %collective-permute-start.4) | collective-permute-done | bytes 524320 | tf_op jit(solution)/shard_map/ppermute | solution.py:460
  203.7 32.6 %collective-permute-done.3 = bf16[128,2048]{1,0:T(8,128)(2,1)S(1)} collective-permute-done((bf16[128,2048]{1,0:T(8,128)(2,1)}, bf16[128,2048]{1,0:T(8,128)(2,1)S(1)}, u32[]{:S(2)}, u32[]{:S(2)}) %collective-permute-start.3) | collective-permute-done | bytes 524320 | tf_op jit(solution)/shard_map/ppermute | solution.py:460
  245.8 42.8 %all-gather.17.cloned.1.call-done = bf16[1024,2048]{1,0:T(8,128)(2,1)} async-done(((bf16[128,2048]{1,0:T(8,128)(2,1)}), bf16[1024,2048]{1,0:T(8,128)(2,1)}) %all-gather.17.cloned.1.call-update) | async-done | bytes 4194320 | tf_op jit(solution)/shard_map/all_gather | solution.py:444
  298.8 38.2 %all-gather.19.cloned.1.call-done = bf16[2048,896]{1,0:T(8,128)(2,1)} async-done(((bf16[512,896]{1,0:T(8,128)(2,1)}), bf16[2048,896]{1,0:T(8,128)(2,1)}) %all-gather.19.cloned.1.call-update) | async-done | bytes 3670032 | tf_op jit(solution)/shard_map/all_gather | solution.py:524
  337.0 9.6 fusion.79
  346.6 41.1 %all-gather.21.cloned.1.call-done = bf16[2048,896]{1,0:T(8,128)(2,1)} async-done(((bf16[512,896]{1,0:T(8,128)(2,1)}), bf16[2048,896]{1,0:T(8,128)(2,1)}) %all-gather.21.cloned.1.call-update) | async-done | bytes 3670032 | tf_op jit(solution)/shard_map/all_gather | solution.py:524
  411.7 31.0 %collective-permute-done.5 = f32[1,2048]{1,0:T(1,128)S(1)} collective-permute-done((f32[1,2048]{1,0:T(1,128)S(1)}, f32[1,2048]{1,0:T(1,128)S(1)}, u32[]{:S(2)}, u32[]{:S(2)}) %collective-permute-start.5) | collective-permute-done | bytes 8224 | tf_op jit(solution)/shard_map/ppermute | solution.py:466
  442.8 9.5 collective-permute-done.8
  459.9 47.4 %all-gather.23.cloned.1.call-done = bf16[1024,2048]{1,0:T(8,128)(2,1)} async-done(((bf16[128,2048]{1,0:T(8,128)(2,1)}), bf16[1024,2048]{1,0:T(8,128)(2,1)}) %all-gather.23.cloned.1.call-update) | async-done | bytes 4194320 | tf_op jit(solution)/shard_map/all_gather | solution.py:444
  507.3 9.0 multiply_convert_fusion
  531.9 8.7 collective-permute-done.13
  540.5 32.6 %collective-permute-done.12 = bf16[128,2048]{1,0:T(8,128)(2,1)S(1)} collective-permute-done((bf16[128,2048]{1,0:T(8,128)(2,1)S(1)}, bf16[128,2048]{1,0:T(8,128)(2,1)S(1)}, u32[]{:S(2)}, u32[]{:S(2)}) %collective-permute-start.12) | collective-permute-done | bytes 524320 | tf_op jit(solution)/shard_map/ppermute | solution.py:460
  581.6 9.2 convolution_convert_fusion.4
  590.8 10.1 %convolution_convert_fusion.3 = bf16[2048,896]{1,0:T(8,128)(2,1)} fusion(bf16[1024,2048]{1,0:T(8,128)(2,1)} %all-gather.23.cloned.1.call-done, f32[1024,896]{1,0:T(8,128)} %fusion.79), kind=kOutput, calls=%fused_computation.13 | convolution fusion | flops 3762683904 | bytes 11534336 | tf_op jit(solution)/shard_map/dot_general | solution.py:20
  610.7 27.1 %all-to-all-done.1 = f32[8,64,256]{2,1,0:T(8,128)S(1)} async-done(((f32[8,64,256]{2,1,0:T(8,128)}), f32[8,64,256]{2,1,0:T(8,128)S(1)}, u32[]{:S(2)}, u32[]{:S(2)}) %all-to-all-start.1) | async-done | bytes 524320 | tf_op jit(solution)/shard_map/all_to_all | solution.py:576
  649.8 21.1 %wkv_backward.1 = (bf16[1024,256]{1,0:T(8,128)(2,1)}, bf16[1024,256]{1,0:T(8,128)(2,1)}, bf16[1024,256]{1,0:T(8,128)(2,1)}, bf16[1024,256]{1,0:T(8,128)(2,1)}, f32[1024,256]{1,0:T(8,128)}, /*index=5*/f32[32,256]{1,0:T(8,128)}) custom-call(f32[1024,256]{1,0:T(8,128)} %fusion.81.refs_0_, bf16[1024,256]{1,0:T(8,128)(2,1)} %get-tuple-element.55.refs_1_, ...), custom_call_target="tpu_custom_call" | custom-call | flops 3355443200 | bytes 10485760 | tf_op jit(solution)/shard_map/wkv_backward/pallas_call | solution.py:398
  701.6 57.2 %mix_backward.1 = (bf16[1024,2048]{1,0:T(8,128)(2,1)}, f32[64,2048]{1,0:T(8,128)}, f32[256,2048]{1,0:T(8,128)}, f32[256,2048]{1,0:T(8,128)}, f32[128,2048]{1,0:T(8,128)}, /*index=5*/f32[128,256]{1,0:T(8,128)}) custom-call(bf16[1024,2048]{1,0:T(8,128)(2,1)} %bitcast.291, bf16[1024,2048]{1,0:T(8,128)(2,1)} %bitcast.292, ...), custom_call_target="tpu_custom_call" | custom-call | flops 23622320128 | bytes 16777216 | tf_op jit(solution)/shard_map/mix_backward/pallas_call | solution.py:426
  813.9 15.8 %collective-permute-done.21 = bf16[1856,64]{0,1:T(8,128)(2,1)S(1)} collective-permute-done((bf16[1856,64]{0,1:T(8,128)(2,1)S(1)}, bf16[1856,64]{0,1:T(8,128)(2,1)S(1)}, u32[]{:S(2)}, u32[]{:S(2)}) %collective-permute-start.21) | collective-permute-done | bytes 237600 | tf_op jit(solution)/shard_map/ppermute | solution.py:460
  868.6 21.8 %collective-permute-done.23 = bf16[64,2048]{1,0:T(8,128)(2,1)S(1)} collective-permute-done((bf16[64,2048]{1,0:T(8,128)(2,1)}, bf16[64,2048]{1,0:T(8,128)(2,1)S(1)}, u32[]{:S(2)}, u32[]{:S(2)}) %collective-permute-start.23) | collective-permute-done | bytes 262176 | tf_op jit(solution)/shard_map/ppermute | solution.py:653
  891.2 40.0 %collective-permute-done.17 = bf16[128,2048]{1,0:T(8,128)(2,1)S(1)} collective-permute-done((bf16[128,2048]{1,0:T(8,128)(2,1)}, bf16[128,2048]{1,0:T(8,128)(2,1)S(1)}, u32[]{:S(2)}, u32[]{:S(2)}) %collective-permute-start.17) | collective-permute-done | bytes 524320 | tf_op jit(solution)/shard_map/ppermute | solution.py:460
  937.0 10.4 %fusion.76 = (f32[1,64,8,256]{3,0,1,2:T(1,128)S(1)}, f32[1,64,8,256]{3,0,1,2:T(1,128)S(1)}, f32[1,64,8,256]{3,0,1,2:T(1,128)S(1)}, f32[1,64,8,256]{3,0,1,2:T(1,128)S(1)}, f32[1,64,8,256]{3,0,1,2:T(1,128)S(1)}) fusion(f32[5,64,8,256]{3,0,1,2:T(8,128)} %bitcast.242), kind=kLoop, calls=%fused_computation.261 | loop fusion | bytes 5242880 | tf_op jit(solution)/shard_map/slice | solution.py:701
  (323 shorter events, 280.9 us)
Async XLA Ops:
  7.2 80.6 %all-gather.11.cloned.1.call-start = ((), (), s32[]{:S(2)}) async-start(), calls=%async_computation.11 | async-start | bytes 5242880 | tf_op jit(solution)/shard_map/all_gather | solution.py:524
  10.7 126.5 %all-gather.27.cloned.1.call-start = ((), (), s32[]{:S(2)}) async-start(), calls=%async_computation.23 | async-start | bytes 4718592 | tf_op jit(solution)/shard_map/all_gather | solution.py:444
  11.5 233.4 %all-gather.13.cloned.1.call-start = ((), (), s32[]{:S(2)}) async-start(), calls=%async_computation.12 | async-start | bytes 5242880 | tf_op jit(solution)/shard_map/all_gather | solution.py:524
  12.6 161.5 %collective-permute-start = (bf16[256,2048]{1,0:T(8,128)(2,1)}, bf16[256,2048]{1,0:T(8,128)(2,1)}, u32[]{:S(2)}, u32[]{:S(2)}) collective-permute-start(bf16[256,2048]{1,0:T(8,128)(2,1)} %constant_dynamic-slice_fusion.3), channel_id=1, source_target_pairs={{0,0},{1,1},{2,8},{3,9},{4,16},{5,17},{6,24},{7,25},{8,2},{9,3},{1... | collective-permute-start | bytes 3145736 | tf_op jit(solution)/shard_map/ppermute | solution.py:535
  19.6 269.0 %all-gather.17.cloned.1.call-start = ((), (), s32[]{:S(2)}) async-start(), calls=%async_computation.14 | async-start | bytes 4718592 | tf_op jit(solution)/shard_map/all_gather | solution.py:444
  190.6 45.7 %collective-permute-start.3 = (bf16[128,2048]{1,0:T(8,128)(2,1)}, bf16[128,2048]{1,0:T(8,128)(2,1)S(1)}, u32[]{:S(2)}, u32[]{:S(2)}) collective-permute-start(bf16[128,2048]{1,0:T(8,128)(2,1)} %get-tuple-element.281), channel_id=1, source_target_pairs={{0,2},{1,3},{2,0},{3,1},{4,6},{5,7},{6,4},{7,5},{8,10},{9,11},{10,... | collective-permute-start | bytes 1572872 | tf_op jit(solution)/shard_map/ppermute | solution.py:460
  190.6 45.7 %collective-permute-start.2 = (bf16[128,2048]{1,0:T(8,128)(2,1)S(1)}, bf16[128,2048]{1,0:T(8,128)(2,1)S(1)}, u32[]{:S(2)}, u32[]{:S(2)}) collective-permute-start(bf16[128,2048]{1,0:T(8,128)(2,1)S(1)} %get-tuple-element.279), channel_id=1, source_target_pairs={{0,1},{1,2},{2,3},{3,0},{4,5},{5,6},{6,7},{7,4},{8,9},{9,10},{10,1... | collective-permute-start | bytes 1572872 | tf_op jit(solution)/shard_map/ppermute | solution.py:460
  240.3 96.7 %all-gather.19.cloned.1.call-start = ((), (), s32[]{:S(2)}) async-start(), calls=%async_computation.15 | async-start | bytes 4587520 | tf_op jit(solution)/shard_map/all_gather | solution.py:524
  242.5 145.1 %all-gather.21.cloned.1.call-start = ((), (), s32[]{:S(2)}) async-start(), calls=%async_computation.16 | async-start | bytes 4587520 | tf_op jit(solution)/shard_map/all_gather | solution.py:524
  244.8 198.0 %all-gather.15.cloned.1.call-start = ((), (), s32[]{:S(2)}) async-start(), calls=%async_computation.13 | async-start | bytes 12582912 | tf_op jit(solution)/shard_map/all_gather | solution.py:546
  245.5 261.8 %all-gather.23.cloned.1.call-start = ((), (), s32[]{:S(2)}) async-start(), calls=%async_computation.17 | async-start | bytes 4718592 | tf_op jit(solution)/shard_map/all_gather | solution.py:444
  407.1 45.1 %collective-permute-start.8 = (bf16[128,2048]{1,0:T(8,128)(2,1)S(1)}, bf16[128,2048]{1,0:T(8,128)(2,1)}, u32[]{:S(2)}, u32[]{:S(2)}) collective-permute-start(bf16[128,2048]{1,0:T(8,128)(2,1)S(1)} %get-tuple-element.278), channel_id=1, source_target_pairs={{0,2},{1,3},{2,0},{3,1},{4,6},{5,7},{6,4},{7,5},{8,10},{9,11},{10,... | collective-permute-start | bytes 1572872 | tf_op jit(solution)/shard_map/ppermute | solution.py:460
  459.7 185.4 %all-gather.25.cloned.1.call-start = ((), (), s32[]{:S(2)}) async-start(), calls=%async_computation.18 | async-start | bytes 4718592 | tf_op jit(solution)/shard_map/all_gather | solution.py:444
  527.6 45.5 %collective-permute-start.12 = (bf16[128,2048]{1,0:T(8,128)(2,1)S(1)}, bf16[128,2048]{1,0:T(8,128)(2,1)S(1)}, u32[]{:S(2)}, u32[]{:S(2)}) collective-permute-start(bf16[128,2048]{1,0:T(8,128)(2,1)S(1)} %get-tuple-element.275), channel_id=1, source_target_pairs={{0,2},{1,3},{2,0},{3,1},{4,6},{5,7},{6,4},{7,5},{8,10},{9,11},{10,... | collective-permute-start | bytes 1572872 | tf_op jit(solution)/shard_map/ppermute | solution.py:460
  527.6 45.5 %collective-permute-start.11 = (bf16[128,2048]{1,0:T(8,128)(2,1)S(1)}, bf16[128,2048]{1,0:T(8,128)(2,1)S(1)}, u32[]{:S(2)}, u32[]{:S(2)}) collective-permute-start(bf16[128,2048]{1,0:T(8,128)(2,1)S(1)} %get-tuple-element.273), channel_id=1, source_target_pairs={{0,1},{1,2},{2,3},{3,0},{4,5},{5,6},{6,7},{7,4},{8,9},{9,10},{10,1... | collective-permute-start | bytes 1572872 | tf_op jit(solution)/shard_map/ppermute | solution.py:460
  581.1 206.9 %reduce-scatter.9.cloned.1.call-start = ((), (), s32[]{:S(2)}) async-start(), calls=%async_computation.21 | async-start | bytes 4587520 | tf_op jit(solution)/shard_map/reduce_scatter | solution.py:611
  590.8 204.5 %reduce-scatter.11.cloned.1.call-start = ((), (), s32[]{:S(2)}) async-start(), calls=%async_computation.22 | async-start | bytes 4587520 | tf_op jit(solution)/shard_map/reduce_scatter | solution.py:611
  644.9 197.0 %reduce-scatter.5.cloned.1.call-start = ((), (), s32[]{:S(2)}) async-start(), calls=%async_computation.19 | async-start | bytes 6553600 | tf_op jit(solution)/shard_map/reduce_scatter | solution.py:611
  696.1 90.8 %all-to-all-start = ((f32[8,64,256]{2,1,0:T(8,128)}), f32[8,64,256]{2,1,0:T(8,128)S(1)}, u32[]{:S(2)}, u32[]{:S(2)}) async-start(f32[8,64,256]{2,1,0:T(8,128)} %bitcast.33), calls=%async_computation | async-start | bytes 1048576 | tf_op jit(solution)/shard_map/all_to_all | solution.py:676
  799.3 61.7 %reduce-scatter.7.cloned.1.call-start = ((), (), s32[]{:S(2)}) async-start(), calls=%async_computation.20 | async-start | bytes 1310720 | tf_op jit(solution)/shard_map/reduce_scatter | solution.py:652
  802.5 48.1 %collective-permute-start.15 = (bf16[4,128,2048]{2,1,0:T(8,128)(2,1)}, bf16[4,128,2048]{2,1,0:T(8,128)(2,1)}, u32[]{:S(2)}, u32[]{:S(2)}) collective-permute-start(bf16[4,128,2048]{2,1,0:T(8,128)(2,1)} %dynamic-slice_bitcast_fusion), channel_id=1, source_target_pairs={{0,4},{4,0},{1,5},{5,1},{2,6},{6,2},{3,7},{7,3},{8,12},{12,8},{9,1... | collective-permute-start | bytes 6291464 | tf_op jit(solution)/shard_map/ppermute | solution.py:452
  844.3 89.8 %all-to-all-start.4 = ((bf16[8,64,1280]{2,1,0:T(8,128)(2,1)}), bf16[8,64,1280]{2,1,0:T(8,128)(2,1)S(1)}, u32[]{:S(2)}, u32[]{:S(2)}) async-start(bf16[8,64,1280]{2,1,0:T(8,128)(2,1)} %bitcast.70), calls=%async_computation.5 | async-start | bytes 2621440 | tf_op jit(solution)/shard_map/all_to_all | solution.py:649
  860.3 70.9 %collective-permute-start.17 = (bf16[128,2048]{1,0:T(8,128)(2,1)}, bf16[128,2048]{1,0:T(8,128)(2,1)S(1)}, u32[]{:S(2)}, u32[]{:S(2)}) collective-permute-start(bf16[128,2048]{1,0:T(8,128)(2,1)} %get-tuple-element.272), channel_id=1, source_target_pairs={{0,2},{1,3},{2,0},{3,1},{4,6},{5,7},{6,4},{7,5},{8,10},{9,11},{10,... | collective-permute-start | bytes 1572872 | tf_op jit(solution)/shard_map/ppermute | solution.py:460
  860.3 70.9 %collective-permute-start.16 = (bf16[128,2048]{1,0:T(8,128)(2,1)}, bf16[128,2048]{1,0:T(8,128)(2,1)S(1)}, u32[]{:S(2)}, u32[]{:S(2)}) collective-permute-start(bf16[128,2048]{1,0:T(8,128)(2,1)} %get-tuple-element.270), channel_id=1, source_target_pairs={{0,1},{1,2},{2,3},{3,0},{4,5},{5,6},{6,7},{7,4},{8,9},{9,10},{10,1... | collective-permute-start | bytes 1572872 | tf_op jit(solution)/shard_map/ppermute | solution.py:460
  (58 other events, 877.8 us)
Sparse Core Ops, SparseCore 0:
  10.8 76.9 all-gather.10
  89.4 47.7 all-gather.26
  139.1 51.0 all-gather.12
  240.4 48.1 all-gather.16
  290.3 46.6 all-gather.18
  339.3 48.3 all-gather.20
  389.2 20.2 all-gather.14
  459.8 47.4 all-gather.22
  581.2 60.4 all-gather.24
  644.5 46.6 reduce-scatter.8
  694.2 48.3 reduce-scatter.10
  745.4 61.4 reduce-scatter.4
  811.9 29.7 reduce-scatter.6

commit v2 on v1

v2 whole, which is shorter than its diff:
```python
import jax
import jax.numpy as jnp
import numpy as np
from jax import lax
from jax.experimental import pallas as pl
from jax.experimental.pallas import tpu as pltpu
from jax.sharding import PartitionSpec as P

HEAD = 64
TP = ("seq", "chan")
ALL = ("seg", "seq", "chan")
LAYER_EPSILON = 1e-05
GROUP_EPSILON = 0.00064
F32 = jnp.float32
BF16 = jnp.bfloat16
CHUNK = 256
VMEM = 56 * 2**20


def dot(a, b, dims):
    return lax.dot_general(
        a.astype(BF16), b.astype(BF16), (dims, ((), ())), preferred_element_type=F32
    )


def nn(a, b):
    return dot(a, b, ((1,), (0,)))


def nt(a, b):
    return dot(a, b, ((1,), (1,)))


def tn(a, b):
    return dot(a, b, ((0,), (0,)))


def iota(shape, axis):
    return lax.broadcasted_iota(jnp.int32, shape, axis)


def head_sum(values, ones):
    high = values.astype(BF16)
    low = (values - high.astype(F32)).astype(BF16)
    return nn(high, ones) + nn(low, ones)


def pyramid(w):
    length = w.shape[0]
    row = iota(w.shape, 0)
    before, after, total = jnp.zeros_like(w), jnp.zeros_like(w), w
    levels = []
    half = 1
    while half < length:
        upper = (row & half) != 0
        levels.append((half, upper, jnp.where(upper, before, after)))
        sibling = jnp.where(upper, pltpu.roll(total, half, 0), pltpu.roll(total, length - half, 0))
        before = jnp.where(upper, before + sibling, before)
        after = jnp.where(upper, after, after + sibling)
        total = total + sibling
        half *= 2
    return levels, before, after, total


def split_heads(values, heads):
    if heads == 1:
        return [values.astype(BF16)]
    lane = iota(values.shape, 1) // HEAD
    return [jnp.where(lane == head, values, 0.0).astype(BF16) for head in range(heads)]


def row_stats(x_ref):
    rows, width = x_ref.shape
    step = 128
    total = jnp.zeros((rows, step), F32)
    for at in range(0, width, step):
        total = total + x_ref[:, at : at + step].astype(F32)
    mean = jnp.sum(total, 1, keepdims=True) / width
    total = jnp.zeros((rows, step), F32)
    for at in range(0, width, step):
        center = x_ref[:, at : at + step].astype(F32) - mean
        total = total + center * center
    return mean, lax.rsqrt(jnp.sum(total, 1, keepdims=True) / width + LAYER_EPSILON)


def fold(values):
    rows, width = values.shape
    return jnp.sum(values.reshape(rows // 8, 8, width), 0)


def rank_blocks(values, rank):
    lane = iota(values.shape, 1) // rank
    return jnp.concatenate([jnp.where(lane == j, values, 0.0).astype(BF16) for j in range(5)], 0)


def spread(states, same):
    flat = states.T
    return jnp.concatenate([flat] * (flat.shape[0] // HEAD), 1) * same


def compact(state):
    return sum(state[:, at : at + HEAD] for at in range(0, state.shape[1], HEAD)).T


def part_copies(place_ref, parts, full_ref, sem):
    rows = parts[0].shape[0]
    copies = []
    for m, part in enumerate(parts):
        at = pl.multiple_of((place_ref[0] ^ m) * rows, rows)
        copies.append(pltpu.make_async_copy(part, full_ref.at[pl.ds(at, rows), :], sem.at[m]))
    return copies


def load_parts(place_ref, parts, full_ref, sem):
    for copy in part_copies(place_ref, parts, full_ref, sem):
        copy.start()


def wait_parts(place_ref, parts, full_ref, sem):
    @pl.when(pl.program_id(0) == 0)
    def _():
        for copy in part_copies(place_ref, parts, full_ref, sem):
            copy.wait()


GAIN, BIAS, MIX, FIRST = 0, 1, 2, 8


def mix_forward(
    rank, x_ref, rows_ref, own_ref, wn_ref, ww_ref, fn_ref, fw_ref,
    ones_ref, start_ref, place_ref, part0, part1, part2, part3, *refs,
):
    (
        gated_ref, xk_ref, xv_ref, xr_ref, xg_ref, r_ref, k_ref, v_ref, w_ref, graw_ref, wkv_ref, lm_ref, dm_ref,
        ends_ref, normed_ref, delta_ref, carry_ref, state_ref, four_ref, sem,
    ) = refs[-20:]
    step = pl.program_id(0)
    length, width = x_ref.shape
    own = own_ref.shape[1]
    heads = own // HEAD

    @pl.when(step == 0)
    def _():
        carry_ref[...] = jnp.broadcast_to(rows_ref[FIRST : FIRST + 1, :], carry_ref.shape)
        state_ref[...] = spread(start_ref[...], ones_ref[...].astype(F32))
        load_parts(place_ref, (part0, part1, part2, part3), four_ref, sem)

    mean, scale = row_stats(x_ref)
    first = iota((length, CHUNK), 0) == 0
    narrow = jnp.zeros((length, wn_ref.shape[0]), F32)
    for at in range(0, width, CHUNK):
        c = slice(at, at + CHUNK)
        normed = (x_ref[:, c].astype(F32) - mean) * scale * rows_ref[GAIN : GAIN + 1, c] + rows_ref[BIAS : BIAS + 1, c]
        delta = jnp.where(first, carry_ref[0:1, c], pltpu.roll(normed, 1, 0)) - normed
        carry_ref[0:1, c] = normed[length - 1 : length, :]
        normed_ref[:, c] = normed
        delta_ref[:, c] = delta
        narrow = narrow + nt(normed + delta * rows_ref[MIX : MIX + 1, c], wn_ref[:, c])
    middle = jnp.tanh(narrow)
    lm_ref[...] = middle
    blocks = rank_blocks(middle, rank)
    decay_in = jnp.zeros((length, fn_ref.shape[0]), F32)
    for at in range(0, width, CHUNK):
        c = slice(at, at + CHUNK)
        normed, delta = normed_ref[:, c], delta_ref[:, c]
        modifiers = nn(blocks, ww_ref[:, c])
        for j, ref in enumerate((None, xk_ref, xv_ref, xr_ref, xg_ref)):
            modifier = modifiers[j * length : (j + 1) * length, :]
            mixed = (normed + delta * (rows_ref[MIX + 1 + j : MIX + 2 + j, c] + modifier)).astype(BF16)
            if ref is None:
                decay_in = decay_in + nt(mixed, fn_ref[:, c])
            else:
                ref[:, c] = mixed
    decay_mid = jnp.tanh(decay_in)
    dm_ref[...] = decay_mid
    w = -jnp.exp(own_ref[0:1, :] + nn(decay_mid, fw_ref[...]))
    w_ref[...] = w
    wait_parts(place_ref, (part0, part1, part2, part3), four_ref, sem)
    r = nn(xr_ref[...], four_ref[:, :own]).astype(BF16)
    k = nn(xk_ref[...], four_ref[:, own : 2 * own]).astype(BF16)
    v = nn(xv_ref[...], four_ref[:, 2 * own : 3 * own]).astype(BF16)
    graw = nn(xg_ref[...], four_ref[:, 3 * own :])
    r_ref[...], k_ref[...], v_ref[...], graw_ref[...] = r, k, v, graw

    rf, kf, vf = r.astype(F32), k.astype(F32), v.astype(F32)
    levels, before, after, total = pyramid(w)
    row, col = iota((length, length), 0), iota((length, length), 1)
    apart = jnp.where(row > col, row ^ col, 0)
    scores = [jnp.zeros((length, length), F32)] * heads
    for half, upper, exponent in levels:
        scaled = jnp.where(upper, rf, kf) * jnp.exp(exponent)
        flat = scaled.astype(BF16)
        here = (apart >= half) & (apart < 2 * half)
        for head, one in enumerate(split_heads(scaled, heads)):
            scores[head] = jnp.where(here, nt(one, flat), scores[head])
    ones = ones_ref[...]
    wkv = nn(jnp.concatenate([s.astype(BF16) for s in scores], 1), jnp.concatenate(split_heads(vf, heads), 0))
    state = state_ref[...]
    wkv = wkv + nt(rf * jnp.exp(before), state) + head_sum(rf * own_ref[1:2, :] * kf, ones) * vf
    wkv_ref[...] = wkv
    state = state * jnp.exp(total[0:1, :]) + tn(v, kf * jnp.exp(after)) * ones.astype(F32)
    state_ref[...] = state
    ends_ref[0] = compact(state)

    center = wkv - head_sum(wkv, ones) / HEAD
    variance = head_sum(center * center, ones) / HEAD
    grouped = center * lax.rsqrt(variance + GROUP_EPSILON) * own_ref[2:3, :] + own_ref[3:4, :]
    gated_ref[...] = (grouped * graw * jax.nn.sigmoid(graw)).astype(BF16)


def wkv_backward(
    d_ref, r_ref, k_ref, v_ref, w_ref, graw_ref, wkv_ref, dm_ref, w_out_ref, own_ref, ones_ref, sums_ref, start_ref,
    ends_ref, adj_ref, *refs,
):
    own_sums_ref, decay_up_ref, dr_ref, dk_ref, dv_ref, dg_ref, dpre_ref, state_ref = refs[-8:]
    step = pl.program_id(0)
    length, own = r_ref.shape
    heads = own // HEAD
    ones = ones_ref[...]

    @pl.when(step == 0)
    def _():
        for ref in (state_ref, own_sums_ref, decay_up_ref):
            ref[...] = jnp.zeros_like(ref)

    reward, gain, bias = own_ref[1:2, :], own_ref[2:3, :], own_ref[3:4, :]
    wkv, graw, d_gated = wkv_ref[...], graw_ref[...], nt(d_ref[...], w_out_ref[...])
    center = wkv - head_sum(wkv, ones) / HEAD
    scale = lax.rsqrt(head_sum(center * center, ones) / HEAD + GROUP_EPSILON)
    normed = center * scale
    sigma = jax.nn.sigmoid(graw)
    d_grouped = d_gated * graw * sigma
    dg_ref[...] = (d_gated * (normed * gain + bias) * sigma * (1.0 + graw * (1.0 - sigma))).astype(BF16)
    d_normed = d_grouped * gain
    do = scale * (d_normed - head_sum(d_normed, ones) / HEAD - normed * (head_sum(d_normed * normed, ones) / HEAD))

    rb, kb, vb, dob = r_ref[...], k_ref[...], v_ref[...], do.astype(BF16)
    r, k, v, w = rb.astype(F32), kb.astype(F32), vb.astype(F32), w_ref[...]
    levels, before, after, total = pyramid(w)
    same = ones.astype(F32)
    d_state = state_ref[...] + spread(adj_ref[0], same)
    state = spread(jnp.where(step == pl.num_programs(0) - 1, start_ref[...], ends_ref[0]), same)
    d_flat, flat = d_state.astype(BF16), state.astype(BF16)
    from_start, to_end, decay = jnp.exp(before), jnp.exp(after), jnp.exp(total[0:1, :])
    dr = from_start * nn(dob, flat)
    dk = to_end * nn(vb, d_flat)
    dv = nt(k * to_end, d_flat)
    through = [r * dr, k * dk]
    state_ref[...] = d_state * decay + tn(dob, r * from_start) * same
    whole = decay * jnp.sum(state * d_state, 0, keepdims=True)

    row, col = iota((length, length), 0), iota((length, length), 1)
    apart = row ^ col
    do_heads, v_heads = split_heads(do, heads), split_heads(v, heads)
    d_scores = [
        jnp.where(row > col, nt(do_heads[h], vb), jnp.where(row < col, nt(v_heads[h], dob), 0.0)).astype(BF16)
        for h in range(heads)
    ]
    scores = [jnp.zeros((length, length), F32)] * heads
    for half, upper, exponent in levels:
        factor = jnp.exp(exponent)
        scaled = jnp.where(upper, r, k) * factor
        mine = split_heads(scaled, heads)
        here = (apart >= half) & (apart < 2 * half)
        late = here & (row < col)
        for h in range(heads):
            scores[h] = jnp.where(late, nt(mine[h], scaled), scores[h])
        pulled = nn(
            jnp.concatenate([jnp.where(here, d, 0.0).astype(BF16) for d in d_scores], 1), jnp.concatenate(mine, 0)
        )
        if half > 1:
            through.append(scaled * pulled)
        pulled = pulled * factor
        dr = dr + jnp.where(upper, pulled, 0.0)
        dk = dk + jnp.where(upper, 0.0, pulled)
    dv = dv + nn(jnp.concatenate([s.astype(BF16) for s in scores], 1), jnp.concatenate(do_heads, 0))
    met = head_sum(v * do, ones)
    dr = dr + reward * k * met
    dk = dk + reward * r * met
    dv = dv + head_sum(r * reward * k, ones) * do
    d_log = whole + nn(sums_ref[...], jnp.concatenate([q.astype(BF16) for q in through], 0))
    d_pre = d_log * w
    dr_ref[...], dk_ref[...], dv_ref[...] = dr.astype(BF16), dk.astype(BF16), dv.astype(BF16)
    dpre_ref[...] = d_pre
    decay_up_ref[...] += tn(dm_ref[...], d_pre)
    for i, part in enumerate((d_pre, r * k * met, d_grouped * normed, d_grouped)):
        own_sums_ref[8 * i : 8 * i + 8, :] += fold(part)


def sum_table(length):
    row, col = np.arange(length)[:, None], np.arange(length)[None, :]
    tables = [col > row, col < row]
    half = 2
    while half < length:
        inside = (row // half) == (col // half)
        upper = (row // half) % 2 == 1
        tables.append(inside & np.where(upper, col > row, col < row))
        half *= 2
    return jnp.asarray(np.concatenate(tables, 1), BF16)


def mix_backward(rank, halves, *refs):
    (
        place_ref, x_ref, edge_ref, rows_ref, lm_ref, dm_ref, dr_ref, dk_ref, dv_ref, dg_ref, dpre_ref,
        wn_ref, ww_ref, fn_ref, fw_ref, more_ref, part0, part1, part2, part3,
    ) = refs[:20]
    packed_ref = refs[-13 - halves]
    outs = refs[-12 - halves : -12]
    (
        row_sums_ref, up_ref, down_ref, decay_down_ref, dx_ref, carry_ref, sum_ref, coef_ref, normed_ref, delta_ref,
        four_ref, sem,
    ) = refs[-12:]
    step = pl.program_id(0)
    from_first = pl.num_programs(0) - 1 - step
    length, width = x_ref.shape

    @pl.when(step == 0)
    def _():
        load_parts(place_ref, (part0, part1, part2, part3), four_ref, sem)
        for ref in (carry_ref, row_sums_ref, up_ref, down_ref, decay_down_ref):
            ref[...] = jnp.zeros_like(ref)

    own = dr_ref.shape[1]
    mean, scale = row_stats(x_ref)
    edge = edge_ref.shape[0]
    edge_mean, edge_scale = row_stats(edge_ref)
    middle, decay_mid = lm_ref[...], dm_ref[...]
    blocks = rank_blocks(middle, rank)
    d_pre = dpre_ref[...]
    d_decay = (nt(d_pre, fw_ref[...]) * (1.0 - decay_mid * decay_mid)).astype(BF16)
    sources = ((d_decay, None), (dk_ref[...], own), (dv_ref[...], 2 * own), (dr_ref[...], 0), (dg_ref[...], 3 * own))
    first = iota((length, CHUNK), 0) == 0
    last = iota((length, CHUNK), 0) == length - 1
    d_mid = jnp.zeros((5 * length, wn_ref.shape[0]), F32)
    wait_parts(place_ref, (part0, part1, part2, part3), four_ref, sem)
    for at in range(0, width, CHUNK):
        c = slice(at, at + CHUNK)
        gain, bias = rows_ref[GAIN : GAIN + 1, c], rows_ref[BIAS : BIAS + 1, c]
        normed = (x_ref[:, c].astype(F32) - mean) * scale * gain + bias
        edge_normed = (edge_ref[:, c].astype(F32) - edge_mean) * edge_scale * gain + bias
        before = jnp.where(from_first == 0, rows_ref[FIRST : FIRST + 1, c], edge_normed[edge - 1 : edge, :])
        delta = jnp.where(first, before, pltpu.roll(normed, 1, 0)) - normed
        normed_ref[:, c] = normed
        delta_ref[:, c] = delta
        modifiers = nn(blocks, ww_ref[:, c])
        total = jnp.zeros_like(normed)
        by_coef = jnp.zeros_like(normed)
        d_mods = []
        for j, (d, begin) in enumerate(sources):
            d_mixed = nt(d, four_ref[c, begin : begin + own]) if j else nn(d, fn_ref[:, c])
            coef = rows_ref[MIX + 1 + j : MIX + 2 + j, c] + modifiers[j * length : (j + 1) * length, :]
            if j == 0:
                decay_down_ref[:, c] += tn(d_decay, normed + delta * coef)
            d_mod = delta * d_mixed
            row_sums_ref[8 * (MIX + 1 + j) : 8 * (MIX + 2 + j), c] += fold(d_mod)
            d_mods.append(d_mod.astype(BF16))
            total = total + d_mixed
            by_coef = by_coef + d_mixed * coef
        d_mods = jnp.concatenate(d_mods, 0)
        up_ref[:, c] += tn(blocks, d_mods)
        d_mid = d_mid + nt(d_mods, ww_ref[:, c])
        sum_ref[:, c] = total
        coef_ref[:, c] = by_coef
    lane = iota(middle.shape, 1) // rank
    d_low = jnp.zeros_like(middle)
    for j in range(5):
        d_low = jnp.where(lane == j, d_mid[j * length : (j + 1) * length, :], d_low)
    d_low = (d_low * (1.0 - middle * middle)).astype(BF16)
    sum_g = jnp.zeros((length, CHUNK), F32)
    sum_gn = jnp.zeros((length, CHUNK), F32)
    for at in range(0, width, CHUNK):
        c = slice(at, at + CHUNK)
        normed, delta = normed_ref[:, c], delta_ref[:, c]
        mix = rows_ref[MIX : MIX + 1, c]
        d_in = nn(d_low, wn_ref[:, c])
        down_ref[:, c] += tn(d_low, normed + delta * mix)
        row_sums_ref[8 * MIX : 8 * MIX + 8, c] += fold(delta * d_in)
        d_delta = coef_ref[:, c] + d_in * mix
        above = jnp.where(last, carry_ref[0:1, c], pltpu.roll(d_delta, length - 1, 0))
        carry_ref[0:1, c] = d_delta[0:1, :]
        d_normed = sum_ref[:, c] + d_in - d_delta + above
        unit = (x_ref[:, c].astype(F32) - mean) * scale
        row_sums_ref[8 * GAIN : 8 * GAIN + 8, c] += fold(d_normed * unit)
        row_sums_ref[8 * BIAS : 8 * BIAS + 8, c] += fold(d_normed)
        g = d_normed * rows_ref[GAIN : GAIN + 1, c]
        sum_g = sum_g + g
        sum_gn = sum_gn + g * unit
        sum_ref[:, c] = g
    mean_g = jnp.sum(sum_g, 1, keepdims=True) / width
    mean_gn = jnp.sum(sum_gn, 1, keepdims=True) / width
    for at in range(0, width, CHUNK):
        c = slice(at, at + CHUNK)
        unit = (x_ref[:, c].astype(F32) - mean) * scale
        dx_ref[:, c] = (scale * (sum_ref[:, c] - mean_g - unit * mean_gn)).astype(BF16)
    store_half(place_ref, dx_ref, outs, from_first)

    @pl.when(step == pl.num_programs(0) - 1)
    def _():
        at = 16
        packed_ref[0:at, :] = jnp.zeros((at, width), BF16)
        for i in range(8):
            packed_ref[i : i + 1, :] = jnp.sum(row_sums_ref[8 * i : 8 * i + 8, :], 0, keepdims=True).astype(BF16)
        more = more_ref.shape[0]
        decays = packed_ref.shape[0] - at - 10 * rank - more
        for ref, size in ((down_ref, 5 * rank), (up_ref, 5 * rank), (decay_down_ref, decays), (more_ref, more)):
            packed_ref[at : at + size, :] = ref[0:size, :].astype(BF16)
            at += size


def whole(a):
    return pl.BlockSpec(a.shape, lambda t: (0,) * a.ndim)


def params(**more):
    return pltpu.CompilerParams(
        dimension_semantics=("arbitrary",), vmem_limit_bytes=VMEM, **more
    )


def light():
    return pl.CostEstimate(flops=0, bytes_accessed=0, transcendentals=0)


def pinned(pins):
    return [pl.BlockSpec(memory_space=pl.ANY)] * len(pins)


def part_specs(parts):
    return [pl.BlockSpec(memory_space=pltpu.SMEM)] + [pl.BlockSpec(memory_space=pl.ANY)] * len(parts)


def part_scratch(parts):
    rows, columns = parts[0].shape
    return [pltpu.VMEM((len(parts) * rows, columns), BF16), pltpu.SemaphoreType.DMA((len(parts),))]


def call_forward(rank, length, x, rows, own, wn, ww, fn, fw, ones, start, place, parts, pins):
    tokens, width = x.shape
    cw = own.shape[1]
    count = tokens // length
    tile = lambda n: pl.BlockSpec((length, n), lambda t: (t, 0))
    shape = lambda n, dtype: jax.ShapeDtypeStruct((tokens, n), dtype)
    fixed = (rows, own, wn, ww, fn, fw, ones, start)
    return pl.pallas_call(
        lambda *refs: mix_forward(rank, *refs),
        grid=(count,),
        in_specs=[tile(width)] + [whole(a) for a in fixed] + part_specs(parts) + pinned(pins),
        out_specs=[tile(cw)] + [tile(width)] * 4 + [tile(cw)] * 6 + [tile(wn.shape[0]), tile(fn.shape[0])]
        + [pl.BlockSpec((1, HEAD, cw), lambda t: (t, 0, 0))],
        out_shape=[shape(cw, BF16)] + [shape(width, BF16)] * 4 + [shape(cw, BF16)] * 3 + [shape(cw, F32)] * 3
        + [shape(wn.shape[0], F32), shape(fn.shape[0], F32), jax.ShapeDtypeStruct((count, HEAD, cw), F32)],
        scratch_shapes=[
            pltpu.VMEM((length, width), F32), pltpu.VMEM((length, width), F32), pltpu.VMEM((8, width), F32),
            pltpu.VMEM((cw, cw), F32),
        ]
        + part_scratch(parts),
        compiler_params=params(),
        cost_estimate=light(),
        name="mix_forward",
    )(x, *fixed, place, *parts, *pins)


def two_halves(tokens, width, length, seqs, backward=False):
    half = tokens // length // 2
    order = (lambda t: tokens // length - 1 - t) if backward else (lambda t: t)
    if seqs != 2:
        return [pl.BlockSpec((length, width), lambda t, place: (order(t), 0))], [jax.ShapeDtypeStruct((tokens, width), BF16)]
    mine = lambda t, place: (jnp.clip(order(t) - place[1] * half, 0, half - 1), 0)
    other = lambda t, place: (jnp.clip(order(t) - (1 - place[1]) * half, 0, half - 1), 0)
    return (
        [pl.BlockSpec((length, width), mine), pl.BlockSpec((length, width), other)],
        [jax.ShapeDtypeStruct((tokens // 2, width), BF16)] * 2,
    )


def store_half(place_ref, value_ref, outs, tile=None):
    if len(outs) == 1:
        outs[0][...] = value_ref[...]
        return
    tile = pl.program_id(0) if tile is None else tile
    is_mine = tile // (pl.num_programs(0) // 2) == place_ref[1]

    @pl.when(is_mine)
    def _():
        outs[0][...] = value_ref[...]

    @pl.when(jnp.logical_not(is_mine))
    def _():
        outs[1][...] = value_ref[...]


def ffn_forward(halves, place_ref, x_ref, edge_ref, rows_ref, w_all, *refs):
    key_ref, recept_ref, hidden_ref, squared_ref = refs[-7 - halves : -3 - halves]
    outs = refs[-3 - halves : -3]
    w_ref, value_ref, sem = refs[-3:]
    length, width = x_ref.shape
    units = hidden_ref.shape[1]
    edge = edge_ref.shape[0]
    load = pltpu.make_async_copy(w_all, w_ref, sem)

    @pl.when(pl.program_id(0) == 0)
    def _():
        load.start()

    first = iota((length, CHUNK), 0) == 0
    for at in range(0, width, CHUNK):
        c = slice(at, at + CHUNK)
        normed = x_ref[:, c].astype(F32)
        before = jnp.where(pl.program_id(0) == 0, rows_ref[2:3, c], edge_ref[edge - 1 : edge, c].astype(F32))
        delta = jnp.where(first, before, pltpu.roll(normed, 1, 0)) - normed
        key_ref[:, c] = (normed + delta * rows_ref[3:4, c]).astype(BF16)
        recept_ref[:, c] = (normed + delta * rows_ref[4:5, c]).astype(BF16)

    @pl.when(pl.program_id(0) == 0)
    def _():
        load.wait()

    hidden = jnp.maximum(nn(key_ref[...], w_ref[:, :units]), 0.0)
    hidden_ref[...] = hidden
    squared = (hidden * hidden).astype(BF16)
    squared_ref[...] = squared
    for at in range(0, width, 2 * CHUNK):
        c = slice(at, at + 2 * CHUNK)
        value_ref[:, c] = nt(squared, w_ref[c, units:]).astype(BF16)
    store_half(place_ref, value_ref, outs)


def call_ffn_forward(x, rows, w, place, seqs, pins):
    tokens, width = x.shape
    length, edge = 256, 16
    units = w.shape[1] // 2
    tile = lambda n: pl.BlockSpec((length, n), lambda t, place: (t, 0))
    shape = lambda n, dtype: jax.ShapeDtypeStruct((tokens, n), dtype)
    specs, shapes = two_halves(tokens, width, length, seqs)
    return pl.pallas_call(
        lambda *refs: ffn_forward(len(specs), *refs),
        grid_spec=pltpu.PrefetchScalarGridSpec(
            num_scalar_prefetch=1,
            grid=(tokens // length,),
            in_specs=[
                tile(width),
                pl.BlockSpec((edge, width), lambda t, place: (jnp.maximum(t * (length // edge) - 1, 0), 0)),
                pl.BlockSpec(rows.shape, lambda t, place: (0, 0)),
            ]
            + pinned([w]) + pinned(pins),
            out_specs=[tile(width)] * 2 + [tile(units)] * 2 + specs,
            scratch_shapes=[
                pltpu.VMEM(w.shape, BF16), pltpu.VMEM((length, width), BF16), pltpu.SemaphoreType.DMA,
            ],
        ),
        out_shape=[shape(width, BF16)] * 2 + [shape(units, F32), shape(units, BF16)] + shapes,
        compiler_params=params(),
        cost_estimate=light(),
        name="ffn_forward",
    )(place, x, x, rows, w, *pins)


def call_ffn_gate(recept, cot_mine, cot_other, gate, place, pins):
    tokens, width = recept.shape
    length = 256
    half = gate.shape[1]
    step = min(2 * CHUNK, half)
    rows = 128
    tiles, per = tokens // length, length // rows
    split = cot_mine.shape[0] < tiles * per

    def kernel(place_ref, recept_ref, mine_ref, other_ref, gate_ref, *refs):
        recept = recept_ref[...]
        is_mine = pl.program_id(0) // (tiles // 2) == place_ref[1]
        for at in range(0, half, step):
            c = slice(at, at + step)
            gate = jax.nn.sigmoid(nn(recept, gate_ref[:, c]))
            for i in range(per):
                r = slice(i * rows, (i + 1) * rows)
                cot = jnp.where(is_mine, mine_ref[i, :, c].astype(F32), other_ref[i, :, c].astype(F32))
                refs[-1][r, c] = (cot * gate[r, :]).astype(BF16)

    column = (lambda place: place[1]) if half < width else (lambda place: 0)

    def cot_spec(core):
        if not split:
            return pl.BlockSpec((per, rows, half), lambda t, place: (t, 0, column(place)))
        at = lambda t, place: jnp.clip(t - core(place) * (tiles // 2), 0, tiles // 2 - 1)
        return pl.BlockSpec((per, rows, half), lambda t, place: (at(t, place), 0, column(place)))

    return pl.pallas_call(
        kernel,
        grid_spec=pltpu.PrefetchScalarGridSpec(
            num_scalar_prefetch=1,
            grid=(tiles,),
            in_specs=[
                pl.BlockSpec((length, width), lambda t, place: (t, 0)),
                cot_spec(lambda place: place[1]), cot_spec(lambda place: 1 - place[1]),
                pl.BlockSpec(gate.shape, lambda t, place: (0, 0), pipeline_mode=pl.Buffered(1)),
            ]
            + pinned(pins),
            out_specs=pl.BlockSpec((length, half), lambda t, place: (t, 0)),
        ),
        out_shape=jax.ShapeDtypeStruct((tokens, half), BF16),
        compiler_params=params(),
        cost_estimate=light(),
        name="ffn_gate",
    )(place, recept, cot_mine, cot_other, gate, *pins)


def ffn_backward(halves, place_ref, mine_ref, other_ref, hidden_ref, w_all, *refs):
    d_values_ref, d_hidden_ref = refs[-5 - halves : -3 - halves]
    outs = refs[-3 - halves : -3]
    w_ref, value_ref, sem = refs[-3:]
    width = d_values_ref.shape[1]
    half = mine_ref.shape[1]
    units = hidden_ref.shape[1]
    load = pltpu.make_async_copy(w_all, w_ref, sem)

    @pl.when(pl.program_id(0) == 0)
    def _():
        load.start()

    cores = ((mine_ref, place_ref[1]), (other_ref, 1 - place_ref[1])) if half < width else ((mine_ref, 0),)
    for ref, core in cores:
        d_values_ref[:, pl.ds(pl.multiple_of(core * half, half), half)] = ref[...]

    @pl.when(pl.program_id(0) == 0)
    def _():
        load.wait()

    d_hidden = (nn(d_values_ref[...], w_ref[:, units:]) * 2.0 * hidden_ref[...]).astype(BF16)
    d_hidden_ref[...] = d_hidden
    for at in range(0, width, 2 * CHUNK):
        c = slice(at, at + 2 * CHUNK)
        value_ref[:, c] = nt(d_hidden, w_ref[c, :units]).astype(BF16)
    store_half(place_ref, value_ref, outs)


def call_ffn_backward(mine, other, hidden, w, place, seqs, pins):
    tokens, half = mine.shape
    width = w.shape[0]
    length = 256
    units = hidden.shape[1]
    tile = lambda n: pl.BlockSpec((length, n), lambda t, place: (t, 0))
    shape = lambda n: jax.ShapeDtypeStruct((tokens, n), BF16)
    specs, shapes = two_halves(tokens, width, length, seqs)
    return pl.pallas_call(
        lambda *refs: ffn_backward(len(specs), *refs),
        grid_spec=pltpu.PrefetchScalarGridSpec(
            num_scalar_prefetch=1,
            grid=(tokens // length,),
            in_specs=[tile(half), tile(half), tile(units)] + pinned([w]) + pinned(pins),
            out_specs=[tile(width), tile(units)] + specs,
            scratch_shapes=[
                pltpu.VMEM(w.shape, BF16), pltpu.VMEM((length, width), BF16), pltpu.SemaphoreType.DMA,
            ],
        ),
        out_shape=[shape(width), shape(units)] + shapes,
        compiler_params=params(),
        cost_estimate=light(),
        name="ffn_backward",
    )(place, mine, other, hidden, w, *pins)


def call_grad(x, d, pins):
    tokens, width = x.shape
    units = d.shape[1]
    columns = 512 if tokens <= 1024 else 256

    def kernel(x_ref, d_ref, *refs):
        refs[-1][...] = tn(x_ref[...], d_ref[...]).astype(BF16)

    return pl.pallas_call(
        kernel,
        grid=(width // columns,),
        in_specs=[
            pl.BlockSpec((tokens, columns), lambda t: (0, t)),
            pl.BlockSpec(d.shape, lambda t: (0, 0), pipeline_mode=pl.Buffered(1)),
        ]
        + pinned(pins),
        out_specs=pl.BlockSpec((columns, units), lambda t: (t, 0)),
        out_shape=jax.ShapeDtypeStruct((width, units), BF16),
        compiler_params=params(),
        cost_estimate=light(),
        name="grad",
    )(x, d, *pins)


def call_grads(xs, ds, gated, d_att, segs, pins):
    tokens, width = d_att.shape
    cw = gated.shape[1]
    rows, count = width // segs, len(xs)
    columns = 512 if tokens <= 1024 else 128
    per, cut = rows // columns, cw // segs

    def kernel(*refs):
        x_refs, d_refs, gated_ref, att_ref, out_ref = refs[:count], refs[count : 2 * count], refs[-3 - len(pins)], refs[-2 - len(pins)], refs[-1]
        s, at = pl.program_id(0) // per, pl.program_id(0) % per
        for j in range(count):
            out_ref[s, j, pl.ds(pl.multiple_of(at * columns, columns), columns), :] = tn(
                x_refs[j][...], d_refs[j][...]
            ).astype(BF16)
        result = tn(gated_ref[...], att_ref[...]).astype(BF16)
        each = columns // cw
        for i in range(each):
            to = pl.multiple_of((pl.program_id(0) * each + i) * cut, cut)
            for m in range(segs):
                out_ref[m, count, pl.ds(to, cut), :] = result[m * cut : (m + 1) * cut, i * cw : (i + 1) * cw]

    block = pl.BlockSpec((tokens, columns), lambda t: (0, t))
    fixed = pl.BlockSpec((tokens, cw), lambda t: (0, 0), pipeline_mode=pl.Buffered(1))
    shape = (segs, count + 1, rows, cw)
    return pl.pallas_call(
        kernel,
        grid=(width // columns,),
        in_specs=[block] * count + [fixed] * count + [fixed, block] + pinned(pins),
        out_specs=pl.BlockSpec(shape, lambda t: (0, 0, 0, 0)),
        out_shape=jax.ShapeDtypeStruct(shape, BF16),
        compiler_params=params(),
        cost_estimate=light(),
        name="grads",
    )(*xs, *ds, gated, d_att, *pins)


def call_ffn_norm(x, blocks, rows, pins):
    length, width = x.shape
    count = blocks.shape[0]

    def kernel(x_ref, blocks_ref, rows_ref, *refs):
        sum_ref, unit_ref, scale_ref, normed_ref, low_ref = refs[-5:]
        lanes = 128
        total = jnp.zeros((length, lanes), F32)
        for at in range(0, width, lanes):
            c = slice(at, at + lanes)
            value = x_ref[:, c].astype(F32)
            for i in range(count):
                value = value + blocks_ref[i, :, c].astype(F32)
            sum_ref[:, c] = value
            total = total + value
        mean = jnp.sum(total, 1, keepdims=True) / width
        total = jnp.zeros((length, lanes), F32)
        for at in range(0, width, lanes):
            center = sum_ref[:, at : at + lanes] - mean
            total = total + center * center
        scale = lax.rsqrt(jnp.sum(total, 1, keepdims=True) / width + LAYER_EPSILON)
        scale_ref[...] = jnp.broadcast_to(scale, scale_ref.shape)
        for at in range(0, width, lanes):
            c = slice(at, at + lanes)
            unit = (sum_ref[:, c] - mean) * scale
            unit_ref[:, c] = unit
            normed = unit * rows_ref[0:1, c] + rows_ref[1:2, c]
            normed_ref[:, c] = normed
            low_ref[:, c] = normed.astype(BF16)

    shape = lambda n, dtype: jax.ShapeDtypeStruct((length, n), dtype)
    return pl.pallas_call(
        kernel,
        grid=(1,),
        in_specs=[whole(x), whole(blocks), whole(rows)] + pinned(pins),
        out_specs=[pl.BlockSpec((length, n), lambda t: (0, 0)) for n in (width, width, 128, width, width)],
        out_shape=[shape(width, F32), shape(width, F32), shape(128, F32), shape(width, F32), shape(width, BF16)],
        compiler_params=params(),
        cost_estimate=light(),
        name="ffn_norm",
    )(x, blocks, rows, *pins)


def call_ffn_local(place, recept_in, blocks, cot, residual, gate_mine, gate_other, group, pins):
    length, width = recept_in.shape
    count, half = blocks.shape[0], gate_mine.shape[1]
    cw = width // group
    step = min(2 * CHUNK, half)

    def kernel(place_ref, recept_ref, blocks_ref, cot_ref, residual_ref, mine_ref, other_ref, *refs):
        out_ref, cut_ref, d_ref, gate_ref = refs[-4:]
        recept = recept_ref[...]
        cores = ((mine_ref, place_ref[1]), (other_ref, 1 - place_ref[1])) if half < width else ((mine_ref, 0),)
        for ref, core in cores:
            for at in range(0, half, step):
                c = pl.ds(pl.multiple_of(core * half + at, step), step)
                gate = jax.nn.sigmoid(nn(recept, ref[:, at : at + step]))
                values = sum(blocks_ref[i, :, c].astype(F32) for i in range(count))
                out_ref[:, c] = (residual_ref[:, c] + gate * values).astype(BF16)
                gate_ref[:, c] = (cot_ref[:, c].astype(F32) * values * gate * (1.0 - gate)).astype(BF16)
        for i in range(group):
            cut_ref[i] = gate_ref[:, i * cw : (i + 1) * cw]
        for at in range(0, width, 2 * CHUNK):
            c = slice(at, at + 2 * CHUNK)
            d = jnp.zeros((length, 2 * CHUNK), F32)
            for ref, core in cores:
                d = d + nt(gate_ref[:, pl.ds(pl.multiple_of(core * half, half), half)], ref[c, :])
            d_ref[:, c] = d

    fixed = lambda a: pl.BlockSpec(a.shape, lambda t, place: (0,) * a.ndim)
    shapes = [(length, width), (group, length, cw), (length, width)]
    return pl.pallas_call(
        kernel,
        grid_spec=pltpu.PrefetchScalarGridSpec(
            num_scalar_prefetch=1,
            grid=(1,),
            in_specs=[fixed(a) for a in (recept_in, blocks, cot, residual, gate_mine, gate_other)] + pinned(pins),
            out_specs=[pl.BlockSpec(s, lambda t, place, n=len(s): (0,) * n) for s in shapes],
            scratch_shapes=[pltpu.VMEM((length, width), BF16)],
        ),
        out_shape=[jax.ShapeDtypeStruct(s, dtype) for s, dtype in zip(shapes, (BF16, BF16, F32))],
        compiler_params=params(),
        cost_estimate=light(),
        name="ffn_local",
    )(place, recept_in, blocks, cot, residual, gate_mine, gate_other, *pins)


def call_out(place, gated, own, parts, sender, seqs, pins):
    tokens, cw = gated.shape
    width = own.shape[1]
    length = 256
    specs, shapes = two_halves(tokens, width, length, seqs)

    def kernel(place_ref, gated_ref, own_ref, *refs):
        w_ref, value_ref = refs[-2:]

        @pl.when(pl.program_id(0) == 0)
        def _():
            received = refs[0][...]
            for ref in refs[1 : len(parts)]:
                received = received + ref[...]
            w_ref[...] = jnp.where(place_ref[2] == 1, own_ref[...], received)

        for at in range(0, width, 2 * CHUNK):
            c = slice(at, at + 2 * CHUNK)
            value_ref[:, c] = nn(gated_ref[...], w_ref[:, c]).astype(BF16)
        store_half(place_ref, value_ref, refs[-2 - len(specs) : -2])

    fixed = lambda a: pl.BlockSpec(a.shape, lambda t, place: (0, 0))

    return pl.pallas_call(
        kernel,
        grid_spec=pltpu.PrefetchScalarGridSpec(
            num_scalar_prefetch=1,
            grid=(tokens // length,),
            in_specs=[pl.BlockSpec((length, cw), lambda t, place: (t, 0))] + [fixed(a) for a in (own, *parts)]
            + pinned(pins),
            out_specs=specs + [pl.BlockSpec((cw, width), lambda t, place: (0, 0))],
            scratch_shapes=[pltpu.VMEM((length, width), BF16)],
        ),
        out_shape=shapes + [jax.ShapeDtypeStruct((cw, width), BF16)],
        compiler_params=params(),
        cost_estimate=light(),
        name="out_projection",
    )(jnp.concatenate([place, sender.reshape(1)]), gated, own, *parts, *pins)


def call_add(mine, other, pins):
    rows, width = mine.shape
    length = 128

    def kernel(a_ref, b_ref, *refs):
        refs[-1][...] = (a_ref[...].astype(F32) + b_ref[...].astype(F32)).astype(BF16)

    tile = pl.BlockSpec((length, width), lambda t: (t, 0))
    return pl.pallas_call(
        kernel,
        grid=(rows // length,),
        in_specs=[tile, tile] + pinned(pins),
        out_specs=tile,
        out_shape=jax.ShapeDtypeStruct((rows, width), BF16),
        compiler_params=params(),
        cost_estimate=light(),
        name="add",
    )(mine, other, *pins)


def call_wkv_backward(length, d, r, k, v, w, graw, wkv, dm, w_out, own, ones, sums, start, ends, adj, pins):
    tokens, cw = r.shape
    count = tokens // length
    tile = lambda n: pl.BlockSpec((length, n), lambda t: (count - 1 - t, 0))
    shape = lambda dtype: jax.ShapeDtypeStruct((tokens, cw), dtype)
    wide = dm.shape[1]
    return pl.pallas_call(
        wkv_backward,
        grid=(count,),
        in_specs=[tile(d.shape[1])] + [tile(cw)] * 6 + [tile(wide)]
        + [whole(a) for a in (w_out, own, ones, sums, start)]
        + [
            pl.BlockSpec((1, HEAD, cw), lambda t: (jnp.maximum(count - 2 - t, 0), 0, 0)),
            pl.BlockSpec((1, HEAD, cw), lambda t: (count - 1 - t, 0, 0)),
        ]
        + pinned(pins),
        out_specs=[pl.BlockSpec((32, cw), lambda t: (0, 0)), pl.BlockSpec((wide, cw), lambda t: (0, 0))] + [tile(cw)] * 5,
        out_shape=[jax.ShapeDtypeStruct((32, cw), F32), jax.ShapeDtypeStruct((wide, cw), F32)]
        + [shape(BF16)] * 4 + [shape(F32)],
        scratch_shapes=[pltpu.VMEM((cw, cw), F32)],
        compiler_params=params(),
        cost_estimate=light(),
        name="wkv_backward",
    )(d, r, k, v, w, graw, wkv, dm, w_out, own, ones, sums, start, ends, adj, *pins)


def call_mix_backward(
    rank, length, x, rows, lm, dm, dr, dk, dv, dg, dpre, wn, ww, fn, fw, more, place, parts, decays, seqs, pins
):
    tokens, width = x.shape
    cw = dr.shape[1]
    count = tokens // length
    edge = 16
    tile = lambda n: pl.BlockSpec((length, n), lambda t, place: (count - 1 - t, 0))
    before = pl.BlockSpec((edge, width), lambda t, place: (jnp.maximum((count - 1 - t) * (length // edge) - 1, 0), 0))
    fixed = lambda a: pl.BlockSpec(a.shape, lambda t, place: (0, 0))
    packed = 16 + 10 * rank + decays + more.shape[0]
    specs, shapes = two_halves(tokens, width, length, seqs, backward=True)
    return pl.pallas_call(
        lambda *refs: mix_backward(rank, len(specs), *refs),
        grid_spec=pltpu.PrefetchScalarGridSpec(
            num_scalar_prefetch=1,
            grid=(count,),
            in_specs=[tile(width), before, fixed(rows), tile(lm.shape[1]), tile(dm.shape[1])] + [tile(cw)] * 5
            + [fixed(a) for a in (wn, ww, fn, fw, more)] + pinned(parts) + pinned(pins),
            out_specs=[pl.BlockSpec((packed, width), lambda t, place: (0, 0))] + specs,
            scratch_shapes=[pltpu.VMEM((n, width), F32) for n in (8 * 8, wn.shape[0], wn.shape[0], fn.shape[0])]
            + [pltpu.VMEM((length, width), BF16), pltpu.VMEM((8, width), F32)]
            + [pltpu.VMEM((length, width), F32)] * 4 + part_scratch(parts),
        ),
        out_shape=[jax.ShapeDtypeStruct((packed, width), BF16)] + shapes,
        compiler_params=params(),
        cost_estimate=light(),
        name="mix_backward",
    )(place, x, x, rows, lm, dm, dr, dk, dv, dg, dpre, wn, ww, fn, fw, more, *parts, *pins)


def gather_group(block):
    return lax.all_gather(block, TP, axis=0, tiled=True)


SWAP = [(0, 1), (1, 0)]


def reduce_halves(mine, other, pins):
    total = call_add(mine, lax.ppermute(other, "seq", SWAP), pins)
    return reduce_chan(total), total


def reduce_chan(total):
    chans = lax.axis_size("chan")
    return lax.all_to_all(total.reshape(chans, -1, total.shape[1]), "chan", 0, 0, tiled=True)


def add_up(blocks):
    return jnp.sum(blocks.astype(F32), 0)


def reduce_group(parts, pins=()):
    if len(parts) == 2:
        return reduce_halves(*parts, pins)
    total = lax.psum_scatter(parts[0], "seq", scatter_dimension=0, tiled=True)
    return reduce_chan(total), total


def after(a, before):
    corner = before[(slice(0, 1),) * before.ndim].reshape((1,) * a.ndim)
    return a + (corner.astype(F32) * 0.0).astype(a.dtype)


def after_all(a, others):
    for other in others:
        a = after(a, other)
    return a


def next_row(row, by):
    count = lax.axis_size(TP)
    return lax.ppermute(row, TP, [(i, i + by) for i in range(count) if 0 <= i + by < count])


def shift_down(values, first_row):
    return jnp.concatenate([first_row, values[:-1]], 0)


def unit_rows(values):
    center = values - jnp.mean(values, -1, keepdims=True)
    scale = lax.rsqrt(jnp.mean(center * center, -1, keepdims=True) + LAYER_EPSILON)
    return center * scale, scale


def on_device(
    sequence_elements,
    segment_predecessor_entries,
    opening_recurrences,
    first_layernorm_gain,
    first_layernorm_shift_term,
    lag_blend_coefficients,
    lag_narrowing_factor,
    lag_widening_factors,
    fading_exponent_baseline,
    fading_narrowing_factor,
    fading_widening_factor,
    present_reward,
    acceptor_projection,
    address_projection,
    content_projection,
    valve_projection,
    timemix_result_projection,
    subspace_cluster_gain,
    subspace_cluster_shift_term,
    second_layernorm_gain,
    second_layernorm_shift_term,
    feedforward_lag_blends,
    feedforward_address_projection,
    feedforward_acceptor_projection,
    feedforward_content_projection,
    result_adjoint,
    final_recurrence_adjoint,
):
    segs, seqs, chans = lax.axis_size("seg"), lax.axis_size("seq"), lax.axis_size("chan")
    group = seqs * chans
    p = lax.axis_index(TP)
    x = sequence_elements[0]
    length, width = x.shape
    tokens = group * length
    cw = width // group
    heads = cw // HEAD
    rank = lag_widening_factors.shape[1] // 5
    ranks, decays = 5 * rank, fading_widening_factor.shape[1]

    def columns(a, axis=-1):
        return lax.dynamic_slice_in_dim(a, p * cw, cw, axis % a.ndim)

    me, seg = lax.axis_index("seq"), lax.axis_index("seg")
    block = width // (segs * group)
    rows_seg = width // segs
    flips = [[(s, s ^ m) for s in range(segs)] for m in range(segs)]

    def seg_parts(a):
        return [a] + [lax.ppermute(a, "seg", flips[m]) for m in range(1, segs)]

    def own_part(a, axis):
        size = a.shape[axis] // seqs
        return lax.dynamic_slice_in_dim(a, me * size, size, axis)

    def reduce_segs(piece):
        sent = [piece(seg ^ m) for m in range(1, segs)]
        return sum((lax.ppermute(a, "seg", flips[m + 1]).astype(F32) for m, a in enumerate(sent)), piece(seg).astype(F32)), sent

    def reduce_rows(a):
        return lax.psum_scatter(a, "seg", scatter_dimension=0, tiled=True)

    x_all = gather_group(x)
    four = seg_parts(
        jnp.concatenate(
            [columns(a) for a in (acceptor_projection, address_projection, content_projection, valve_projection)], 1
        )
    )
    share = group // segs
    out_rows = after(lax.dynamic_slice_in_dim(timemix_result_projection, (p % share) * cw, cw, 0), four[-1])
    out_parts = [
        lax.ppermute(out_rows, ALL, [((j // share) * group + j, ((j // share) ^ m) * group + j) for j in range(group)])
        for m in range(1, segs)
    ]
    ffn_part = jnp.concatenate([own_part(a, 1) for a in (feedforward_address_projection, feedforward_content_projection)], 1)
    w_ffn = lax.all_gather(after_all(ffn_part, four[1:]), "seg", axis=0, tiled=True)
    cot = after(result_adjoint[0], x_all)
    adjoints = final_recurrence_adjoint[0, 0]
    if seqs == 2:
        adjoints = adjoints.reshape(HEAD, seqs, chans, cw).transpose(2, 0, 1, 3).reshape(chans, HEAD, seqs * cw)
        high = adjoints.astype(BF16)
        adjoints = jnp.concatenate([high, (adjoints - high.astype(F32)).astype(BF16)], 1).reshape(chans, -1, width)
        sent = jnp.concatenate([jnp.broadcast_to(cot[None], (chans, length, width)), adjoints], 1)
        cot_mine = lax.all_to_all(sent, "chan", 0, 0, tiled=True)
        cot_other = lax.ppermute(cot_mine, "seq", SWAP)

        def state_part(a):
            a = a[:, length:].reshape(chans, 2, HEAD, seqs, cw).astype(F32)
            return lax.dynamic_index_in_dim(a[:, 0] + a[:, 1], me, 2, False)

        low, high = state_part(cot_mine), state_part(cot_other)
        adjoints = jnp.where(me == 0, jnp.concatenate([low, high]), jnp.concatenate([high, low]))
    else:
        cot_mine = cot_other = gather_group(cot).reshape(group, length, width)
        adjoints = lax.all_to_all(adjoints.reshape(HEAD, group, cw).transpose(1, 0, 2), TP, 0, 0, tiled=True)

    rows = jnp.concatenate(
        [
            first_layernorm_gain[None], first_layernorm_shift_term[None], lag_blend_coefficients.T,
            segment_predecessor_entries[0, 0][None], fading_exponent_baseline[None], present_reward[None],
            subspace_cluster_gain[None], subspace_cluster_shift_term[None], jnp.zeros((11, width), F32),
        ]
    )
    own = lax.dynamic_slice(rows, (FIRST + 1, p * cw), (8, cw))
    wn, ww, fn = lag_narrowing_factor.T, lag_widening_factors.T, fading_narrowing_factor.T
    fw = columns(fading_widening_factor.T)
    head_of = np.arange(cw) // HEAD
    ones = jnp.asarray(head_of[:, None] == head_of[None, :], BF16)
    start = columns(opening_recurrences[0])
    place = jnp.stack([seg, me]).astype(jnp.int32)

    gated, xk, xv, xr, xg, r, k, v, w, graw, wkv, lm, dm, ends = call_forward(
        rank, length, x_all, rows, own, wn, ww, fn, fw, ones, start, place, four, ()
    )
    *out, w_out = call_out(
        place, gated, out_rows, out_parts, (seg == p // share).astype(jnp.int32), seqs, [cot_mine]
    )
    out_blocks, _ = reduce_group(out)

    mix_key, mix_recept = feedforward_lag_blends[:, 0], feedforward_lag_blends[:, 1]
    first_row = segment_predecessor_entries[0, 1][None]
    ffn_rows = jnp.concatenate(
        [second_layernorm_gain[None], second_layernorm_shift_term[None], first_row, feedforward_lag_blends.T, jnp.zeros((3, width), F32)]
    )
    residual, ffn_unit, ffn_scale, ffn_normed, normed_low = call_ffn_norm(
        x, out_blocks, ffn_rows, [w_ffn]
    )
    ffn_scale = ffn_scale[:, :1]
    normed_all = gather_group(normed_low)
    gate_part = after(own_part(feedforward_acceptor_projection, 1), normed_all)
    gate_mine = lax.all_gather(gate_part, "seg", axis=0, tiled=True)
    before = lax.dynamic_slice_in_dim(normed_all, jnp.maximum(p * length - 1, 0), 1, 0).astype(F32)
    previous = jnp.where(p == 0, first_row, before)
    ffn_delta = shift_down(ffn_normed, previous) - ffn_normed
    recept_in = (ffn_normed + ffn_delta * mix_recept).astype(BF16)
    cot = result_adjoint[0].astype(F32)
    if seqs == 2:
        gate_other = lax.ppermute(gate_mine, "seq", SWAP)
    else:
        gate_mine = gate_other = lax.all_gather(gate_mine, "seq", axis=1, tiled=True)

    key_in, recept_all, hidden, squared, *values = call_ffn_forward(normed_all, ffn_rows, w_ffn, place, seqs, ())
    value_blocks, sent = reduce_group(values)
    d_mine = call_ffn_gate(recept_all, cot_mine, cot_other, gate_mine, place, [sent])
    d_other = lax.ppermute(d_mine, "seq", SWAP) if seqs == 2 else d_mine
    d_values, d_hidden, *d_key = call_ffn_backward(d_mine, d_other, hidden, w_ffn, place, seqs, [value_blocks])
    key_blocks, sent = reduce_group(d_key)
    grad_ffn_value = reduce_rows(call_grad(d_values, squared, [sent]))

    output, d_gate_cut, d_fr = call_ffn_local(
        place, recept_in, value_blocks, result_adjoint[0], residual, gate_mine, gate_other, group, ()
    )
    d_fk = add_up(key_blocks)
    d_fdelta = d_fk * mix_key + d_fr * mix_recept
    d_normed = d_fk + d_fr - d_fdelta + jnp.concatenate([d_fdelta[1:], next_row(d_fdelta[:1], -1)], 0)
    g = d_normed * second_layernorm_gain
    d_residual = cot + ffn_scale * (
        g - jnp.mean(g, -1, keepdims=True) - ffn_unit * jnp.mean(g * ffn_unit, -1, keepdims=True)
    )
    d_att_own = after(d_residual.astype(BF16), grad_ffn_value)
    d_att = gather_group(d_att_own)
    grad_ffn_key = call_grad(key_in, d_hidden, [d_att_own])
    ffn_sums = jnp.stack(
        [
            jnp.sum(d_normed * ffn_unit, 0), jnp.sum(d_normed, 0),
            jnp.sum(ffn_delta * d_fk, 0), jnp.sum(ffn_delta * d_fr, 0),
        ]
    )

    def join_hidden(a):
        return lax.all_to_all(a, "seq", 0, 1, tiled=True).astype(F32)

    ends_high = ends.astype(BF16)
    ends_low = (ends - ends_high.astype(F32)).astype(BF16)
    moved = after(jnp.concatenate([d_gate_cut, ends_high, ends_low], 1), d_att)
    moved = lax.all_to_all(moved, TP, 0, 0, tiled=True)
    d_gate_own = moved[:, :length].reshape(tokens, cw)
    end_states = moved[:, length : length + HEAD].astype(F32) + moved[:, length + HEAD :].astype(F32)
    own_sums, decay_up, dr, dk, dv, dg, d_pre = call_wkv_backward(
        length, d_att, r, k, v, w, graw, wkv, dm, w_out, own, ones, sum_table(length), start, ends, adjoints,
        [grad_ffn_key],
    )
    grads = call_grads([xr, xk, xv, xg, recept_all], [dr, dk, dv, dg, d_gate_own], gated, d_att, segs, ())
    summed = reduce_rows(grads.reshape(-1, cw)).reshape(6, rows_seg, cw)
    more = jnp.concatenate([jnp.sum(own_sums.reshape(4, 8, cw), 1), decay_up[:decays]], 0)
    more = lax.dynamic_update_slice(jnp.zeros((16 * -(-(8 + decays) // 16), width), F32), more, (4, p * cw))
    more = lax.dynamic_update_slice(more, ffn_sums, (0, 0)).astype(BF16)
    packed, *dx = call_mix_backward(
        rank, length, x_all, rows, lm, dm, dr, dk, dv, dg, d_pre, wn, ww, fn, fw, more, place, four, decays, seqs,
        [grads],
    )
    dx_blocks, _ = reduce_group(dx)
    dx_total = add_up(dx_blocks)
    input_grad = d_residual + dx_total

    five = summed[:5].reshape(5, group, block, cw).transpose(1, 0, 2, 3).reshape(group, -1, cw)
    grad_ffn_value = join_hidden(after(grad_ffn_value, dx_blocks))
    grad_ffn_key = join_hidden(after(reduce_rows(grad_ffn_key), dx_blocks))
    grad_out = summed[5].reshape(group, cw // segs, cw).transpose(1, 0, 2).reshape(cw // segs, width)
    grad_out = lax.ppermute(
        grad_out, ALL, [(i * group + j, segs * j + i) for i in range(segs) for j in range(group)]
    ).astype(F32)
    small, _ = reduce_segs(lambda s: lax.dynamic_slice_in_dim(packed, s * rows_seg, rows_seg, 1))
    count = small.shape[0]
    small = small.astype(BF16).reshape(count, group, block).transpose(1, 0, 2).reshape(group, -1, cw)
    mixed = after(jnp.concatenate([five, small], 1), dx_blocks)
    mixed = lax.all_to_all(mixed, TP, 0, 0, tiled=True)
    five, small = mixed[:, : 5 * block], mixed[:, 5 * block :]
    five = five.reshape(group, 5, block, cw).transpose(1, 2, 0, 3).reshape(5, block, width).astype(F32)
    small = jnp.sum(small.astype(F32).reshape(group, count, block), 0)
    norm_gain, norm_bias, shift_mix = small[0], small[1], small[2:8].T
    at = 16
    shift_down_grad, at = small[at : at + ranks].T, at + ranks
    shift_up_grad, at = small[at : at + ranks].T, at + ranks
    d_down, at = small[at : at + decays].T, at + decays
    ffn_gain, ffn_bias, ffn_shift_mix = small[at], small[at + 1], small[at + 2 : at + 4].T
    decay_base, reward, group_gain, group_bias = (small[at + 4 + i] for i in range(4))
    d_up = small[at + 8 : at + 8 + decays].T
    end_states = end_states.transpose(1, 0, 2).reshape(HEAD, width)
    return (
        output[None],
        end_states[None, None],
        input_grad[None],
        norm_gain,
        norm_bias,
        shift_mix,
        shift_down_grad,
        shift_up_grad,
        decay_base,
        d_down,
        d_up,
        reward,
        five[0],
        five[1],
        five[2],
        five[3],
        grad_out,
        group_gain,
        group_bias,
        ffn_gain,
        ffn_bias,
        ffn_shift_mix,
        grad_ffn_key,
        five[4],
        grad_ffn_value,
    )


def solution(mesh):
    rows, tokens = P("seg", None), P("seg", TP, None)
    matrix = P("seg", "chan")
    vector_out, matrix_out = P(ALL), P(ALL, None)
    ffn_out = P(("seg", "seq"), "chan")
    return jax.shard_map(
        on_device,
        mesh=mesh,
        in_specs=(tokens, P("seg", None, None), P("seg", None, None)) + (P(),) * 9 + (rows,) * 5 + (P(),) * 5
        + (matrix, rows, matrix, tokens, P("seg", TP, None, None)),
        out_specs=(tokens, P("seg", TP, None, None), tokens) + (vector_out,) * 2 + (matrix_out,) * 3 + (vector_out,)
        + (matrix_out,) * 2 + (vector_out,) + (matrix_out,) * 5 + (vector_out,) * 4
        + (matrix_out, ffn_out, matrix_out, ffn_out),
        check_vma=False,
    )
```

time: 976 us -> 782 us (0.80)
  waiting for transfers between devices: 524 us -> 347 us
  Pallas kernels: 115 us -> 236 us
  matrix products: 88.6 us -> 0 us
  local copies, waits for them, and re-layouts: 110 us -> 61.1 us
    all_to_all x5 -> x7, waiting for transfers between devices: 32 us -> 157 us  [the longest x4 118 us: reduce_chan(): lax.all_to_all(total.reshape(chans, -1, total.shape[1]), 'chan', 0, 0, ti...]
    pallas_call x2 -> x15, Pallas kernels: 78.3 us -> 201 us  [the longest x1 55.5 us: call_mix_backward(): pl.pallas_call(lambda *refs: mix_backward(rank, len(specs), *refs), grid_...]
    all_gather x5 -> x2, waiting for transfers between devices: 135 us -> 16.2 us  [the longest x1 16.2 us: on_device(): gate_mine = lax.all_gather(gate_part, 'seg', axis=0, tiled=True)]
    dot_general x16 -> x0, matrix products: 88.6 us -> none  [dot(): lax.dot_general(a.astype(BF16), b.astype(BF16), (dims, ((), ())), preferr...]
    ppermute x21 -> x16, waiting for transfers between devices: 165 us -> 82.2 us  [the longest x3 43 us: seg_parts(): return [a] + [lax.ppermute(a, 'seg', flips[m]) for m in range(1, segs)]]
    all_gather x4 -> x3, waiting for transfers between devices: 135 us -> 82.5 us  [gather_group(): return lax.all_gather(block, TP, axis=0, tiled=True)]
    ppermute x2 -> x1, waiting for transfers between devices: 33.4 us -> 0.55 us  [next_row(): lax.ppermute(row, TP, [(i, i + by) for i in range(count) if 0 <= i + by <...]
    convert_element_type x10 -> x7, other arithmetic: 25.7 us -> 6.82 us  [the longest x2 3.64 us: state_part(): a = a[:, length:].reshape(chans, 2, HEAD, seqs, cw).astype(F32)]
  transfers between devices with their start and end apart: 43 -> 34, of which waited for: 22 -> 20; matrix products, arithmetic and copies ran while one was open for 19% -> 8% of each run, Pallas kernels for 12% -> 26%
where the time goes in v2:
time: 782 us; the launch traced here: 767 us
  waiting for transfers between devices  347 us (44%)
  Pallas kernels  236 us (30%)
  local copies, waits for them, and re-layouts  61.1 us (8%)
  starting transfers between devices  60.4 us (8%)
  other arithmetic  37.3 us (5%)
  between operations  20.7 us (3%)
    all_to_all x4, waiting for transfers between devices, reduce_chan(): lax.all_to_all(total.reshape(chans, -1, total.shape[1]), 'chan', 0, 0, ti...  118 us
    all_gather x3, waiting for transfers between devices, gather_group(): return lax.all_gather(block, TP, axis=0, tiled=True)  82.5 us
    pallas_call x1, Pallas kernels, call_mix_backward(): pl.pallas_call(lambda *refs: mix_backward(rank, len(specs), *refs), grid_...  55.5 us
    ppermute x3, waiting for transfers between devices, seg_parts(): return [a] + [lax.ppermute(a, 'seg', flips[m]) for m in range(1, segs)]  43 us
    pallas_call x1, Pallas kernels, call_forward(): pl.pallas_call(lambda *refs: mix_forward(rank, *refs), grid=(count,), in_...  35.2 us
    all_to_all x1, waiting for transfers between devices, on_device(): mixed = lax.all_to_all(mixed, TP, 0, 0, tiled=True)  28.6 us
    pallas_call x1, Pallas kernels, call_wkv_backward(): pl.pallas_call(wkv_backward, grid=(count,), in_specs=[tile(d.shape[1])] +...  25.6 us
    ppermute x3, waiting for transfers between devices, reduce_segs(): lax.ppermute(a, 'seg', flips[m + 1]).astype(F32)  22.2 us
  transfers between devices with their start and end apart: 34, of which 20 were waited for; matrix products, arithmetic and copies ran while one was open for 8% of the time, Pallas kernels for 26%

profile of v2, /device:TPU:1, one launch (start us, length us, event | category | flops | bytes accessed | tf_op | source)
XLA Modules:
  0.0 766.9 jit_solution(8188677502513515548)
XLA Ops:
  15.3 21.1 %collective-permute-done.2.refs_13_.refs_19_ = bf16[512,1024]{1,0:T(8,128)(2,1)S(1)} collective-permute-done((bf16[512,1024]{1,0:T(8,128)(2,1)S(1)}, bf16[512,1024]{1,0:T(8,128)(2,1)S(1)}, u32[]{:S(2)}, u32[]{:S(2)}) %collective-permute-start.2) | collective-permute-done | bytes 1048608 | tf_op jit(solution)/shard_map/ppermute | solution.py:1028
  37.6 22.0 %collective-permute-done.1.refs_12_.refs_18_ = bf16[512,1024]{1,0:T(8,128)(2,1)} collective-permute-done((bf16[512,1024]{1,0:T(8,128)(2,1)S(1)}, bf16[512,1024]{1,0:T(8,128)(2,1)}, u32[]{:S(2)}, u32[]{:S(2)}) %collective-permute-start.1) | collective-permute-done | bytes 1048608 | tf_op jit(solution)/shard_map/ppermute | solution.py:1028
  88.7 35.2 %mix_forward.1 = (bf16[1024,256]{1,0:T(8,128)(2,1)}, bf16[1024,2048]{1,0:T(8,128)(2,1)}, bf16[1024,2048]{1,0:T(8,128)(2,1)}, bf16[1024,2048]{1,0:T(8,128)(2,1)},...) custom-call(bf16[1024,2048]{1,0:T(8,128)(2,1)} %bitcast.140, ...), custom_call_target="tpu_custom_call" | custom-call | tf_op jit(solution)/shard_map/mix_forward/pallas_call | solution.py:444
  123.9 10.4 %all-to-all-done.refs_3_.mine_ref = bf16[4,160,2048]{2,1,0:T(8,128)(2,1)S(1)} async-done(((bf16[4,160,2048]{2,1,0:T(8,128)(2,1)}), bf16[4,160,2048]{2,1,0:T(8,128)(2,1)S(1)}, u32[]{:S(2)}, u32[]{:S(2)}) %all-to-all-start) | async-done | bytes 2621472 | tf_op jit(solution)/shard_map/all_to_all | solution.py:1062
  135.7 7.7 %out_projection.1 = (bf16[512,2048]{1,0:T(8,128)(2,1)}, bf16[512,2048]{1,0:T(8,128)(2,1)}, bf16[256,2048]{1,0:T(8,128)(2,1)}) custom-call(s32[3]{0:T(128)} %pad_add_fusion.1.place_ref, bf16[1024,256]{1,0:T(8,128)(2,1)} %get-tuple-element.70.gated_ref.refs_10_, bf16[256,2048]{1,0:T(8,128)(2,1)} %dynamic-slice_add_fusion.1.own_ref, ...), custom_call_target="tpu_custom_call" | custom-call | tf_op jit(solution)/shard_map/out_projection/pallas_call | solution.py:831
  159.6 47.1 %all-to-all-done.1.blocks_ref = bf16[4,128,2048]{2,1,0:T(8,128)(2,1)S(1)} async-done(((bf16[4,128,2048]{2,1,0:T(8,128)(2,1)}), bf16[4,128,2048]{2,1,0:T(8,128)(2,1)S(1)}, u32[]{:S(2)}, u32[]{:S(2)}) %all-to-all-start.1) | async-done | bytes 2097184 | tf_op jit(solution)/shard_map/all_to_all | solution.py:939
  212.8 45.4 %all-gather.9.cloned.1.call-done.refs_1_.refs_2_ = bf16[1024,2048]{1,0:T(8,128)(2,1)} async-done(((bf16[128,2048]{1,0:T(8,128)(2,1)}), bf16[1024,2048]{1,0:T(8,128)(2,1)}) %all-gather.9.cloned.1.call-update) | async-done | bytes 4194320 | tf_op jit(solution)/shard_map/all_gather | solution.py:926
  262.5 19.6 %ffn_forward.1 = (bf16[1024,2048]{1,0:T(8,128)(2,1)}, bf16[1024,2048]{1,0:T(8,128)(2,1)}, f32[1024,896]{1,0:T(8,128)}, bf16[1024,896]{1,0:T(8,128)(2,1)}, bf16[5...) custom-call(s32[2]{0:T(128)} %pad_add_fusion.refs_9_.refs_0_.place_ref, ...), custom_call_target="tpu_custom_call" | custom-call | tf_op jit(solution)/shard_map/ffn_forward/pallas_call | solution.py:535
  297.5 16.2 %all-gather.11.cloned.1.call-done.mine_ref.gate_ref = bf16[2048,1024]{1,0:T(8,128)(2,1)} async-done(((bf16[512,1024]{1,0:T(8,128)(2,1)}), bf16[2048,1024]{1,0:T(8,128)(2,1)}) %all-gather.11.cloned.1.call-update) | async-done | bytes 4194320 | tf_op jit(solution)/shard_map/all_gather | solution.py:1109
  313.7 9.8 %ffn_gate.1.refs_1_ = bf16[1024,1024]{1,0:T(8,128)(2,1)} custom-call(s32[2]{0:T(128)} %pad_add_fusion.refs_9_.refs_0_.place_ref, bf16[1024,2048]{1,0:T(8,128)(2,1)} %get-tuple-element.82.recept_ref.refs_4_, bf16[4,160,2048]{2,1,0:T(8,128)(2,1)} %copy-done.2, bf16[4,160,2048]{2,1,0:T(8,128)(2,1)} %collective-permute-done.9.other_ref, ...), custom_call_target="tpu_custom_call" | custom-call | tf_op jit(solution)/shard_map/ffn_gate/pallas_call | solution.py:586
  324.2 21.2 %all-to-all-done.2.blocks_ref.refs_5_ = bf16[4,128,2048]{2,1,0:T(8,128)(2,1)} async-done(((bf16[4,128,2048]{2,1,0:T(8,128)(2,1)}), bf16[4,128,2048]{2,1,0:T(8,128)(2,1)}, u32[]{:S(2)}, u32[]{:S(2)}) %all-to-all-start.2) | async-done | bytes 2097184 | tf_op jit(solution)/shard_map/all_to_all | solution.py:939
  346.7 17.3 %ffn_backward.1 = (bf16[1024,2048]{1,0:T(8,128)(2,1)}, bf16[1024,896]{1,0:T(8,128)(2,1)}, bf16[512,2048]{1,0:T(8,128)(2,1)}, bf16[512,2048]{1,0:T(8,128)(2,1)}) custom-call(s32[2]{0:T(128)} %pad_add_fusion.refs_9_.refs_0_.place_ref, bf16[1024,1024]{1,0:T(8,128)(2,1)} %ffn_gate.1.refs_1_, bf16[1024,1024]{1,0:T(8,128)(2,1)} %copy-done.15, ...), custom_call_target="tpu_custom_call" | custom-call | tf_op jit(solution)/shard_map/ffn_backward/pallas_call | solution.py:643
  375.0 8.3 %grad.2 = bf16[2048,896]{1,0:T(8,128)(2,1)} custom-call(bf16[1024,2048]{1,0:T(8,128)(2,1)} %get-tuple-element.88.x_ref, bf16[1024,896]{1,0:T(8,128)(2,1)} %get-tuple-element.89.d_ref, bf16[512,2048]{1,0:T(8,128)(2,1)} %add.312.refs_0_), custom_call_target="tpu_custom_call" | custom-call | tf_op jit(solution)/shard_map/grad/pallas_call | solution.py:669
  390.9 11.0 %ffn_local.1 = (bf16[128,2048]{1,0:T(8,128)(2,1)}, bf16[8,128,256]{2,1,0:T(8,128)(2,1)}, f32[128,2048]{1,0:T(8,128)}) custom-call(s32[2]{0:T(128)} %pad_add_fusion.refs_9_.refs_0_.place_ref, bf16[128,2048]{1,0:T(8,128)(2,1)} %add_convert_fusion.recept_ref, bf16[4,128,2048]{2,1,0:T(8,128)(2,1)} %all-to-all-done.2.blocks_ref.refs_5_, ...), custom_call_target="tpu_custom_call" | custom-call | tf_op jit(solution)/shard_map/ffn_local/pallas_call | solution.py:792
  401.9 34.7 %all-to-all-done.3 = bf16[4,128,2048]{2,1,0:T(8,128)(2,1)} async-done(((bf16[4,128,2048]{2,1,0:T(8,128)(2,1)}), bf16[4,128,2048]{2,1,0:T(8,128)(2,1)}, u32[]{:S(2)}, u32[]{:S(2)}) %all-to-all-start.3) | async-done | bytes 2097184 | tf_op jit(solution)/shard_map/all_to_all | solution.py:939
  450.2 8.3 %grad.3.refs_0_ = bf16[2048,896]{1,0:T(8,128)(2,1)} custom-call(bf16[1024,2048]{1,0:T(8,128)(2,1)} %get-tuple-element.99.x_ref, bf16[1024,896]{1,0:T(8,128)(2,1)} %get-tuple-element.100.d_ref, bf16[128,2048]{1,0:T(8,128)(2,1)} %get-tuple-element.171.refs_0_), custom_call_target="tpu_custom_call" | custom-call | tf_op jit(solution)/shard_map/grad/pallas_call | solution.py:669
  461.8 37.1 %all-gather.13.cloned.1.call-done.d_ref.refs_11_ = bf16[1024,2048]{1,0:T(8,128)(2,1)} async-done(((bf16[128,2048]{1,0:T(8,128)(2,1)}), bf16[1024,2048]{1,0:T(8,128)(2,1)}) %all-gather.13.cloned.1.call-update) | async-done | bytes 4194320 | tf_op jit(solution)/shard_map/all_gather | solution.py:926
  512.8 25.6 %wkv_backward.1 = (f32[32,256]{1,0:T(8,128)}, f32[64,256]{1,0:T(8,128)}, bf16[1024,256]{1,0:T(8,128)(2,1)}, bf16[1024,256]{1,0:T(8,128)(2,1)}, bf16[1024,256]{1,...) custom-call(bf16[1024,2048]{1,0:T(8,128)(2,1)} %all-gather.13.cloned.1.call-done.d_ref.refs_11_, ...), custom_call_target="tpu_custom_call" | custom-call | tf_op jit(solution)/shard_map/wkv_backward/pallas_call | solution.py:874
  539.4 15.8 %grads.1.refs_20_ = bf16[4,6,512,256]{3,2,1,0:T(8,128)(2,1)} custom-call(bf16[1024,2048]{1,0:T(8,128)(2,1)} %get-tuple-element.108.refs_0_, bf16[1024,2048]{1,0:T(8,128)(2,1)} %get-tuple-element.109.refs_1_, bf16[1024,2048]{1,0:T(8,128)(2,1)} %get-tuple-element.110.refs_2_, bf16[1024,2048]{1,0:T(8,128)(2,1)} %get-tuple-element.111.refs_3_, ...), custom_call_target="tpu_custom_call" | custom-call | tf_op jit(solution)/shard_map/grads/pallas_call | solution.py:709
  557.9 55.5 %mix_backward.1 = (bf16[480,2048]{1,0:T(8,128)(2,1)}, bf16[512,2048]{1,0:T(8,128)(2,1)}, bf16[512,2048]{1,0:T(8,128)(2,1)}) custom-call(s32[2]{0:T(128)} %pad_add_fusion.refs_9_.refs_0_.place_ref, bf16[1024,2048]{1,0:T(8,128)(2,1)} %bitcast.141, bf16[1024,2048]{1,0:T(8,128)(2,1)} %bitcast.142, f32[24,2048]{1,0:T(8,128)} %copy-done.21, ...), custom_call_target="tpu_custom_call" | custom-call | tf_op jit(solution)/shard_map/mix_backward/pallas_call | solution.py:906
  633.4 10.6 %collective-permute-done.16 = bf16[480,512]{1,0:T(8,128)(2,1)S(1)} collective-permute-done((bf16[480,512]{1,0:T(8,128)(2,1)}, bf16[480,512]{1,0:T(8,128)(2,1)S(1)}, u32[]{:S(2)}, u32[]{:S(2)}) %collective-permute-start.16) | collective-permute-done | bytes 491552 | tf_op jit(solution)/shard_map/ppermute | solution.py:1036
  644.0 11.6 %collective-permute-done.15 = bf16[480,512]{1,0:T(8,128)(2,1)} collective-permute-done((bf16[480,512]{1,0:T(8,128)(2,1)}, bf16[480,512]{1,0:T(8,128)(2,1)}, u32[]{:S(2)}, u32[]{:S(2)}) %collective-permute-start.15) | collective-permute-done | bytes 491552 | tf_op jit(solution)/shard_map/ppermute | solution.py:1036
  660.8 15.3 %all-to-all-done.5 = bf16[4,128,2048]{2,1,0:T(8,128)(2,1)S(1)} async-done(((bf16[4,128,2048]{2,1,0:T(8,128)(2,1)}), bf16[4,128,2048]{2,1,0:T(8,128)(2,1)S(1)}, u32[]{:S(2)}, u32[]{:S(2)}) %all-to-all-start.5) | async-done | bytes 2097184 | tf_op jit(solution)/shard_map/all_to_all | solution.py:939
  718.7 28.6 %all-to-all-done.6 = bf16[8,440,256]{2,1,0:T(8,128)(2,1)} async-done(((bf16[8,440,256]{2,1,0:T(8,128)(2,1)}), bf16[8,440,256]{2,1,0:T(8,128)(2,1)}, u32[]{:S(2)}, u32[]{:S(2)}) %all-to-all-start.6) | async-done | bytes 1802272 | tf_op jit(solution)/shard_map/all_to_all | solution.py:1185
  (251 shorter events, 210.9 us)
Async XLA Ops:
  7.2 59.4 %all-gather.15.cloned.1.call-start = ((), (), s32[]{:S(2)}) async-start(), calls=%async_computation.19 | async-start | bytes 4718592 | tf_op jit(solution)/shard_map/all_gather | solution.py:926
  8.0 151.7 %all-gather.7.cloned.1.call-start = ((), (), s32[]{:S(2)}) async-start(), calls=%async_computation.12 | async-start | bytes 9175040 | tf_op jit(solution)/shard_map/all_gather | solution.py:1054
  10.3 26.1 %collective-permute-start.2 = (bf16[512,1024]{1,0:T(8,128)(2,1)S(1)}, bf16[512,1024]{1,0:T(8,128)(2,1)S(1)}, u32[]{:S(2)}, u32[]{:S(2)}) collective-permute-start(bf16[512,1024]{1,0:T(8,128)(2,1)S(1)} %pad_maximum_fusion.1.refs_10_.refs_16_), channel_id=1, source_target_pairs={{0,24},{8,16},{16,8},{24,0},{1,25},{9,17},{17,9},{25,1},{2,26},{10... | collective-permute-start | bytes 3145736 | tf_op jit(solution)/shard_map/ppermute | solution.py:1028
  13.4 46.2 %collective-permute-start.1 = (bf16[512,1024]{1,0:T(8,128)(2,1)S(1)}, bf16[512,1024]{1,0:T(8,128)(2,1)}, u32[]{:S(2)}, u32[]{:S(2)}) collective-permute-start(bf16[512,1024]{1,0:T(8,128)(2,1)S(1)} %pad_maximum_fusion.1.refs_10_.refs_16_), channel_id=1, source_target_pairs={{0,16},{8,24},{16,0},{24,8},{1,17},{9,25},{17,1},{25,9},{2,18},{10... | collective-permute-start | bytes 3145736 | tf_op jit(solution)/shard_map/ppermute | solution.py:1028
  13.6 47.8 %collective-permute-start = (bf16[512,1024]{1,0:T(8,128)(2,1)S(1)}, bf16[512,1024]{1,0:T(8,128)(2,1)}, u32[]{:S(2)}, u32[]{:S(2)}) collective-permute-start(bf16[512,1024]{1,0:T(8,128)(2,1)S(1)} %pad_maximum_fusion.1.refs_10_.refs_16_), channel_id=1, source_target_pairs={{0,8},{8,0},{16,24},{24,16},{1,9},{9,1},{17,25},{25,17},{2,10},{10... | collective-permute-start | bytes 3145736 | tf_op jit(solution)/shard_map/ppermute | solution.py:1028
  70.5 63.7 %all-to-all-start = ((bf16[4,160,2048]{2,1,0:T(8,128)(2,1)}), bf16[4,160,2048]{2,1,0:T(8,128)(2,1)S(1)}, u32[]{:S(2)}, u32[]{:S(2)}) async-start(bf16[4,160,2048]{2,1,0:T(8,128)(2,1)} %pad_maximum_fusion), calls=%async_computation | async-start | bytes 5242880 | tf_op jit(solution)/shard_map/all_to_all | solution.py:1062
  77.8 46.1 %collective-permute-start.3 = (bf16[256,2048]{1,0:T(8,128)(2,1)}, bf16[256,2048]{1,0:T(8,128)(2,1)}, u32[]{:S(2)}, u32[]{:S(2)}) collective-permute-start(bf16[256,2048]{1,0:T(8,128)(2,1)} %dynamic-slice_add_fusion.1.own_ref), channel_id=1, source_target_pairs={{0,8},{1,9},{10,2},{11,3},{20,28},{21,29},{30,22},{31,23}} | collective-permute-start | bytes 3145736 | tf_op jit(solution)/shard_map/ppermute | solution.py:1050
  79.5 44.4 %collective-permute-start.4 = (bf16[256,2048]{1,0:T(8,128)(2,1)}, bf16[256,2048]{1,0:T(8,128)(2,1)}, u32[]{:S(2)}, u32[]{:S(2)}) collective-permute-start(bf16[256,2048]{1,0:T(8,128)(2,1)} %dynamic-slice_add_fusion.1.own_ref), channel_id=1, source_target_pairs={{0,16},{1,17},{10,26},{11,27},{20,4},{21,5},{30,14},{31,15}} | collective-permute-start | bytes 3145736 | tf_op jit(solution)/shard_map/ppermute | solution.py:1050
  80.8 43.1 %collective-permute-start.5 = (bf16[256,2048]{1,0:T(8,128)(2,1)}, bf16[256,2048]{1,0:T(8,128)(2,1)}, u32[]{:S(2)}, u32[]{:S(2)}) collective-permute-start(bf16[256,2048]{1,0:T(8,128)(2,1)} %dynamic-slice_add_fusion.1.own_ref), channel_id=1, source_target_pairs={{0,24},{1,25},{10,18},{11,19},{20,12},{21,13},{30,6},{31,7}} | collective-permute-start | bytes 3145736 | tf_op jit(solution)/shard_map/ppermute | solution.py:1050
  154.6 52.2 %all-to-all-start.1 = ((bf16[4,128,2048]{2,1,0:T(8,128)(2,1)}), bf16[4,128,2048]{2,1,0:T(8,128)(2,1)S(1)}, u32[]{:S(2)}, u32[]{:S(2)}) async-start(bf16[4,128,2048]{2,1,0:T(8,128)(2,1)} %bitcast.147), calls=%async_computation.1 | async-start | bytes 4194304 | tf_op jit(solution)/shard_map/all_to_all | solution.py:939
  158.9 99.3 %all-gather.9.cloned.1.call-start = ((), (), s32[]{:S(2)}) async-start(), calls=%async_computation.13 | async-start | bytes 4718592 | tf_op jit(solution)/shard_map/all_gather | solution.py:926
  212.3 101.4 %all-gather.11.cloned.1.call-start = ((), (), s32[]{:S(2)}) async-start(), calls=%async_computation.14 | async-start | bytes 5242880 | tf_op jit(solution)/shard_map/all_gather | solution.py:1109
  293.0 52.4 %all-to-all-start.2 = ((bf16[4,128,2048]{2,1,0:T(8,128)(2,1)}), bf16[4,128,2048]{2,1,0:T(8,128)(2,1)}, u32[]{:S(2)}, u32[]{:S(2)}) async-start(bf16[4,128,2048]{2,1,0:T(8,128)(2,1)} %bitcast.143), calls=%async_computation.2 | async-start | bytes 4194304 | tf_op jit(solution)/shard_map/all_to_all | solution.py:939
  297.4 148.1 %reduce-scatter.4.cloned.1.call-start = ((), (), s32[]{:S(2)}) async-start(), calls=%async_computation.15 | async-start | bytes 4587520 | tf_op jit(solution)/shard_map/reduce_scatter | solution.py:1039
  323.5 21.9 %collective-permute-start.10 = (bf16[1024,1024]{1,0:T(8,128)(2,1)}, bf16[1024,1024]{1,0:T(8,128)(2,1)S(1)}, u32[]{:S(2)}, u32[]{:S(2)}) collective-permute-start(bf16[1024,1024]{1,0:T(8,128)(2,1)} %ffn_gate.1.refs_1_), channel_id=1, source_target_pairs={{0,4},{4,0},{1,5},{5,1},{2,6},{6,2},{3,7},{7,3},{8,12},{12,8},{9,1... | collective-permute-start | bytes 6291464 | tf_op jit(solution)/shard_map/ppermute | solution.py:1123
  383.8 52.8 %all-to-all-start.3 = ((bf16[4,128,2048]{2,1,0:T(8,128)(2,1)}), bf16[4,128,2048]{2,1,0:T(8,128)(2,1)}, u32[]{:S(2)}, u32[]{:S(2)}) async-start(bf16[4,128,2048]{2,1,0:T(8,128)(2,1)} %bitcast.34), calls=%async_computation.3 | async-start | bytes 4194304 | tf_op jit(solution)/shard_map/all_to_all | solution.py:939
  388.3 110.6 %all-gather.13.cloned.1.call-start = ((), (), s32[]{:S(2)}) async-start(), calls=%async_computation.16 | async-start | bytes 4718592 | tf_op jit(solution)/shard_map/all_gather | solution.py:926
  450.1 227.1 %reduce-scatter.8.cloned.1.call-start = ((), (), s32[]{:S(2)}) async-start(), calls=%async_computation.18 | async-start | bytes 4587520 | tf_op jit(solution)/shard_map/reduce_scatter | solution.py:1039
  501.9 36.6 %all-to-all-start.4 = ((bf16[8,256,256]{2,1,0:T(8,128)(2,1)}), bf16[8,256,256]{2,1,0:T(8,128)(2,1)S(1)}, u32[]{:S(2)}, u32[]{:S(2)}) async-start(bf16[8,256,256]{2,1,0:T(8,128)(2,1)} %maximum_add_fusion.2), calls=%async_computation.5 | async-start | bytes 2097152 | tf_op jit(solution)/shard_map/all_to_all | solution.py:1154
  505.7 180.8 %reduce-scatter.6.cloned.1.call-start = ((), (), s32[]{:S(2)}) async-start(), calls=%async_computation.17 | async-start | bytes 7864320 | tf_op jit(solution)/shard_map/reduce_scatter | solution.py:1039
  623.6 52.5 %all-to-all-start.5 = ((bf16[4,128,2048]{2,1,0:T(8,128)(2,1)}), bf16[4,128,2048]{2,1,0:T(8,128)(2,1)S(1)}, u32[]{:S(2)}, u32[]{:S(2)}) async-start(bf16[4,128,2048]{2,1,0:T(8,128)(2,1)} %bitcast.146), calls=%async_computation.6 | async-start | bytes 4194304 | tf_op jit(solution)/shard_map/all_to_all | solution.py:939
  632.8 22.8 %collective-permute-start.15 = (bf16[480,512]{1,0:T(8,128)(2,1)}, bf16[480,512]{1,0:T(8,128)(2,1)}, u32[]{:S(2)}, u32[]{:S(2)}) collective-permute-start(bf16[480,512]{1,0:T(8,128)(2,1)} %get-tuple-element.186), channel_id=1, source_target_pairs={{0,16},{8,24},{16,0},{24,8},{1,17},{9,25},{17,1},{25,9},{2,18},{10... | collective-permute-start | bytes 1474568 | tf_op jit(solution)/shard_map/ppermute | solution.py:1036
  633.0 22.6 %collective-permute-start.14 = (bf16[480,512]{1,0:T(8,128)(2,1)S(1)}, bf16[480,512]{1,0:T(8,128)(2,1)}, u32[]{:S(2)}, u32[]{:S(2)}) collective-permute-start(bf16[480,512]{1,0:T(8,128)(2,1)S(1)} %get-tuple-element.184), channel_id=1, source_target_pairs={{0,8},{8,0},{16,24},{24,16},{1,9},{9,1},{17,25},{25,17},{2,10},{10... | collective-permute-start | bytes 1474568 | tf_op jit(solution)/shard_map/ppermute | solution.py:1036
  694.4 52.8 %all-to-all-start.6 = ((bf16[8,440,256]{2,1,0:T(8,128)(2,1)}), bf16[8,440,256]{2,1,0:T(8,128)(2,1)}, u32[]{:S(2)}, u32[]{:S(2)}) async-start(bf16[8,440,256]{2,1,0:T(8,128)(2,1)} %maximum_add_fusion.1), calls=%async_computation.8 | async-start | bytes 3604480 | tf_op jit(solution)/shard_map/all_to_all | solution.py:1185
  (47 other events, 457.1 us)
Sparse Core Ops, SparseCore 0:
  9.7 49.6 all-gather.14
  65.2 91.6 all-gather.6
  212.4 45.7 all-gather.8
  262.6 51.0 all-gather.10
  383.4 46.8 reduce-scatter.3
  450.2 48.6 all-gather.12
  501.9 46.6 reduce-scatter.7
  555.4 71.0 reduce-scatter.5

commit v3 on v2

--- a/solution.py
+++ b/solution.py
@@ -13,7 +13,8 @@
 GROUP_EPSILON = 0.00064
 F32 = jnp.float32
 BF16 = jnp.bfloat16
-CHUNK = 256
+CHUNK = 512
+TOKENS = 128
 VMEM = 56 * 2**20
 
 
@@ -182,7 +183,18 @@
     graw = nn(xg_ref[...], four_ref[:, 3 * own :])
     r_ref[...], k_ref[...], v_ref[...], graw_ref[...] = r, k, v, graw
 
-    rf, kf, vf = r.astype(F32), k.astype(F32), v.astype(F32)
+    ones = ones_ref[...]
+    for at in range(0, length, TOKENS):
+        one_chunk(
+            slice(at, at + TOKENS), r, k, v, w, graw, heads, ones, own_ref, wkv_ref, gated_ref, ends_ref.at[at // TOKENS],
+            state_ref,
+        )
+
+
+def one_chunk(c, r, k, v, w, graw, heads, ones, own_ref, wkv_ref, gated_ref, end_ref, state_ref):
+    v, w, graw = v[c, :], w[c, :], graw[c, :]
+    rf, kf, vf = r[c, :].astype(F32), k[c, :].astype(F32), v.astype(F32)
+    length = w.shape[0]
     levels, before, after, total = pyramid(w)
     row, col = iota((length, length), 0), iota((length, length), 1)
     apart = jnp.where(row > col, row ^ col, 0)
@@ -193,24 +205,37 @@
         here = (apart >= half) & (apart < 2 * half)
         for head, one in enumerate(split_heads(scaled, heads)):
             scores[head] = jnp.where(here, nt(one, flat), scores[head])
-    ones = ones_ref[...]
     wkv = nn(jnp.concatenate([s.astype(BF16) for s in scores], 1), jnp.concatenate(split_heads(vf, heads), 0))
     state = state_ref[...]
     wkv = wkv + nt(rf * jnp.exp(before), state) + head_sum(rf * own_ref[1:2, :] * kf, ones) * vf
-    wkv_ref[...] = wkv
+    wkv_ref[c, :] = wkv
     state = state * jnp.exp(total[0:1, :]) + tn(v, kf * jnp.exp(after)) * ones.astype(F32)
     state_ref[...] = state
-    ends_ref[0] = compact(state)
+    end_ref[...] = compact(state)
 
     center = wkv - head_sum(wkv, ones) / HEAD
     variance = head_sum(center * center, ones) / HEAD
     grouped = center * lax.rsqrt(variance + GROUP_EPSILON) * own_ref[2:3, :] + own_ref[3:4, :]
-    gated_ref[...] = (grouped * graw * jax.nn.sigmoid(graw)).astype(BF16)
+    gated_ref[c, :] = (grouped * graw * jax.nn.sigmoid(graw)).astype(BF16)
+
+
+def state_cotangent(place_ref, mine_ref, other_ref, own):
+    if mine_ref.dtype == F32:
+        return mine_ref[0]
+    tile = pl.num_programs(0) - 1 - pl.program_id(0)
+    is_mine = tile // (pl.num_programs(0) // 2) == place_ref[1]
+    wide = 2 * own
+    parts = []
+    for at in range(0, mine_ref.shape[2], wide):
+        q = pl.ds(pl.multiple_of(place_ref[1] * own + at, own), own)
+        parts.append(jnp.where(is_mine, mine_ref[0, :, q].astype(F32), other_ref[0, :, q].astype(F32)))
+    both = jnp.concatenate(parts, 0)
+    return both[:HEAD] + both[HEAD:]
 
 
 def wkv_backward(
-    d_ref, r_ref, k_ref, v_ref, w_ref, graw_ref, wkv_ref, dm_ref, w_out_ref, own_ref, ones_ref, sums_ref, start_ref,
-    ends_ref, adj_ref, *refs,
+    place_ref, d_ref, r_ref, k_ref, v_ref, w_ref, graw_ref, wkv_ref, dm_ref, w_out_ref, own_ref, ones_ref, sums_ref,
+    start_ref, ends_ref, adj_ref, *refs,
 ):
     own_sums_ref, decay_up_ref, dr_ref, dk_ref, dv_ref, dg_ref, dpre_ref, state_ref = refs[-8:]
     step = pl.program_id(0)
@@ -238,7 +263,7 @@
     r, k, v, w = rb.astype(F32), kb.astype(F32), vb.astype(F32), w_ref[...]
     levels, before, after, total = pyramid(w)
     same = ones.astype(F32)
-    d_state = state_ref[...] + spread(adj_ref[0], same)
+    d_state = state_ref[...] + spread(state_cotangent(place_ref, adj_ref, refs[0], own), same)
     state = spread(jnp.where(step == pl.num_programs(0) - 1, start_ref[...], ends_ref[0]), same)
     d_flat, flat = d_state.astype(BF16), state.astype(BF16)
     from_start, to_end, decay = jnp.exp(before), jnp.exp(after), jnp.exp(total[0:1, :])
@@ -446,9 +471,9 @@
         grid=(count,),
         in_specs=[tile(width)] + [whole(a) for a in fixed] + part_specs(parts) + pinned(pins),
         out_specs=[tile(cw)] + [tile(width)] * 4 + [tile(cw)] * 6 + [tile(wn.shape[0]), tile(fn.shape[0])]
-        + [pl.BlockSpec((1, HEAD, cw), lambda t: (t, 0, 0))],
+        + [pl.BlockSpec((length // TOKENS, HEAD, cw), lambda t: (t, 0, 0))],
         out_shape=[shape(cw, BF16)] + [shape(width, BF16)] * 4 + [shape(cw, BF16)] * 3 + [shape(cw, F32)] * 3
-        + [shape(wn.shape[0], F32), shape(fn.shape[0], F32), jax.ShapeDtypeStruct((count, HEAD, cw), F32)],
+        + [shape(wn.shape[0], F32), shape(fn.shape[0], F32), jax.ShapeDtypeStruct((tokens // TOKENS, HEAD, cw), F32)],
         scratch_shapes=[
             pltpu.VMEM((length, width), F32), pltpu.VMEM((length, width), F32), pltpu.VMEM((8, width), F32),
             pltpu.VMEM((cw, cw), F32),
@@ -519,8 +544,8 @@
     hidden_ref[...] = hidden
     squared = (hidden * hidden).astype(BF16)
     squared_ref[...] = squared
-    for at in range(0, width, 2 * CHUNK):
-        c = slice(at, at + 2 * CHUNK)
+    for at in range(0, width, CHUNK):
+        c = slice(at, at + CHUNK)
         value_ref[:, c] = nt(squared, w_ref[c, units:]).astype(BF16)
     store_half(place_ref, value_ref, outs)
 
@@ -559,7 +584,7 @@
     tokens, width = recept.shape
     length = 256
     half = gate.shape[1]
-    step = min(2 * CHUNK, half)
+    step = min(CHUNK, half)
     rows = 128
     tiles, per = tokens // length, length // rows
     split = cot_mine.shape[0] < tiles * per
@@ -604,9 +629,9 @@
 
 
 def ffn_backward(halves, place_ref, mine_ref, other_ref, hidden_ref, w_all, *refs):
-    d_values_ref, d_hidden_ref = refs[-5 - halves : -3 - halves]
-    outs = refs[-3 - halves : -3]
-    w_ref, value_ref, sem = refs[-3:]
+    d_hidden_ref = refs[-5 - halves]
+    outs = refs[-4 - halves : -4]
+    w_ref, d_values_ref, value_ref, sem = refs[-4:]
     width = d_values_ref.shape[1]
     half = mine_ref.shape[1]
     units = hidden_ref.shape[1]
@@ -626,8 +651,8 @@
 
     d_hidden = (nn(d_values_ref[...], w_ref[:, units:]) * 2.0 * hidden_ref[...]).astype(BF16)
     d_hidden_ref[...] = d_hidden
-    for at in range(0, width, 2 * CHUNK):
-        c = slice(at, at + 2 * CHUNK)
+    for at in range(0, width, CHUNK):
+        c = slice(at, at + CHUNK)
         value_ref[:, c] = nt(d_hidden, w_ref[c, :units]).astype(BF16)
     store_half(place_ref, value_ref, outs)
 
@@ -646,12 +671,13 @@
             num_scalar_prefetch=1,
             grid=(tokens // length,),
             in_specs=[tile(half), tile(half), tile(units)] + pinned([w]) + pinned(pins),
-            out_specs=[tile(width), tile(units)] + specs,
+            out_specs=[tile(units)] + specs,
             scratch_shapes=[
-                pltpu.VMEM(w.shape, BF16), pltpu.VMEM((length, width), BF16), pltpu.SemaphoreType.DMA,
+                pltpu.VMEM(w.shape, BF16), pltpu.VMEM((length, width), BF16), pltpu.VMEM((length, width), BF16),
+                pltpu.SemaphoreType.DMA,
             ],
         ),
-        out_shape=[shape(width), shape(units)] + shapes,
+        out_shape=[shape(units)] + shapes,
         compiler_params=params(),
         cost_estimate=light(),
         name="ffn_backward",
@@ -680,6 +706,43 @@
         cost_estimate=light(),
         name="grad",
     )(x, d, *pins)
+
+
+def call_grad_halves(place, mine, other, d):
+    tokens, half = mine.shape
+    units = d.shape[1]
+    columns = 512
+    per = half // columns
+
+    def kernel(place_ref, mine_ref, other_ref, d_ref, out_ref):
+        @pl.when(pl.program_id(0) < per)
+        def _():
+            out_ref[...] = tn(mine_ref[...], d_ref[...]).astype(BF16)
+
+        @pl.when(pl.program_id(0) >= per)
+        def _():
+            out_ref[...] = tn(other_ref[...], d_ref[...]).astype(BF16)
+
+    def to(t, place):
+        return (jnp.where(t < per, place[1] * per + t, (1 - place[1]) * per + t - per), 0)
+
+    return pl.pallas_call(
+        kernel,
+        grid_spec=pltpu.PrefetchScalarGridSpec(
+            num_scalar_prefetch=1,
+            grid=(2 * per,),
+            in_specs=[
+                pl.BlockSpec((tokens, columns), lambda t, place: (0, jnp.minimum(t, per - 1))),
+                pl.BlockSpec((tokens, columns), lambda t, place: (0, jnp.maximum(t - per, 0))),
+                pl.BlockSpec(d.shape, lambda t, place: (0, 0), pipeline_mode=pl.Buffered(1)),
+            ],
+            out_specs=pl.BlockSpec((columns, units), to),
+        ),
+        out_shape=jax.ShapeDtypeStruct((2 * half, units), BF16),
+        compiler_params=params(),
+        cost_estimate=light(),
+        name="grad_halves",
+    )(place, mine, other, d)
 
 
 def call_grads(xs, ds, gated, d_att, segs, pins):
@@ -765,7 +828,7 @@
     length, width = recept_in.shape
     count, half = blocks.shape[0], gate_mine.shape[1]
     cw = width // group
-    step = min(2 * CHUNK, half)
+    step = min(CHUNK, half)
 
     def kernel(place_ref, recept_ref, blocks_ref, cot_ref, residual_ref, mine_ref, other_ref, *refs):
         out_ref, cut_ref, d_ref, gate_ref = refs[-4:]
@@ -780,9 +843,9 @@
                 gate_ref[:, c] = (cot_ref[:, c].astype(F32) * values * gate * (1.0 - gate)).astype(BF16)
         for i in range(group):
             cut_ref[i] = gate_ref[:, i * cw : (i + 1) * cw]
-        for at in range(0, width, 2 * CHUNK):
-            c = slice(at, at + 2 * CHUNK)
-            d = jnp.zeros((length, 2 * CHUNK), F32)
+        for at in range(0, width, CHUNK):
+            c = slice(at, at + CHUNK)
+            d = jnp.zeros((length, CHUNK), F32)
             for ref, core in cores:
                 d = d + nt(gate_ref[:, pl.ds(pl.multiple_of(core * half, half), half)], ref[c, :])
             d_ref[:, c] = d
@@ -821,8 +884,8 @@
                 received = received + ref[...]
             w_ref[...] = jnp.where(place_ref[2] == 1, own_ref[...], received)
 
-        for at in range(0, width, 2 * CHUNK):
-            c = slice(at, at + 2 * CHUNK)
+        for at in range(0, width, CHUNK):
+            c = slice(at, at + CHUNK)
             value_ref[:, c] = nn(gated_ref[...], w_ref[:, c]).astype(BF16)
         store_half(place_ref, value_ref, refs[-2 - len(specs) : -2])
 
@@ -847,7 +910,7 @@
 
 def call_add(mine, other, pins):
     rows, width = mine.shape
-    length = 128
+    length = 256
 
     def kernel(a_ref, b_ref, *refs):
         refs[-1][...] = (a_ref[...].astype(F32) + b_ref[...].astype(F32)).astype(BF16)
@@ -865,30 +928,44 @@
     )(mine, other, *pins)
 
 
-def call_wkv_backward(length, d, r, k, v, w, graw, wkv, dm, w_out, own, ones, sums, start, ends, adj, pins):
+def call_wkv_backward(
+    length, d, r, k, v, w, graw, wkv, dm, w_out, own, ones, sums, start, ends, adjoints, place, pins
+):
     tokens, cw = r.shape
     count = tokens // length
-    tile = lambda n: pl.BlockSpec((length, n), lambda t: (count - 1 - t, 0))
+    tile = lambda n: pl.BlockSpec((length, n), lambda t, place: (count - 1 - t, 0))
+    fixed = lambda a: pl.BlockSpec(a.shape, lambda t, place: (0, 0))
     shape = lambda dtype: jax.ShapeDtypeStruct((tokens, cw), dtype)
     wide = dm.shape[1]
+
+    def folded(a, core):
+        rows = a.shape[1] - length
+        at = lambda t, place: jnp.clip(count - 1 - t - core(place) * (count // 2), 0, count // 2 - 1)
+        return pl.BlockSpec((1, rows, a.shape[2]), lambda t, place: (at(t, place), length // rows, 0))
+
+    if len(adjoints) == 2:
+        states = [folded(adjoints[0], lambda place: place[1]), folded(adjoints[1], lambda place: 1 - place[1])]
+    else:
+        states = [pl.BlockSpec((1, HEAD, cw), lambda t, place: (count - 1 - t, 0, 0))]
     return pl.pallas_call(
         wkv_backward,
-        grid=(count,),
-        in_specs=[tile(d.shape[1])] + [tile(cw)] * 6 + [tile(wide)]
-        + [whole(a) for a in (w_out, own, ones, sums, start)]
-        + [
-            pl.BlockSpec((1, HEAD, cw), lambda t: (jnp.maximum(count - 2 - t, 0), 0, 0)),
-            pl.BlockSpec((1, HEAD, cw), lambda t: (count - 1 - t, 0, 0)),
-        ]
-        + pinned(pins),
-        out_specs=[pl.BlockSpec((32, cw), lambda t: (0, 0)), pl.BlockSpec((wide, cw), lambda t: (0, 0))] + [tile(cw)] * 5,
+        grid_spec=pltpu.PrefetchScalarGridSpec(
+            num_scalar_prefetch=1,
+            grid=(count,),
+            in_specs=[tile(d.shape[1])] + [tile(cw)] * 6 + [tile(wide)]
+            + [fixed(a) for a in (w_out, own, ones, sums, start)]
+            + [pl.BlockSpec((1, HEAD, cw), lambda t, place: (jnp.maximum(count - 2 - t, 0), 0, 0))]
+            + states + pinned(pins),
+            out_specs=[pl.BlockSpec((32, cw), lambda t, place: (0, 0)), pl.BlockSpec((wide, cw), lambda t, place: (0, 0))]
+            + [tile(cw)] * 5,
+            scratch_shapes=[pltpu.VMEM((cw, cw), F32)],
+        ),
         out_shape=[jax.ShapeDtypeStruct((32, cw), F32), jax.ShapeDtypeStruct((wide, cw), F32)]
         + [shape(BF16)] * 4 + [shape(F32)],
-        scratch_shapes=[pltpu.VMEM((cw, cw), F32)],
         compiler_params=params(),
         cost_estimate=light(),
         name="wkv_backward",
-    )(d, r, k, v, w, graw, wkv, dm, w_out, own, ones, sums, start, ends, adj, *pins)
+    )(place, d, r, k, v, w, graw, wkv, dm, w_out, own, ones, sums, start, ends, *adjoints, *pins)
 
 
 def call_mix_backward(
@@ -1057,20 +1134,17 @@
     if seqs == 2:
         adjoints = adjoints.reshape(HEAD, seqs, chans, cw).transpose(2, 0, 1, 3).reshape(chans, HEAD, seqs * cw)
         high = adjoints.astype(BF16)
-        adjoints = jnp.concatenate([high, (adjoints - high.astype(F32)).astype(BF16)], 1).reshape(chans, -1, width)
+        adjoints = jnp.concatenate([high, (adjoints - high.astype(F32)).astype(BF16)], 1)
+        fold_rows = 2 * HEAD * seqs * cw // width
+        adjoints = adjoints.reshape(chans, -1, fold_rows, seqs * cw).transpose(0, 2, 1, 3).reshape(chans, fold_rows, width)
         sent = jnp.concatenate([jnp.broadcast_to(cot[None], (chans, length, width)), adjoints], 1)
         cot_mine = lax.all_to_all(sent, "chan", 0, 0, tiled=True)
         cot_other = lax.ppermute(cot_mine, "seq", SWAP)
 
-        def state_part(a):
-            a = a[:, length:].reshape(chans, 2, HEAD, seqs, cw).astype(F32)
-            return lax.dynamic_index_in_dim(a[:, 0] + a[:, 1], me, 2, False)
-
-        low, high = state_part(cot_mine), state_part(cot_other)
-        adjoints = jnp.where(me == 0, jnp.concatenate([low, high]), jnp.concatenate([high, low]))
+        adjoints = (cot_mine, cot_other)
     else:
         cot_mine = cot_other = gather_group(cot).reshape(group, length, width)
-        adjoints = lax.all_to_all(adjoints.reshape(HEAD, group, cw).transpose(1, 0, 2), TP, 0, 0, tiled=True)
+        adjoints = (lax.all_to_all(adjoints.reshape(HEAD, group, cw).transpose(1, 0, 2), TP, 0, 0, tiled=True),)
 
     rows = jnp.concatenate(
         [
@@ -1088,7 +1162,7 @@
     place = jnp.stack([seg, me]).astype(jnp.int32)
 
     gated, xk, xv, xr, xg, r, k, v, w, graw, wkv, lm, dm, ends = call_forward(
-        rank, length, x_all, rows, own, wn, ww, fn, fw, ones, start, place, four, ()
+        rank, 2 * length, x_all, rows, own, wn, ww, fn, fw, ones, start, place, four, ()
     )
     *out, w_out = call_out(
         place, gated, out_rows, out_parts, (seg == p // share).astype(jnp.int32), seqs, [cot_mine]
@@ -1121,9 +1195,15 @@
     value_blocks, sent = reduce_group(values)
     d_mine = call_ffn_gate(recept_all, cot_mine, cot_other, gate_mine, place, [sent])
     d_other = lax.ppermute(d_mine, "seq", SWAP) if seqs == 2 else d_mine
-    d_values, d_hidden, *d_key = call_ffn_backward(d_mine, d_other, hidden, w_ffn, place, seqs, [value_blocks])
-    key_blocks, sent = reduce_group(d_key)
-    grad_ffn_value = reduce_rows(call_grad(d_values, squared, [sent]))
+    if seqs == 2:
+        grad_ffn_value = call_grad_halves(place, d_mine, d_other, squared)
+    else:
+        grad_ffn_value = call_grad(d_mine, squared, ())
+    d_hidden, *d_key = call_ffn_backward(
+        d_mine, d_other, hidden, w_ffn, place, seqs, [value_blocks, grad_ffn_value]
+    )
+    grad_ffn_value = reduce_rows(grad_ffn_value)
+    key_blocks, _ = reduce_group(d_key)
 
     output, d_gate_cut, d_fr = call_ffn_local(
         place, recept_in, value_blocks, result_adjoint[0], residual, gate_mine, gate_other, group, ()
@@ -1146,16 +1226,21 @@
     )
 
     def join_hidden(a):
-        return lax.all_to_all(a, "seq", 0, 1, tiled=True).astype(F32)
+        if seqs != 2:
+            return lax.all_to_all(a, "seq", 0, 1, tiled=True).astype(F32)
+        part = a.shape[0] // 2
+        kept = lax.dynamic_slice_in_dim(a, me * part, part, 0).astype(F32)
+        came = lax.ppermute(lax.dynamic_slice_in_dim(a, (1 - me) * part, part, 0), "seq", SWAP).astype(F32)
+        return jnp.where(me == 0, jnp.concatenate([kept, came], 1), jnp.concatenate([came, kept], 1))
 
     ends_high = ends.astype(BF16)
     ends_low = (ends - ends_high.astype(F32)).astype(BF16)
-    moved = after(jnp.concatenate([d_gate_cut, ends_high, ends_low], 1), d_att)
+    moved = after_all(jnp.concatenate([d_gate_cut, ends_high, ends_low], 1), [d_att, grad_ffn_key])
     moved = lax.all_to_all(moved, TP, 0, 0, tiled=True)
     d_gate_own = moved[:, :length].reshape(tokens, cw)
     end_states = moved[:, length : length + HEAD].astype(F32) + moved[:, length + HEAD :].astype(F32)
     own_sums, decay_up, dr, dk, dv, dg, d_pre = call_wkv_backward(
-        length, d_att, r, k, v, w, graw, wkv, dm, w_out, own, ones, sum_table(length), start, ends, adjoints,
+        length, d_att, r, k, v, w, graw, wkv, dm, w_out, own, ones, sum_table(length), start, ends, adjoints, place,
         [grad_ffn_key],
     )
     grads = call_grads([xr, xk, xv, xg, recept_all], [dr, dk, dv, dg, d_gate_own], gated, d_att, segs, ())
@@ -1164,7 +1249,7 @@
     more = lax.dynamic_update_slice(jnp.zeros((16 * -(-(8 + decays) // 16), width), F32), more, (4, p * cw))
     more = lax.dynamic_update_slice(more, ffn_sums, (0, 0)).astype(BF16)
     packed, *dx = call_mix_backward(
-        rank, length, x_all, rows, lm, dm, dr, dk, dv, dg, d_pre, wn, ww, fn, fw, more, place, four, decays, seqs,
+        rank, 2 * length, x_all, rows, lm, dm, dr, dk, dv, dg, d_pre, wn, ww, fn, fw, more, place, four, decays, seqs,
         [grads],
     )
     dx_blocks, _ = reduce_group(dx)
@@ -1172,8 +1257,8 @@
     input_grad = d_residual + dx_total
 
     five = summed[:5].reshape(5, group, block, cw).transpose(1, 0, 2, 3).reshape(group, -1, cw)
-    grad_ffn_value = join_hidden(after(grad_ffn_value, dx_blocks))
-    grad_ffn_key = join_hidden(after(reduce_rows(grad_ffn_key), dx_blocks))
+    grad_ffn_value = join_hidden(grad_ffn_value)
+    grad_ffn_key = join_hidden(reduce_rows(grad_ffn_key))
     grad_out = summed[5].reshape(group, cw // segs, cw).transpose(1, 0, 2).reshape(cw // segs, width)
     grad_out = lax.ppermute(
         grad_out, ALL, [(i * group + j, segs * j + i) for i in range(segs) for j in range(group)]

time: 782 us -> 747 us (0.955); the launches traced: 767 us -> 742 us
  Pallas kernels: 236 us -> 226 us
  local copies, waits for them, and re-layouts: 61.1 us -> 52.4 us
    all_to_all x1, waiting for transfers between devices: 28.6 us -> 0.01 us  [on_device(): mixed = lax.all_to_all(mixed, TP, 0, 0, tiled=True)]
    ppermute x1, waiting for transfers between devices: 6.98 us -> 35 us  [on_device(): lax.ppermute(grad_out, ALL, [(i * group + j, segs * j + i) for i in range...]
    all_to_all x4, waiting for transfers between devices: 118 us -> 93.2 us  [reduce_chan(): lax.all_to_all(total.reshape(chans, -1, total.shape[1]), 'chan', 0, 0, ti...]
    ppermute x3, waiting for transfers between devices: 22.2 us -> 32.5 us  [reduce_segs(): lax.ppermute(a, 'seg', flips[m + 1]).astype(F32)]
    pallas_call x1 -> x2, Pallas kernels: 25.6 us -> 35.8 us  [the longest x1 26.5 us: call_wkv_backward(): pl.pallas_call(wkv_backward, grid_spec=pltpu.PrefetchScalarGridSpec(num_s...]
    pallas_call x2 -> x1, Pallas kernels: 16.5 us -> 8.33 us  [call_grad(): pl.pallas_call(kernel, grid=(width // columns,), in_specs=[pl.BlockSpec((...]
    reduce_scatter x3, waiting for transfers between devices: 0.04 us -> 8.17 us  [reduce_rows(): return lax.psum_scatter(a, 'seg', scatter_dimension=0, tiled=True)]
    add x8 -> x6, other arithmetic: 15.7 us -> 12.4 us  [after(): return a + (corner.astype(F32) * 0.0).astype(a.dtype)]
  transfers between devices with their start and end apart: 34 -> 35, of which waited for: 20 -> 20; matrix products, arithmetic and copies ran while one was open for 8% -> 7% of each run, Pallas kernels for 26% -> 28%
where the time goes in v3:
time: 747 us; the launch traced here: 742 us
  waiting for transfers between devices  351 us (47%)
  Pallas kernels  226 us (30%)
  starting transfers between devices  56.1 us (8%)
  local copies, waits for them, and re-layouts  52.4 us (7%)
  other arithmetic  35.7 us (5%)
  between operations  21.2 us (3%)
    all_to_all x4, waiting for transfers between devices, reduce_chan(): lax.all_to_all(total.reshape(chans, -1, total.shape[1]), 'chan', 0, 0, ti...  93.2 us
    all_gather x3, waiting for transfers between devices, gather_group(): return lax.all_gather(block, TP, axis=0, tiled=True)  84.1 us
    pallas_call x1, Pallas kernels, call_mix_backward(): pl.pallas_call(lambda *refs: mix_backward(rank, len(specs), *refs), grid_...  50.6 us
    ppermute x3, waiting for transfers between devices, seg_parts(): return [a] + [lax.ppermute(a, 'seg', flips[m]) for m in range(1, segs)]  43 us
    ppermute x1, waiting for transfers between devices, on_device(): lax.ppermute(grad_out, ALL, [(i * group + j, segs * j + i) for i in range...  35 us
    ppermute x3, waiting for transfers between devices, reduce_segs(): lax.ppermute(a, 'seg', flips[m + 1]).astype(F32)  32.5 us
    pallas_call x1, Pallas kernels, call_forward(): pl.pallas_call(lambda *refs: mix_forward(rank, *refs), grid=(count,), in_...  31.8 us
    pallas_call x1, Pallas kernels, call_wkv_backward(): pl.pallas_call(wkv_backward, grid_spec=pltpu.PrefetchScalarGridSpec(num_s...  26.5 us
  transfers between devices with their start and end apart: 35, of which 20 were waited for; matrix products, arithmetic and copies ran while one was open for 7% of the time, Pallas kernels for 28%

profile of v3, /device:TPU:1, one launch (start us, length us, event | category | flops | bytes accessed | tf_op | source)
XLA Modules:
  0.0 741.8 jit_solution(5100803128737886029)
XLA Ops:
  15.3 21.1 %collective-permute-done.2.refs_13_.refs_19_ = bf16[512,1024]{1,0:T(8,128)(2,1)S(1)} collective-permute-done((bf16[512,1024]{1,0:T(8,128)(2,1)S(1)}, bf16[512,1024]{1,0:T(8,128)(2,1)S(1)}, u32[]{:S(2)}, u32[]{:S(2)}) %collective-permute-start.2) | collective-permute-done | bytes 1048608 | tf_op jit(solution)/shard_map/ppermute | solution.py:1105
  37.6 22.0 %collective-permute-done.1.refs_12_.refs_18_ = bf16[512,1024]{1,0:T(8,128)(2,1)} collective-permute-done((bf16[512,1024]{1,0:T(8,128)(2,1)S(1)}, bf16[512,1024]{1,0:T(8,128)(2,1)}, u32[]{:S(2)}, u32[]{:S(2)}) %collective-permute-start.1) | collective-permute-done | bytes 1048608 | tf_op jit(solution)/shard_map/ppermute | solution.py:1105
  88.8 31.8 %mix_forward.1 = (bf16[1024,256]{1,0:T(8,128)(2,1)}, bf16[1024,2048]{1,0:T(8,128)(2,1)}, bf16[1024,2048]{1,0:T(8,128)(2,1)}, bf16[1024,2048]{1,0:T(8,128)(2,1)},...) custom-call(bf16[1024,2048]{1,0:T(8,128)(2,1)} %bitcast.134, ...), custom_call_target="tpu_custom_call" | custom-call | tf_op jit(solution)/shard_map/mix_forward/pallas_call | solution.py:469
  120.7 13.3 %all-to-all-done.refs_3_.mine_ref.adj_ref = bf16[4,160,2048]{2,1,0:T(8,128)(2,1)S(1)} async-done(((bf16[4,160,2048]{2,1,0:T(8,128)(2,1)}), bf16[4,160,2048]{2,1,0:T(8,128)(2,1)S(1)}, u32[]{:S(2)}, u32[]{:S(2)}) %all-to-all-start) | async-done | bytes 2621472 | tf_op jit(solution)/shard_map/all_to_all | solution.py:1141
  135.5 7.7 %out_projection.1 = (bf16[512,2048]{1,0:T(8,128)(2,1)}, bf16[512,2048]{1,0:T(8,128)(2,1)}, bf16[256,2048]{1,0:T(8,128)(2,1)}) custom-call(s32[3]{0:T(128)} %pad_add_fusion.1.place_ref, bf16[1024,256]{1,0:T(8,128)(2,1)} %get-tuple-element.69.gated_ref.refs_10_, bf16[256,2048]{1,0:T(8,128)(2,1)} %dynamic-slice_add_fusion.1.own_ref, ...), custom_call_target="tpu_custom_call" | custom-call | tf_op jit(solution)/shard_map/out_projection/pallas_call | solution.py:894
  158.5 47.1 %all-to-all-done.1.blocks_ref = bf16[4,128,2048]{2,1,0:T(8,128)(2,1)S(1)} async-done(((bf16[4,128,2048]{2,1,0:T(8,128)(2,1)}), bf16[4,128,2048]{2,1,0:T(8,128)(2,1)S(1)}, u32[]{:S(2)}, u32[]{:S(2)}) %all-to-all-start.1) | async-done | bytes 2097184 | tf_op jit(solution)/shard_map/all_to_all | solution.py:1016
  211.8 45.3 %all-gather.9.cloned.1.call-done.refs_1_.refs_2_ = bf16[1024,2048]{1,0:T(8,128)(2,1)} async-done(((bf16[128,2048]{1,0:T(8,128)(2,1)}), bf16[1024,2048]{1,0:T(8,128)(2,1)}) %all-gather.9.cloned.1.call-update) | async-done | bytes 4194320 | tf_op jit(solution)/shard_map/all_gather | solution.py:1003
  261.7 19.5 %ffn_forward.1 = (bf16[1024,2048]{1,0:T(8,128)(2,1)}, bf16[1024,2048]{1,0:T(8,128)(2,1)}, f32[1024,896]{1,0:T(8,128)}, bf16[1024,896]{1,0:T(8,128)(2,1)}, bf16[5...) custom-call(s32[2]{0:T(128)} %pad_add_fusion.refs_9_.refs_0_.place_ref, ...), custom_call_target="tpu_custom_call" | custom-call | tf_op jit(solution)/shard_map/ffn_forward/pallas_call | solution.py:560
  295.6 16.9 %all-gather.11.cloned.1.call-done.mine_ref.gate_ref = bf16[2048,1024]{1,0:T(8,128)(2,1)} async-done(((bf16[512,1024]{1,0:T(8,128)(2,1)}), bf16[2048,1024]{1,0:T(8,128)(2,1)}) %all-gather.11.cloned.1.call-update) | async-done | bytes 4194320 | tf_op jit(solution)/shard_map/all_gather | solution.py:1183
  312.5 9.8 %ffn_gate.1.mine_ref.refs_1_ = bf16[1024,1024]{1,0:T(8,128)(2,1)} custom-call(s32[2]{0:T(128)} %pad_add_fusion.refs_9_.refs_0_.place_ref, bf16[1024,2048]{1,0:T(8,128)(2,1)} %get-tuple-element.81.recept_ref.refs_4_, bf16[4,160,2048]{2,1,0:T(8,128)(2,1)} %copy-done.2, bf16[4,160,2048]{2,1,0:T(8,128)(2,1)} %collective-permute-done.9.other_ref.refs_0_, ...), custom_call_target="tpu_custom_call" | custom-call | tf_op jit(solution)/shard_map/ffn_gate/pallas_call | solution.py:611
  328.3 9.3 %grad_halves.1.refs_6_ = bf16[2048,896]{1,0:T(8,128)(2,1)} custom-call(s32[2]{0:T(128)} %pad_add_fusion.refs_9_.refs_0_.place_ref, bf16[1024,1024]{1,0:T(8,128)(2,1)} %ffn_gate.1.mine_ref.refs_1_, bf16[1024,1024]{1,0:T(8,128)(2,1)} %copy-done.6, bf16[1024,896]{1,0:T(8,128)(2,1)} %get-tuple-element.83.d_ref), custom_call_target="tpu_custom_call" | custom-call | tf_op jit(solution)/shard_map/grad_halves/pallas_call | solution.py:729
  343.7 17.1 %ffn_backward.1 = (bf16[1024,896]{1,0:T(8,128)(2,1)}, bf16[512,2048]{1,0:T(8,128)(2,1)}, bf16[512,2048]{1,0:T(8,128)(2,1)}) custom-call(s32[2]{0:T(128)} %pad_add_fusion.refs_9_.refs_0_.place_ref, bf16[1024,1024]{1,0:T(8,128)(2,1)} %ffn_gate.1.mine_ref.refs_1_, bf16[1024,1024]{1,0:T(8,128)(2,1)} %copy-done.6, f32[1024,896]{1,0:T(8,128)} %get-tuple-element.82.refs_3_, ...), custom_call_target="tpu_custom_call" | custom-call | tf_op jit(solution)/shard_map/ffn_backward/pallas_call | solution.py:668
  361.9 6.1 collective-permute-done.11.b_ref
  379.3 11.0 %ffn_local.1 = (bf16[128,2048]{1,0:T(8,128)(2,1)}, bf16[8,128,256]{2,1,0:T(8,128)(2,1)}, f32[128,2048]{1,0:T(8,128)}) custom-call(s32[2]{0:T(128)} %pad_add_fusion.refs_9_.refs_0_.place_ref, bf16[128,2048]{1,0:T(8,128)(2,1)} %add_convert_fusion.recept_ref, bf16[4,128,2048]{2,1,0:T(8,128)(2,1)} %all-to-all-done.2.blocks_ref.refs_5_, ...), custom_call_target="tpu_custom_call" | custom-call | tf_op jit(solution)/shard_map/ffn_local/pallas_call | solution.py:855
  390.3 35.0 %all-to-all-done.3 = bf16[4,128,2048]{2,1,0:T(8,128)(2,1)} async-done(((bf16[4,128,2048]{2,1,0:T(8,128)(2,1)}), bf16[4,128,2048]{2,1,0:T(8,128)(2,1)}, u32[]{:S(2)}, u32[]{:S(2)}) %all-to-all-start.3) | async-done | bytes 2097184 | tf_op jit(solution)/shard_map/all_to_all | solution.py:1016
  439.2 8.3 %grad.1.refs_1_ = bf16[2048,896]{1,0:T(8,128)(2,1)} custom-call(bf16[1024,2048]{1,0:T(8,128)(2,1)} %get-tuple-element.88.x_ref, bf16[1024,896]{1,0:T(8,128)(2,1)} %get-tuple-element.89.d_ref, bf16[128,2048]{1,0:T(8,128)(2,1)} %get-tuple-element.169.refs_0_), custom_call_target="tpu_custom_call" | custom-call | tf_op jit(solution)/shard_map/grad/pallas_call | solution.py:695
  449.4 38.7 %all-gather.13.cloned.1.call-done.d_ref.refs_11_ = bf16[1024,2048]{1,0:T(8,128)(2,1)} async-done(((bf16[128,2048]{1,0:T(8,128)(2,1)}), bf16[1024,2048]{1,0:T(8,128)(2,1)}) %all-gather.13.cloned.1.call-update) | async-done | bytes 4194320 | tf_op jit(solution)/shard_map/all_gather | solution.py:1003
  494.9 26.5 %wkv_backward.1 = (f32[32,256]{1,0:T(8,128)}, f32[64,256]{1,0:T(8,128)}, bf16[1024,256]{1,0:T(8,128)(2,1)}, bf16[1024,256]{1,0:T(8,128)(2,1)}, bf16[1024,256]{1,...) custom-call(s32[2]{0:T(128)} %pad_add_fusion.refs_9_.refs_0_.place_ref, ...), custom_call_target="tpu_custom_call" | custom-call | tf_op jit(solution)/shard_map/wkv_backward/pallas_call | solution.py:950
  522.4 15.6 %grads.1.refs_20_ = bf16[4,6,512,256]{3,2,1,0:T(8,128)(2,1)} custom-call(bf16[1024,2048]{1,0:T(8,128)(2,1)} %get-tuple-element.106.refs_0_, bf16[1024,2048]{1,0:T(8,128)(2,1)} %get-tuple-element.107.refs_1_, bf16[1024,2048]{1,0:T(8,128)(2,1)} %get-tuple-element.108.refs_2_, bf16[1024,2048]{1,0:T(8,128)(2,1)} %get-tuple-element.109.refs_3_, ...), custom_call_target="tpu_custom_call" | custom-call | tf_op jit(solution)/shard_map/grads/pallas_call | solution.py:772
  540.7 50.6 %mix_backward.1 = (bf16[480,2048]{1,0:T(8,128)(2,1)}, bf16[512,2048]{1,0:T(8,128)(2,1)}, bf16[512,2048]{1,0:T(8,128)(2,1)}) custom-call(s32[2]{0:T(128)} %pad_add_fusion.refs_9_.refs_0_.place_ref, bf16[1024,2048]{1,0:T(8,128)(2,1)} %bitcast.135, bf16[1024,2048]{1,0:T(8,128)(2,1)} %bitcast.136, f32[24,2048]{1,0:T(8,128)} %copy-done.22, ...), custom_call_target="tpu_custom_call" | custom-call | tf_op jit(solution)/shard_map/mix_backward/pallas_call | solution.py:983
  610.0 10.7 %collective-permute-done.16 = bf16[480,512]{1,0:T(8,128)(2,1)S(1)} collective-permute-done((bf16[480,512]{1,0:T(8,128)(2,1)}, bf16[480,512]{1,0:T(8,128)(2,1)S(1)}, u32[]{:S(2)}, u32[]{:S(2)}) %collective-permute-start.16) | collective-permute-done | bytes 491552 | tf_op jit(solution)/shard_map/ppermute | solution.py:1113
  620.7 21.9 %collective-permute-done.15 = bf16[480,512]{1,0:T(8,128)(2,1)} collective-permute-done((bf16[480,512]{1,0:T(8,128)(2,1)}, bf16[480,512]{1,0:T(8,128)(2,1)}, u32[]{:S(2)}, u32[]{:S(2)}) %collective-permute-start.15) | collective-permute-done | bytes 491552 | tf_op jit(solution)/shard_map/ppermute | solution.py:1113
  664.1 8.1 %reduce-scatter.8.cloned.1.call-done = bf16[512,896]{1,0:T(8,128)(2,1)} async-done(((bf16[2048,896]{1,0:T(8,128)(2,1)}), bf16[512,896]{1,0:T(8,128)(2,1)}) %reduce-scatter.8.cloned.1.call-update) | async-done | bytes 917520 | tf_op jit(solution)/shard_map/reduce_scatter | solution.py:1116
  686.5 35.0 %collective-permute-done.17 = bf16[64,2048]{1,0:T(8,128)(2,1)S(1)} collective-permute-done((bf16[64,2048]{1,0:T(8,128)(2,1)S(1)}, bf16[64,2048]{1,0:T(8,128)(2,1)S(1)}, u32[]{:S(2)}, u32[]{:S(2)}) %collective-permute-start.17) | collective-permute-done | bytes 262176 | tf_op jit(solution)/shard_map/ppermute | solution.py:1263
  (244 shorter events, 192.3 us)
Async XLA Ops:
  7.2 59.2 %all-gather.15.cloned.1.call-start = ((), (), s32[]{:S(2)}) async-start(), calls=%async_computation.17 | async-start | bytes 4718592 | tf_op jit(solution)/shard_map/all_gather | solution.py:1003
  8.0 150.5 %all-gather.7.cloned.1.call-start = ((), (), s32[]{:S(2)}) async-start(), calls=%async_computation.10 | async-start | bytes 9175040 | tf_op jit(solution)/shard_map/all_gather | solution.py:1131
  13.4 46.2 %collective-permute-start.1 = (bf16[512,1024]{1,0:T(8,128)(2,1)S(1)}, bf16[512,1024]{1,0:T(8,128)(2,1)}, u32[]{:S(2)}, u32[]{:S(2)}) collective-permute-start(bf16[512,1024]{1,0:T(8,128)(2,1)S(1)} %pad_maximum_fusion.1.refs_10_.refs_16_), channel_id=1, source_target_pairs={{0,16},{8,24},{16,0},{24,8},{1,17},{9,25},{17,1},{25,9},{2,18},{10... | collective-permute-start | bytes 3145736 | tf_op jit(solution)/shard_map/ppermute | solution.py:1105
  13.6 47.8 %collective-permute-start = (bf16[512,1024]{1,0:T(8,128)(2,1)S(1)}, bf16[512,1024]{1,0:T(8,128)(2,1)}, u32[]{:S(2)}, u32[]{:S(2)}) collective-permute-start(bf16[512,1024]{1,0:T(8,128)(2,1)S(1)} %pad_maximum_fusion.1.refs_10_.refs_16_), channel_id=1, source_target_pairs={{0,8},{8,0},{16,24},{24,16},{1,9},{9,1},{17,25},{25,17},{2,10},{10... | collective-permute-start | bytes 3145736 | tf_op jit(solution)/shard_map/ppermute | solution.py:1105
  70.3 63.7 %all-to-all-start = ((bf16[4,160,2048]{2,1,0:T(8,128)(2,1)}), bf16[4,160,2048]{2,1,0:T(8,128)(2,1)S(1)}, u32[]{:S(2)}, u32[]{:S(2)}) async-start(bf16[4,160,2048]{2,1,0:T(8,128)(2,1)} %pad_maximum_fusion), calls=%async_computation | async-start | bytes 5242880 | tf_op jit(solution)/shard_map/all_to_all | solution.py:1141
  77.6 43.0 %collective-permute-start.3 = (bf16[256,2048]{1,0:T(8,128)(2,1)}, bf16[256,2048]{1,0:T(8,128)(2,1)}, u32[]{:S(2)}, u32[]{:S(2)}) collective-permute-start(bf16[256,2048]{1,0:T(8,128)(2,1)} %dynamic-slice_add_fusion.1.own_ref), channel_id=1, source_target_pairs={{0,8},{1,9},{10,2},{11,3},{20,28},{21,29},{30,22},{31,23}} | collective-permute-start | bytes 3145736 | tf_op jit(solution)/shard_map/ppermute | solution.py:1127
  79.3 41.4 %collective-permute-start.4 = (bf16[256,2048]{1,0:T(8,128)(2,1)}, bf16[256,2048]{1,0:T(8,128)(2,1)}, u32[]{:S(2)}, u32[]{:S(2)}) collective-permute-start(bf16[256,2048]{1,0:T(8,128)(2,1)} %dynamic-slice_add_fusion.1.own_ref), channel_id=1, source_target_pairs={{0,16},{1,17},{10,26},{11,27},{20,4},{21,5},{30,14},{31,15}} | collective-permute-start | bytes 3145736 | tf_op jit(solution)/shard_map/ppermute | solution.py:1127
  80.5 40.1 %collective-permute-start.5 = (bf16[256,2048]{1,0:T(8,128)(2,1)}, bf16[256,2048]{1,0:T(8,128)(2,1)}, u32[]{:S(2)}, u32[]{:S(2)}) collective-permute-start(bf16[256,2048]{1,0:T(8,128)(2,1)} %dynamic-slice_add_fusion.1.own_ref), channel_id=1, source_target_pairs={{0,24},{1,25},{10,18},{11,19},{20,12},{21,13},{30,6},{31,7}} | collective-permute-start | bytes 3145736 | tf_op jit(solution)/shard_map/ppermute | solution.py:1127
  153.3 52.3 %all-to-all-start.1 = ((bf16[4,128,2048]{2,1,0:T(8,128)(2,1)}), bf16[4,128,2048]{2,1,0:T(8,128)(2,1)S(1)}, u32[]{:S(2)}, u32[]{:S(2)}) async-start(bf16[4,128,2048]{2,1,0:T(8,128)(2,1)} %bitcast.142), calls=%async_computation.1 | async-start | bytes 4194304 | tf_op jit(solution)/shard_map/all_to_all | solution.py:1016
  157.8 99.3 %all-gather.9.cloned.1.call-start = ((), (), s32[]{:S(2)}) async-start(), calls=%async_computation.11 | async-start | bytes 4718592 | tf_op jit(solution)/shard_map/all_gather | solution.py:1003
  211.2 101.4 %all-gather.11.cloned.1.call-start = ((), (), s32[]{:S(2)}) async-start(), calls=%async_computation.12 | async-start | bytes 5242880 | tf_op jit(solution)/shard_map/all_gather | solution.py:1183
  261.4 34.2 %collective-permute-start.9 = (bf16[4,160,2048]{2,1,0:T(8,128)(2,1)S(1)}, bf16[4,160,2048]{2,1,0:T(8,128)(2,1)}, u32[]{:S(2)}, u32[]{:S(2)}) collective-permute-start(bf16[4,160,2048]{2,1,0:T(8,128)(2,1)S(1)} %copy-done.3), channel_id=1, source_target_pairs={{0,4},{4,0},{1,5},{5,1},{2,6},{6,2},{3,7},{7,3},{8,12},{12,8},{9,1... | collective-permute-start | bytes 7864328 | tf_op jit(solution)/shard_map/ppermute | solution.py:1142
  291.1 52.6 %all-to-all-start.2 = ((bf16[4,128,2048]{2,1,0:T(8,128)(2,1)}), bf16[4,128,2048]{2,1,0:T(8,128)(2,1)}, u32[]{:S(2)}, u32[]{:S(2)}) async-start(bf16[4,128,2048]{2,1,0:T(8,128)(2,1)} %bitcast.137), calls=%async_computation.2 | async-start | bytes 4194304 | tf_op jit(solution)/shard_map/all_to_all | solution.py:1016
  295.5 138.9 %reduce-scatter.4.cloned.1.call-start = ((), (), s32[]{:S(2)}) async-start(), calls=%async_computation.13 | async-start | bytes 4587520 | tf_op jit(solution)/shard_map/reduce_scatter | solution.py:1116
  372.7 52.6 %all-to-all-start.3 = ((bf16[4,128,2048]{2,1,0:T(8,128)(2,1)}), bf16[4,128,2048]{2,1,0:T(8,128)(2,1)}, u32[]{:S(2)}, u32[]{:S(2)}) async-start(bf16[4,128,2048]{2,1,0:T(8,128)(2,1)} %bitcast.141), calls=%async_computation.3 | async-start | bytes 4194304 | tf_op jit(solution)/shard_map/all_to_all | solution.py:1016
  377.3 110.9 %all-gather.13.cloned.1.call-start = ((), (), s32[]{:S(2)}) async-start(), calls=%async_computation.14 | async-start | bytes 4718592 | tf_op jit(solution)/shard_map/all_gather | solution.py:1003
  491.2 30.3 %all-to-all-start.4 = ((bf16[8,256,256]{2,1,0:T(8,128)(2,1)}), bf16[8,256,256]{2,1,0:T(8,128)(2,1)S(1)}, u32[]{:S(2)}, u32[]{:S(2)}) async-start(bf16[8,256,256]{2,1,0:T(8,128)(2,1)} %fusion.2), calls=%async_computation.5 | async-start | bytes 2097152 | tf_op jit(solution)/shard_map/all_to_all | solution.py:1239
  494.9 159.0 %reduce-scatter.6.cloned.1.call-start = ((), (), s32[]{:S(2)}) async-start(), calls=%async_computation.15 | async-start | bytes 7864320 | tf_op jit(solution)/shard_map/reduce_scatter | solution.py:1116
  538.0 134.2 %reduce-scatter.8.cloned.1.call-start = ((), (), s32[]{:S(2)}) async-start(), calls=%async_computation.16 | async-start | bytes 4587520 | tf_op jit(solution)/shard_map/reduce_scatter | solution.py:1116
  600.8 52.0 %all-to-all-start.5 = ((bf16[4,128,2048]{2,1,0:T(8,128)(2,1)}), bf16[4,128,2048]{2,1,0:T(8,128)(2,1)S(1)}, u32[]{:S(2)}, u32[]{:S(2)}) async-start(bf16[4,128,2048]{2,1,0:T(8,128)(2,1)} %bitcast.140), calls=%async_computation.6 | async-start | bytes 4194304 | tf_op jit(solution)/shard_map/all_to_all | solution.py:1016
  609.5 33.1 %collective-permute-start.15 = (bf16[480,512]{1,0:T(8,128)(2,1)}, bf16[480,512]{1,0:T(8,128)(2,1)}, u32[]{:S(2)}, u32[]{:S(2)}) collective-permute-start(bf16[480,512]{1,0:T(8,128)(2,1)} %get-tuple-element.184), channel_id=1, source_target_pairs={{0,16},{8,24},{16,0},{24,8},{1,17},{9,25},{17,1},{25,9},{2,18},{10... | collective-permute-start | bytes 1474568 | tf_op jit(solution)/shard_map/ppermute | solution.py:1113
  609.8 32.7 %collective-permute-start.14 = (bf16[480,512]{1,0:T(8,128)(2,1)S(1)}, bf16[480,512]{1,0:T(8,128)(2,1)}, u32[]{:S(2)}, u32[]{:S(2)}) collective-permute-start(bf16[480,512]{1,0:T(8,128)(2,1)S(1)} %get-tuple-element.182), channel_id=1, source_target_pairs={{0,8},{8,0},{16,24},{24,16},{1,9},{9,1},{17,25},{25,17},{2,10},{10... | collective-permute-start | bytes 1474568 | tf_op jit(solution)/shard_map/ppermute | solution.py:1113
  657.0 65.4 %all-to-all-start.6 = ((bf16[8,440,256]{2,1,0:T(8,128)(2,1)}), bf16[8,440,256]{2,1,0:T(8,128)(2,1)}, u32[]{:S(2)}, u32[]{:S(2)}) async-start(bf16[8,440,256]{2,1,0:T(8,128)(2,1)} %maximum_add_fusion.1), calls=%async_computation.8 | async-start | bytes 3604480 | tf_op jit(solution)/shard_map/all_to_all | solution.py:1270
  682.5 39.0 %collective-permute-start.17 = (bf16[64,2048]{1,0:T(8,128)(2,1)S(1)}, bf16[64,2048]{1,0:T(8,128)(2,1)S(1)}, u32[]{:S(2)}, u32[]{:S(2)}) collective-permute-start(bf16[64,2048]{1,0:T(8,128)(2,1)S(1)} %bitcast.172), channel_id=1, source_target_pairs={{0,0},{1,4},{2,8},{3,12},{4,16},{5,20},{6,24},{7,28},{8,1},{9,5},{... | collective-permute-start | bytes 786440 | tf_op jit(solution)/shard_map/ppermute | solution.py:1263
  (49 other events, 532.4 us)
Sparse Core Ops, SparseCore 0:
  9.7 49.6 all-gather.14
  65.2 91.6 all-gather.6
  211.3 45.7 all-gather.8
  261.5 51.0 all-gather.10
  337.8 48.0 reduce-scatter.3
  439.3 48.8 all-gather.12
  538.1 70.8 reduce-scatter.5
  612.0 60.1 reduce-scatter.7

commit v4 on v3

--- a/solution.py
+++ b/solution.py
@@ -13,7 +13,7 @@
 GROUP_EPSILON = 0.00064
 F32 = jnp.float32
 BF16 = jnp.bfloat16
-CHUNK = 512
+CHUNK = 256
 TOKENS = 128
 VMEM = 56 * 2**20
 
@@ -928,6 +928,33 @@
     )(mine, other, *pins)
 
 
+def call_combine(order, mine, other):
+    count, rows, width = mine.shape
+
+    def kernel(order_ref, mine_ref, other_ref, *outs):
+        total = mine_ref[0].astype(F32) + other_ref[0].astype(F32)
+        for k in range(count):
+
+            @pl.when(pl.program_id(0) == k)
+            def _():
+                outs[k][...] = total.astype(outs[k].dtype)
+
+    block = pl.BlockSpec((1, rows, width), lambda k, order: (order[k], 0, 0))
+    return pl.pallas_call(
+        kernel,
+        grid_spec=pltpu.PrefetchScalarGridSpec(
+            num_scalar_prefetch=1,
+            grid=(count,),
+            in_specs=[block, block],
+            out_specs=[pl.BlockSpec((rows, width), lambda k, order: (0, 0))] * count,
+        ),
+        out_shape=[jax.ShapeDtypeStruct((rows, width), F32 if k == 0 else BF16) for k in range(count)],
+        compiler_params=params(),
+        cost_estimate=light(),
+        name="combine",
+    )(order, mine, other)
+
+
 def call_wkv_backward(
     length, d, r, k, v, w, graw, wkv, dm, w_out, own, ones, sums, start, ends, adjoints, place, pins
 ):
@@ -1014,6 +1041,22 @@
 def reduce_chan(total):
     chans = lax.axis_size("chan")
     return lax.all_to_all(total.reshape(chans, -1, total.shape[1]), "chan", 0, 0, tiled=True)
+
+
+def reduce_apart(parts):
+    chans, at = lax.axis_size("chan"), lax.axis_index("chan")
+    if len(parts) == 2:
+        mine, other = parts[0], lax.ppermute(parts[1], "seq", SWAP)
+    else:
+        mine = lax.psum_scatter(parts[0], "seq", scatter_dimension=0, tiled=True)
+        other = jnp.zeros_like(mine)
+    order = ((at + jnp.arange(chans)) % chans).astype(jnp.int32)
+    cut = lambda a: a.reshape(chans, -1, a.shape[1])
+    total, *sent = call_combine(order, cut(mine), cut(other))
+    came = [
+        lax.ppermute(a, "chan", [(i, (i + k + 1) % chans) for i in range(chans)]) for k, a in enumerate(sent)
+    ]
+    return sum((a.astype(F32) for a in came), total), came
 
 
 def add_up(blocks):
@@ -1252,8 +1295,7 @@
         rank, 2 * length, x_all, rows, lm, dm, dr, dk, dv, dg, d_pre, wn, ww, fn, fw, more, place, four, decays, seqs,
         [grads],
     )
-    dx_blocks, _ = reduce_group(dx)
-    dx_total = add_up(dx_blocks)
+    dx_total, dx_came = reduce_apart(dx)
     input_grad = d_residual + dx_total
 
     five = summed[:5].reshape(5, group, block, cw).transpose(1, 0, 2, 3).reshape(group, -1, cw)
@@ -1266,9 +1308,8 @@
     small, _ = reduce_segs(lambda s: lax.dynamic_slice_in_dim(packed, s * rows_seg, rows_seg, 1))
     count = small.shape[0]
     small = small.astype(BF16).reshape(count, group, block).transpose(1, 0, 2).reshape(group, -1, cw)
-    mixed = after(jnp.concatenate([five, small], 1), dx_blocks)
-    mixed = lax.all_to_all(mixed, TP, 0, 0, tiled=True)
-    five, small = mixed[:, : 5 * block], mixed[:, 5 * block :]
+    five = lax.all_to_all(five, TP, 0, 0, tiled=True)
+    small = lax.all_to_all(after_all(small, dx_came), TP, 0, 0, tiled=True)
     five = five.reshape(group, 5, block, cw).transpose(1, 2, 0, 3).reshape(5, block, width).astype(F32)
     small = jnp.sum(small.astype(F32).reshape(group, count, block), 0)
     norm_gain, norm_bias, shift_mix = small[0], small[1], small[2:8].T

time: 747 us -> 740 us (level)
  waiting for transfers between devices: 351 us -> 335 us
    ppermute x0 -> x4, waiting for transfers between devices: none -> 40.7 us  [the longest x3 36.9 us: reduce_apart(): lax.ppermute(a, 'chan', [(i, (i + k + 1) % chans) for i in range(chans)])]
    ppermute x3, waiting for transfers between devices: 32.5 us -> 0.01 us  [reduce_segs(): lax.ppermute(a, 'seg', flips[m + 1]).astype(F32)]
    reduce_scatter x3, waiting for transfers between devices: 8.17 us -> 0.01 us  [reduce_rows(): return lax.psum_scatter(a, 'seg', scatter_dimension=0, tiled=True)]
    ppermute x1, waiting for transfers between devices: 35 us -> 27.1 us  [on_device(): lax.ppermute(grad_out, ALL, [(i * group + j, segs * j + i) for i in range...]
    all_to_all x4 -> x3, waiting for transfers between devices: 93.2 us -> 88.1 us  [reduce_chan(): lax.all_to_all(total.reshape(chans, -1, total.shape[1]), 'chan', 0, 0, ti...]
    ppermute x4 -> x3, waiting for transfers between devices: 18.6 us -> 14.2 us  [reduce_halves(): total = call_add(mine, lax.ppermute(other, 'seq', SWAP), pins)]
    all_to_all x4 -> x3, starting transfers between devices: 17.7 us -> 13.4 us  [reduce_chan(): lax.all_to_all(total.reshape(chans, -1, total.shape[1]), 'chan', 0, 0, ti...]
    unnamed x81 -> x83, local copies, waits for them, and re-layouts: 17.3 us -> 19.2 us
  transfers between devices with their start and end apart: 35 -> 38, of which waited for: 20 -> 19; matrix products, arithmetic and copies ran while one was open for 7% -> 9% of each run, Pallas kernels for 28% -> 30%
where the time goes in v4:
time: 740 us; the launch traced here: 734 us
  waiting for transfers between devices  335 us (45%)
  Pallas kernels  227 us (31%)
  starting transfers between devices  59.3 us (8%)
  local copies, waits for them, and re-layouts  53.2 us (7%)
  other arithmetic  38.2 us (5%)
  between operations  22.5 us (3%)
    all_to_all x3, waiting for transfers between devices, reduce_chan(): lax.all_to_all(total.reshape(chans, -1, total.shape[1]), 'chan', 0, 0, ti...  88.1 us
    all_gather x3, waiting for transfers between devices, gather_group(): return lax.all_gather(block, TP, axis=0, tiled=True)  83.1 us
    pallas_call x1, Pallas kernels, call_mix_backward(): pl.pallas_call(lambda *refs: mix_backward(rank, len(specs), *refs), grid_...  48.3 us
    ppermute x3, waiting for transfers between devices, seg_parts(): return [a] + [lax.ppermute(a, 'seg', flips[m]) for m in range(1, segs)]  43 us
    ppermute x3, waiting for transfers between devices, reduce_apart(): lax.ppermute(a, 'chan', [(i, (i + k + 1) % chans) for i in range(chans)])  36.9 us
    pallas_call x1, Pallas kernels, call_forward(): pl.pallas_call(lambda *refs: mix_forward(rank, *refs), grid=(count,), in_...  31.6 us
    ppermute x1, waiting for transfers between devices, on_device(): lax.ppermute(grad_out, ALL, [(i * group + j, segs * j + i) for i in range...  27.1 us
    pallas_call x1, Pallas kernels, call_wkv_backward(): pl.pallas_call(wkv_backward, grid_spec=pltpu.PrefetchScalarGridSpec(num_s...  27 us
  transfers between devices with their start and end apart: 38, of which 19 were waited for; matrix products, arithmetic and copies ran while one was open for 9% of the time, Pallas kernels for 30%

profile of v4, /device:TPU:1, one launch (start us, length us, event | category | flops | bytes accessed | tf_op | source)
XLA Modules:
  0.0 734.4 jit_solution(17289695553405722024)
XLA Ops:
  15.3 21.1 %collective-permute-done.2.refs_13_.refs_19_ = bf16[512,1024]{1,0:T(8,128)(2,1)S(1)} collective-permute-done((bf16[512,1024]{1,0:T(8,128)(2,1)S(1)}, bf16[512,1024]{1,0:T(8,128)(2,1)S(1)}, u32[]{:S(2)}, u32[]{:S(2)}) %collective-permute-start.2) | collective-permute-done | bytes 1048608 | tf_op jit(solution)/shard_map/ppermute | solution.py:1148
  37.6 22.0 %collective-permute-done.1.refs_12_.refs_18_ = bf16[512,1024]{1,0:T(8,128)(2,1)} collective-permute-done((bf16[512,1024]{1,0:T(8,128)(2,1)S(1)}, bf16[512,1024]{1,0:T(8,128)(2,1)}, u32[]{:S(2)}, u32[]{:S(2)}) %collective-permute-start.1) | collective-permute-done | bytes 1048608 | tf_op jit(solution)/shard_map/ppermute | solution.py:1148
  88.8 31.6 %mix_forward.1 = (bf16[1024,256]{1,0:T(8,128)(2,1)}, bf16[1024,2048]{1,0:T(8,128)(2,1)}, bf16[1024,2048]{1,0:T(8,128)(2,1)}, bf16[1024,2048]{1,0:T(8,128)(2,1)},...) custom-call(bf16[1024,2048]{1,0:T(8,128)(2,1)} %bitcast.137, ...), custom_call_target="tpu_custom_call" | custom-call | tf_op jit(solution)/shard_map/mix_forward/pallas_call | solution.py:469
  120.4 13.6 %all-to-all-done.refs_3_.mine_ref.adj_ref = bf16[4,160,2048]{2,1,0:T(8,128)(2,1)S(1)} async-done(((bf16[4,160,2048]{2,1,0:T(8,128)(2,1)}), bf16[4,160,2048]{2,1,0:T(8,128)(2,1)S(1)}, u32[]{:S(2)}, u32[]{:S(2)}) %all-to-all-start) | async-done | bytes 2621472 | tf_op jit(solution)/shard_map/all_to_all | solution.py:1184
  135.4 7.7 %out_projection.1 = (bf16[512,2048]{1,0:T(8,128)(2,1)}, bf16[512,2048]{1,0:T(8,128)(2,1)}, bf16[256,2048]{1,0:T(8,128)(2,1)}) custom-call(s32[3]{0:T(128)} %pad_add_fusion.1.place_ref, bf16[1024,256]{1,0:T(8,128)(2,1)} %get-tuple-element.73.gated_ref.refs_10_, bf16[256,2048]{1,0:T(8,128)(2,1)} %dynamic-slice_add_fusion.1.own_ref, ...), custom_call_target="tpu_custom_call" | custom-call | tf_op jit(solution)/shard_map/out_projection/pallas_call | solution.py:894
  158.5 47.1 %all-to-all-done.1.blocks_ref = bf16[4,128,2048]{2,1,0:T(8,128)(2,1)S(1)} async-done(((bf16[4,128,2048]{2,1,0:T(8,128)(2,1)}), bf16[4,128,2048]{2,1,0:T(8,128)(2,1)S(1)}, u32[]{:S(2)}, u32[]{:S(2)}) %all-to-all-start.1) | async-done | bytes 2097184 | tf_op jit(solution)/shard_map/all_to_all | solution.py:1043
  211.7 45.3 %all-gather.9.cloned.1.call-done.refs_1_.refs_2_ = bf16[1024,2048]{1,0:T(8,128)(2,1)} async-done(((bf16[128,2048]{1,0:T(8,128)(2,1)}), bf16[1024,2048]{1,0:T(8,128)(2,1)}) %all-gather.9.cloned.1.call-update) | async-done | bytes 4194320 | tf_op jit(solution)/shard_map/all_gather | solution.py:1030
  261.6 19.6 %ffn_forward.1 = (bf16[1024,2048]{1,0:T(8,128)(2,1)}, bf16[1024,2048]{1,0:T(8,128)(2,1)}, f32[1024,896]{1,0:T(8,128)}, bf16[1024,896]{1,0:T(8,128)(2,1)}, bf16[5...) custom-call(s32[2]{0:T(128)} %pad_add_fusion.refs_9_.refs_0_.place_ref, ...), custom_call_target="tpu_custom_call" | custom-call | tf_op jit(solution)/shard_map/ffn_forward/pallas_call | solution.py:560
  295.6 16.9 %all-gather.11.cloned.1.call-done.mine_ref.gate_ref = bf16[2048,1024]{1,0:T(8,128)(2,1)} async-done(((bf16[512,1024]{1,0:T(8,128)(2,1)}), bf16[2048,1024]{1,0:T(8,128)(2,1)}) %all-gather.11.cloned.1.call-update) | async-done | bytes 4194320 | tf_op jit(solution)/shard_map/all_gather | solution.py:1226
  312.5 9.8 %ffn_gate.1.mine_ref.refs_1_ = bf16[1024,1024]{1,0:T(8,128)(2,1)} custom-call(s32[2]{0:T(128)} %pad_add_fusion.refs_9_.refs_0_.place_ref, bf16[1024,2048]{1,0:T(8,128)(2,1)} %get-tuple-element.85.recept_ref.refs_4_, bf16[4,160,2048]{2,1,0:T(8,128)(2,1)} %copy-done.2, bf16[4,160,2048]{2,1,0:T(8,128)(2,1)} %collective-permute-done.9.other_ref.refs_0_, ...), custom_call_target="tpu_custom_call" | custom-call | tf_op jit(solution)/shard_map/ffn_gate/pallas_call | solution.py:611
  328.3 9.2 %grad_halves.1.refs_6_ = bf16[2048,896]{1,0:T(8,128)(2,1)} custom-call(s32[2]{0:T(128)} %pad_add_fusion.refs_9_.refs_0_.place_ref, bf16[1024,1024]{1,0:T(8,128)(2,1)} %ffn_gate.1.mine_ref.refs_1_, bf16[1024,1024]{1,0:T(8,128)(2,1)} %copy-done.6, bf16[1024,896]{1,0:T(8,128)(2,1)} %get-tuple-element.87.d_ref), custom_call_target="tpu_custom_call" | custom-call | tf_op jit(solution)/shard_map/grad_halves/pallas_call | solution.py:729
  337.5 6.1 all-to-all-done.2.blocks_ref.refs_5_
  343.7 17.0 %ffn_backward.1 = (bf16[1024,896]{1,0:T(8,128)(2,1)}, bf16[512,2048]{1,0:T(8,128)(2,1)}, bf16[512,2048]{1,0:T(8,128)(2,1)}) custom-call(s32[2]{0:T(128)} %pad_add_fusion.refs_9_.refs_0_.place_ref, bf16[1024,1024]{1,0:T(8,128)(2,1)} %ffn_gate.1.mine_ref.refs_1_, bf16[1024,1024]{1,0:T(8,128)(2,1)} %copy-done.6, f32[1024,896]{1,0:T(8,128)} %get-tuple-element.86.refs_3_, ...), custom_call_target="tpu_custom_call" | custom-call | tf_op jit(solution)/shard_map/ffn_backward/pallas_call | solution.py:668
  361.9 6.1 collective-permute-done.11.b_ref
  379.3 11.1 %ffn_local.1 = (bf16[128,2048]{1,0:T(8,128)(2,1)}, bf16[8,128,256]{2,1,0:T(8,128)(2,1)}, f32[128,2048]{1,0:T(8,128)}) custom-call(s32[2]{0:T(128)} %pad_add_fusion.refs_9_.refs_0_.place_ref, bf16[128,2048]{1,0:T(8,128)(2,1)} %add_convert_fusion.recept_ref, bf16[4,128,2048]{2,1,0:T(8,128)(2,1)} %all-to-all-done.2.blocks_ref.refs_5_, ...), custom_call_target="tpu_custom_call" | custom-call | tf_op jit(solution)/shard_map/ffn_local/pallas_call | solution.py:855
  390.4 34.9 %all-to-all-done.3 = bf16[4,128,2048]{2,1,0:T(8,128)(2,1)} async-done(((bf16[4,128,2048]{2,1,0:T(8,128)(2,1)}), bf16[4,128,2048]{2,1,0:T(8,128)(2,1)}, u32[]{:S(2)}, u32[]{:S(2)}) %all-to-all-start.3) | async-done | bytes 2097184 | tf_op jit(solution)/shard_map/all_to_all | solution.py:1043
  439.1 8.3 %grad.1.refs_1_ = bf16[2048,896]{1,0:T(8,128)(2,1)} custom-call(bf16[1024,2048]{1,0:T(8,128)(2,1)} %get-tuple-element.92.x_ref, bf16[1024,896]{1,0:T(8,128)(2,1)} %get-tuple-element.93.d_ref, bf16[128,2048]{1,0:T(8,128)(2,1)} %get-tuple-element.177.refs_0_), custom_call_target="tpu_custom_call" | custom-call | tf_op jit(solution)/shard_map/grad/pallas_call | solution.py:695
  450.4 37.8 %all-gather.13.cloned.1.call-done.d_ref.refs_11_ = bf16[1024,2048]{1,0:T(8,128)(2,1)} async-done(((bf16[128,2048]{1,0:T(8,128)(2,1)}), bf16[1024,2048]{1,0:T(8,128)(2,1)}) %all-gather.13.cloned.1.call-update) | async-done | bytes 4194320 | tf_op jit(solution)/shard_map/all_gather | solution.py:1030
  495.0 27.0 %wkv_backward.1 = (f32[32,256]{1,0:T(8,128)}, f32[64,256]{1,0:T(8,128)}, bf16[1024,256]{1,0:T(8,128)(2,1)}, bf16[1024,256]{1,0:T(8,128)(2,1)}, bf16[1024,256]{1,...) custom-call(s32[2]{0:T(128)} %pad_add_fusion.refs_9_.refs_0_.place_ref, ...), custom_call_target="tpu_custom_call" | custom-call | tf_op jit(solution)/shard_map/wkv_backward/pallas_call | solution.py:977
  522.8 16.3 %grads.1.refs_20_ = bf16[4,6,512,256]{3,2,1,0:T(8,128)(2,1)} custom-call(bf16[1024,2048]{1,0:T(8,128)(2,1)} %get-tuple-element.110.refs_0_, bf16[1024,2048]{1,0:T(8,128)(2,1)} %get-tuple-element.111.refs_1_, bf16[1024,2048]{1,0:T(8,128)(2,1)} %get-tuple-element.112.refs_2_, bf16[1024,2048]{1,0:T(8,128)(2,1)} %get-tuple-element.113.refs_3_, ...), custom_call_target="tpu_custom_call" | custom-call | tf_op jit(solution)/shard_map/grads/pallas_call | solution.py:772
  541.9 48.3 %mix_backward.1 = (bf16[480,2048]{1,0:T(8,128)(2,1)}, bf16[512,2048]{1,0:T(8,128)(2,1)}, bf16[512,2048]{1,0:T(8,128)(2,1)}) custom-call(s32[2]{0:T(128)} %pad_add_fusion.refs_9_.refs_0_.place_ref, bf16[1024,2048]{1,0:T(8,128)(2,1)} %bitcast.138, bf16[1024,2048]{1,0:T(8,128)(2,1)} %bitcast.139, f32[24,2048]{1,0:T(8,128)} %copy-done.21, ...), custom_call_target="tpu_custom_call" | custom-call | tf_op jit(solution)/shard_map/mix_backward/pallas_call | solution.py:1010
  610.5 5.7 collective-permute-done.16
  618.6 31.3 %collective-permute-done.15 = bf16[128,2048]{1,0:T(8,128)(2,1)S(1)} collective-permute-done((bf16[128,2048]{1,0:T(8,128)(2,1)}, bf16[128,2048]{1,0:T(8,128)(2,1)S(1)}, u32[]{:S(2)}, u32[]{:S(2)}) %collective-permute-start.15) | collective-permute-done | bytes 524320 | tf_op jit(solution)/shard_map/ppermute | solution.py:1057
  694.5 27.1 %collective-permute-done.20 = bf16[64,2048]{1,0:T(8,128)(2,1)S(1)} collective-permute-done((bf16[64,2048]{1,0:T(8,128)(2,1)S(1)}, bf16[64,2048]{1,0:T(8,128)(2,1)S(1)}, u32[]{:S(2)}, u32[]{:S(2)}) %collective-permute-start.20) | collective-permute-done | bytes 262176 | tf_op jit(solution)/shard_map/ppermute | solution.py:1305
  (252 shorter events, 191.1 us)
Async XLA Ops:
  7.2 59.1 %all-gather.15.cloned.1.call-start = ((), (), s32[]{:S(2)}) async-start(), calls=%async_computation.17 | async-start | bytes 4718592 | tf_op jit(solution)/shard_map/all_gather | solution.py:1030
  8.0 150.5 %all-gather.7.cloned.1.call-start = ((), (), s32[]{:S(2)}) async-start(), calls=%async_computation.10 | async-start | bytes 9175040 | tf_op jit(solution)/shard_map/all_gather | solution.py:1174
  13.4 46.2 %collective-permute-start.1 = (bf16[512,1024]{1,0:T(8,128)(2,1)S(1)}, bf16[512,1024]{1,0:T(8,128)(2,1)}, u32[]{:S(2)}, u32[]{:S(2)}) collective-permute-start(bf16[512,1024]{1,0:T(8,128)(2,1)S(1)} %pad_maximum_fusion.1.refs_10_.refs_16_), channel_id=1, source_target_pairs={{0,16},{8,24},{16,0},{24,8},{1,17},{9,25},{17,1},{25,9},{2,18},{10... | collective-permute-start | bytes 3145736 | tf_op jit(solution)/shard_map/ppermute | solution.py:1148
  13.6 47.8 %collective-permute-start = (bf16[512,1024]{1,0:T(8,128)(2,1)S(1)}, bf16[512,1024]{1,0:T(8,128)(2,1)}, u32[]{:S(2)}, u32[]{:S(2)}) collective-permute-start(bf16[512,1024]{1,0:T(8,128)(2,1)S(1)} %pad_maximum_fusion.1.refs_10_.refs_16_), channel_id=1, source_target_pairs={{0,8},{8,0},{16,24},{24,16},{1,9},{9,1},{17,25},{25,17},{2,10},{10... | collective-permute-start | bytes 3145736 | tf_op jit(solution)/shard_map/ppermute | solution.py:1148
  70.2 63.7 %all-to-all-start = ((bf16[4,160,2048]{2,1,0:T(8,128)(2,1)}), bf16[4,160,2048]{2,1,0:T(8,128)(2,1)S(1)}, u32[]{:S(2)}, u32[]{:S(2)}) async-start(bf16[4,160,2048]{2,1,0:T(8,128)(2,1)} %pad_maximum_fusion), calls=%async_computation | async-start | bytes 5242880 | tf_op jit(solution)/shard_map/all_to_all | solution.py:1184
  77.6 42.8 %collective-permute-start.3 = (bf16[256,2048]{1,0:T(8,128)(2,1)}, bf16[256,2048]{1,0:T(8,128)(2,1)}, u32[]{:S(2)}, u32[]{:S(2)}) collective-permute-start(bf16[256,2048]{1,0:T(8,128)(2,1)} %dynamic-slice_add_fusion.1.own_ref), channel_id=1, source_target_pairs={{0,8},{1,9},{10,2},{11,3},{20,28},{21,29},{30,22},{31,23}} | collective-permute-start | bytes 3145736 | tf_op jit(solution)/shard_map/ppermute | solution.py:1170
  79.2 41.2 %collective-permute-start.4 = (bf16[256,2048]{1,0:T(8,128)(2,1)}, bf16[256,2048]{1,0:T(8,128)(2,1)}, u32[]{:S(2)}, u32[]{:S(2)}) collective-permute-start(bf16[256,2048]{1,0:T(8,128)(2,1)} %dynamic-slice_add_fusion.1.own_ref), channel_id=1, source_target_pairs={{0,16},{1,17},{10,26},{11,27},{20,4},{21,5},{30,14},{31,15}} | collective-permute-start | bytes 3145736 | tf_op jit(solution)/shard_map/ppermute | solution.py:1170
  80.5 39.9 %collective-permute-start.5 = (bf16[256,2048]{1,0:T(8,128)(2,1)}, bf16[256,2048]{1,0:T(8,128)(2,1)}, u32[]{:S(2)}, u32[]{:S(2)}) collective-permute-start(bf16[256,2048]{1,0:T(8,128)(2,1)} %dynamic-slice_add_fusion.1.own_ref), channel_id=1, source_target_pairs={{0,24},{1,25},{10,18},{11,19},{20,12},{21,13},{30,6},{31,7}} | collective-permute-start | bytes 3145736 | tf_op jit(solution)/shard_map/ppermute | solution.py:1170
  153.3 52.3 %all-to-all-start.1 = ((bf16[4,128,2048]{2,1,0:T(8,128)(2,1)}), bf16[4,128,2048]{2,1,0:T(8,128)(2,1)S(1)}, u32[]{:S(2)}, u32[]{:S(2)}) async-start(bf16[4,128,2048]{2,1,0:T(8,128)(2,1)} %bitcast.144), calls=%async_computation.1 | async-start | bytes 4194304 | tf_op jit(solution)/shard_map/all_to_all | solution.py:1043
  157.7 99.3 %all-gather.9.cloned.1.call-start = ((), (), s32[]{:S(2)}) async-start(), calls=%async_computation.11 | async-start | bytes 4718592 | tf_op jit(solution)/shard_map/all_gather | solution.py:1030
  211.1 101.3 %all-gather.11.cloned.1.call-start = ((), (), s32[]{:S(2)}) async-start(), calls=%async_computation.12 | async-start | bytes 5242880 | tf_op jit(solution)/shard_map/all_gather | solution.py:1226
  291.1 52.6 %all-to-all-start.2 = ((bf16[4,128,2048]{2,1,0:T(8,128)(2,1)}), bf16[4,128,2048]{2,1,0:T(8,128)(2,1)}, u32[]{:S(2)}, u32[]{:S(2)}) async-start(bf16[4,128,2048]{2,1,0:T(8,128)(2,1)} %bitcast.140), calls=%async_computation.2 | async-start | bytes 4194304 | tf_op jit(solution)/shard_map/all_to_all | solution.py:1043
  295.6 138.9 %reduce-scatter.4.cloned.1.call-start = ((), (), s32[]{:S(2)}) async-start(), calls=%async_computation.13 | async-start | bytes 4587520 | tf_op jit(solution)/shard_map/reduce_scatter | solution.py:1159
  372.7 52.6 %all-to-all-start.3 = ((bf16[4,128,2048]{2,1,0:T(8,128)(2,1)}), bf16[4,128,2048]{2,1,0:T(8,128)(2,1)}, u32[]{:S(2)}, u32[]{:S(2)}) async-start(bf16[4,128,2048]{2,1,0:T(8,128)(2,1)} %bitcast.143), calls=%async_computation.3 | async-start | bytes 4194304 | tf_op jit(solution)/shard_map/all_to_all | solution.py:1043
  377.3 110.9 %all-gather.13.cloned.1.call-start = ((), (), s32[]{:S(2)}) async-start(), calls=%async_computation.14 | async-start | bytes 4718592 | tf_op jit(solution)/shard_map/all_gather | solution.py:1030
  439.0 223.2 %reduce-scatter.8.cloned.1.call-start = ((), (), s32[]{:S(2)}) async-start(), calls=%async_computation.16 | async-start | bytes 4587520 | tf_op jit(solution)/shard_map/reduce_scatter | solution.py:1159
  495.0 174.7 %reduce-scatter.6.cloned.1.call-start = ((), (), s32[]{:S(2)}) async-start(), calls=%async_computation.15 | async-start | bytes 7864320 | tf_op jit(solution)/shard_map/reduce_scatter | solution.py:1159
  604.8 45.1 %collective-permute-start.15 = (bf16[128,2048]{1,0:T(8,128)(2,1)}, bf16[128,2048]{1,0:T(8,128)(2,1)S(1)}, u32[]{:S(2)}, u32[]{:S(2)}) collective-permute-start(bf16[128,2048]{1,0:T(8,128)(2,1)} %get-tuple-element.118), channel_id=1, source_target_pairs={{0,2},{1,3},{2,0},{3,1},{4,6},{5,7},{6,4},{7,5},{8,10},{9,11},{10,... | collective-permute-start | bytes 1572872 | tf_op jit(solution)/shard_map/ppermute | solution.py:1057
  604.8 46.3 %collective-permute-start.14 = (bf16[128,2048]{1,0:T(8,128)(2,1)}, bf16[128,2048]{1,0:T(8,128)(2,1)S(1)}, u32[]{:S(2)}, u32[]{:S(2)}) collective-permute-start(bf16[128,2048]{1,0:T(8,128)(2,1)} %get-tuple-element.117), channel_id=1, source_target_pairs={{0,1},{1,2},{2,3},{3,0},{4,5},{5,6},{6,7},{7,4},{8,9},{9,10},{10,1... | collective-permute-start | bytes 1572872 | tf_op jit(solution)/shard_map/ppermute | solution.py:1057
  608.0 44.2 %collective-permute-start.19 = (bf16[480,512]{1,0:T(8,128)(2,1)}, bf16[480,512]{1,0:T(8,128)(2,1)}, u32[]{:S(2)}, u32[]{:S(2)}) collective-permute-start(bf16[480,512]{1,0:T(8,128)(2,1)} %get-tuple-element.191), channel_id=1, source_target_pairs={{0,24},{8,16},{16,8},{24,0},{1,25},{9,17},{17,9},{25,1},{2,26},{10... | collective-permute-start | bytes 1474568 | tf_op jit(solution)/shard_map/ppermute | solution.py:1156
  610.1 42.2 %collective-permute-start.18 = (bf16[480,512]{1,0:T(8,128)(2,1)}, bf16[480,512]{1,0:T(8,128)(2,1)}, u32[]{:S(2)}, u32[]{:S(2)}) collective-permute-start(bf16[480,512]{1,0:T(8,128)(2,1)} %get-tuple-element.192), channel_id=1, source_target_pairs={{0,16},{8,24},{16,0},{24,8},{1,17},{9,25},{17,1},{25,9},{2,18},{10... | collective-permute-start | bytes 1474568 | tf_op jit(solution)/shard_map/ppermute | solution.py:1156
  616.1 36.2 %collective-permute-start.17 = (bf16[480,512]{1,0:T(8,128)(2,1)S(1)}, bf16[480,512]{1,0:T(8,128)(2,1)}, u32[]{:S(2)}, u32[]{:S(2)}) collective-permute-start(bf16[480,512]{1,0:T(8,128)(2,1)S(1)} %get-tuple-element.190), channel_id=1, source_target_pairs={{0,8},{8,0},{16,24},{24,16},{1,9},{9,1},{17,25},{25,17},{2,10},{10... | collective-permute-start | bytes 1474568 | tf_op jit(solution)/shard_map/ppermute | solution.py:1156
  674.8 47.7 %all-to-all-start.6 = ((bf16[8,320,256]{2,1,0:T(8,128)(2,1)}), bf16[8,320,256]{2,1,0:T(8,128)(2,1)S(1)}, u32[]{:S(2)}, u32[]{:S(2)}) async-start(bf16[8,320,256]{2,1,0:T(8,128)(2,1)} %bitcast.68), calls=%async_computation.8 | async-start | bytes 2621440 | tf_op jit(solution)/shard_map/all_to_all | solution.py:1311
  687.1 34.5 %collective-permute-start.20 = (bf16[64,2048]{1,0:T(8,128)(2,1)S(1)}, bf16[64,2048]{1,0:T(8,128)(2,1)S(1)}, u32[]{:S(2)}, u32[]{:S(2)}) collective-permute-start(bf16[64,2048]{1,0:T(8,128)(2,1)S(1)} %bitcast.175), channel_id=1, source_target_pairs={{0,0},{1,4},{2,8},{3,12},{4,16},{5,20},{6,24},{7,28},{8,1},{9,5},{... | collective-permute-start | bytes 786440 | tf_op jit(solution)/shard_map/ppermute | solution.py:1305
  (53 other events, 604.9 us)
Sparse Core Ops, SparseCore 0:
  9.7 49.6 all-gather.14
  65.2 91.6 all-gather.6
  211.3 45.7 all-gather.8
  261.4 51.0 all-gather.10
  337.7 48.0 reduce-scatter.3
  439.2 48.9 all-gather.12
  491.1 46.6 reduce-scatter.7
  540.8 70.2 reduce-scatter.5

commit v5 on v4

--- a/solution.py
+++ b/solution.py
@@ -15,7 +15,7 @@
 BF16 = jnp.bfloat16
 CHUNK = 256
 TOKENS = 128
-VMEM = 56 * 2**20
+VMEM = 62 * 2**20
 
 
 def dot(a, b, dims):
@@ -219,23 +219,23 @@
     gated_ref[c, :] = (grouped * graw * jax.nn.sigmoid(graw)).astype(BF16)
 
 
-def state_cotangent(place_ref, mine_ref, other_ref, own):
+def state_cotangent(place_ref, mine_ref, other_ref, own, i):
     if mine_ref.dtype == F32:
-        return mine_ref[0]
+        return mine_ref[i]
     tile = pl.num_programs(0) - 1 - pl.program_id(0)
     is_mine = tile // (pl.num_programs(0) // 2) == place_ref[1]
     wide = 2 * own
     parts = []
     for at in range(0, mine_ref.shape[2], wide):
         q = pl.ds(pl.multiple_of(place_ref[1] * own + at, own), own)
-        parts.append(jnp.where(is_mine, mine_ref[0, :, q].astype(F32), other_ref[0, :, q].astype(F32)))
+        parts.append(jnp.where(is_mine, mine_ref[i, :, q].astype(F32), other_ref[i, :, q].astype(F32)))
     both = jnp.concatenate(parts, 0)
     return both[:HEAD] + both[HEAD:]
 
 
 def wkv_backward(
     place_ref, d_ref, r_ref, k_ref, v_ref, w_ref, graw_ref, wkv_ref, dm_ref, w_out_ref, own_ref, ones_ref, sums_ref,
-    start_ref, ends_ref, adj_ref, *refs,
+    start_ref, ends_ref, earlier_ref, adj_ref, *refs,
 ):
     own_sums_ref, decay_up_ref, dr_ref, dk_ref, dv_ref, dg_ref, dpre_ref, state_ref = refs[-8:]
     step = pl.program_id(0)
@@ -259,12 +259,33 @@
     d_normed = d_grouped * gain
     do = scale * (d_normed - head_sum(d_normed, ones) / HEAD - normed * (head_sum(d_normed * normed, ones) / HEAD))
 
-    rb, kb, vb, dob = r_ref[...], k_ref[...], v_ref[...], do.astype(BF16)
-    r, k, v, w = rb.astype(F32), kb.astype(F32), vb.astype(F32), w_ref[...]
+    dob = do.astype(BF16)
+    for i in reversed(range(length // TOKENS)):
+        c = slice(i * TOKENS, (i + 1) * TOKENS)
+        before = ends_ref[i - 1] if i else jnp.where(
+            step == pl.num_programs(0) - 1, start_ref[...], earlier_ref[length // TOKENS - 1]
+        )
+        d_end = spread(state_cotangent(place_ref, adj_ref, refs[0], own, i), ones.astype(F32))
+        one_chunk_backward(
+            c, r_ref, k_ref, v_ref, w_ref, do[c, :], dob[c, :], before, d_end, heads, ones, reward, sums_ref,
+            dr_ref, dk_ref, dv_ref, dpre_ref, own_sums_ref, state_ref,
+        )
+    decay_up_ref[...] += tn(dm_ref[...], dpre_ref[...])
+    for i, part in enumerate((d_grouped * normed, d_grouped)):
+        own_sums_ref[8 * i + 16 : 8 * i + 24, :] += fold(part)
+
+
+def one_chunk_backward(
+    c, r_ref, k_ref, v_ref, w_ref, do, dob, before_state, d_end, heads, ones, reward, sums_ref,
+    dr_ref, dk_ref, dv_ref, dpre_ref, own_sums_ref, state_ref,
+):
+    rb, kb, vb = r_ref[c, :], k_ref[c, :], v_ref[c, :]
+    length = rb.shape[0]
+    same = ones.astype(F32)
+    r, k, v, w = rb.astype(F32), kb.astype(F32), vb.astype(F32), w_ref[c, :]
     levels, before, after, total = pyramid(w)
-    same = ones.astype(F32)
-    d_state = state_ref[...] + spread(state_cotangent(place_ref, adj_ref, refs[0], own), same)
-    state = spread(jnp.where(step == pl.num_programs(0) - 1, start_ref[...], ends_ref[0]), same)
+    d_state = state_ref[...] + d_end
+    state = spread(before_state, same)
     d_flat, flat = d_state.astype(BF16), state.astype(BF16)
     from_start, to_end, decay = jnp.exp(before), jnp.exp(after), jnp.exp(total[0:1, :])
     dr = from_start * nn(dob, flat)
@@ -305,10 +326,9 @@
     dv = dv + head_sum(r * reward * k, ones) * do
     d_log = whole + nn(sums_ref[...], jnp.concatenate([q.astype(BF16) for q in through], 0))
     d_pre = d_log * w
-    dr_ref[...], dk_ref[...], dv_ref[...] = dr.astype(BF16), dk.astype(BF16), dv.astype(BF16)
-    dpre_ref[...] = d_pre
-    decay_up_ref[...] += tn(dm_ref[...], d_pre)
-    for i, part in enumerate((d_pre, r * k * met, d_grouped * normed, d_grouped)):
+    dr_ref[c, :], dk_ref[c, :], dv_ref[c, :] = dr.astype(BF16), dk.astype(BF16), dv.astype(BF16)
+    dpre_ref[c, :] = d_pre
+    for i, part in enumerate((d_pre, r * k * met)):
         own_sums_ref[8 * i : 8 * i + 8, :] += fold(part)
 
 
@@ -963,17 +983,17 @@
     tile = lambda n: pl.BlockSpec((length, n), lambda t, place: (count - 1 - t, 0))
     fixed = lambda a: pl.BlockSpec(a.shape, lambda t, place: (0, 0))
     shape = lambda dtype: jax.ShapeDtypeStruct((tokens, cw), dtype)
-    wide = dm.shape[1]
+    wide, per = dm.shape[1], length // TOKENS
 
     def folded(a, core):
-        rows = a.shape[1] - length
+        rows = a.shape[1] - TOKENS
         at = lambda t, place: jnp.clip(count - 1 - t - core(place) * (count // 2), 0, count // 2 - 1)
-        return pl.BlockSpec((1, rows, a.shape[2]), lambda t, place: (at(t, place), length // rows, 0))
+        return pl.BlockSpec((per, rows, a.shape[2]), lambda t, place: (at(t, place), TOKENS // rows, 0))
 
     if len(adjoints) == 2:
         states = [folded(adjoints[0], lambda place: place[1]), folded(adjoints[1], lambda place: 1 - place[1])]
     else:
-        states = [pl.BlockSpec((1, HEAD, cw), lambda t, place: (count - 1 - t, 0, 0))]
+        states = [pl.BlockSpec((per, HEAD, cw), lambda t, place: (count - 1 - t, 0, 0))]
     return pl.pallas_call(
         wkv_backward,
         grid_spec=pltpu.PrefetchScalarGridSpec(
@@ -981,7 +1001,8 @@
             grid=(count,),
             in_specs=[tile(d.shape[1])] + [tile(cw)] * 6 + [tile(wide)]
             + [fixed(a) for a in (w_out, own, ones, sums, start)]
-            + [pl.BlockSpec((1, HEAD, cw), lambda t, place: (jnp.maximum(count - 2 - t, 0), 0, 0))]
+            + [pl.BlockSpec((per, HEAD, cw), lambda t, place: (count - 1 - t, 0, 0))]
+            + [pl.BlockSpec((per, HEAD, cw), lambda t, place: (jnp.maximum(count - 2 - t, 0), 0, 0))]
             + states + pinned(pins),
             out_specs=[pl.BlockSpec((32, cw), lambda t, place: (0, 0)), pl.BlockSpec((wide, cw), lambda t, place: (0, 0))]
             + [tile(cw)] * 5,
@@ -992,7 +1013,7 @@
         compiler_params=params(),
         cost_estimate=light(),
         name="wkv_backward",
-    )(place, d, r, k, v, w, graw, wkv, dm, w_out, own, ones, sums, start, ends, *adjoints, *pins)
+    )(place, d, r, k, v, w, graw, wkv, dm, w_out, own, ones, sums, start, ends, ends, *adjoints, *pins)
 
 
 def call_mix_backward(
@@ -1283,7 +1304,7 @@
     d_gate_own = moved[:, :length].reshape(tokens, cw)
     end_states = moved[:, length : length + HEAD].astype(F32) + moved[:, length + HEAD :].astype(F32)
     own_sums, decay_up, dr, dk, dv, dg, d_pre = call_wkv_backward(
-        length, d_att, r, k, v, w, graw, wkv, dm, w_out, own, ones, sum_table(length), start, ends, adjoints, place,
+        2 * length, d_att, r, k, v, w, graw, wkv, dm, w_out, own, ones, sum_table(length), start, ends, adjoints, place,
         [grad_ffn_key],
     )
     grads = call_grads([xr, xk, xv, xg, recept_all], [dr, dk, dv, dg, d_gate_own], gated, d_att, segs, ())

time: 740 us -> 728 us (0.984)
  local copies, waits for them, and re-layouts: 53.2 us -> 42.7 us
    unnamed x83 -> x77, local copies, waits for them, and re-layouts: 19.2 us -> 9.78 us
  transfers between devices with their start and end apart: 38 -> 38, of which waited for: 19 -> 21; matrix products, arithmetic and copies ran while one was open for 9% -> 9% of each run, Pallas kernels for 30% -> 30%
where the time goes in v5:
time: 728 us; the launch traced here: 722 us
  waiting for transfers between devices  341 us (47%)
  Pallas kernels  223 us (31%)
  starting transfers between devices  56.7 us (8%)
  local copies, waits for them, and re-layouts  42.7 us (6%)
  other arithmetic  36.5 us (5%)
  between operations  22.5 us (3%)
    all_to_all x3, waiting for transfers between devices, reduce_chan(): lax.all_to_all(total.reshape(chans, -1, total.shape[1]), 'chan', 0, 0, ti...  87.5 us
    all_gather x3, waiting for transfers between devices, gather_group(): return lax.all_gather(block, TP, axis=0, tiled=True)  84.2 us
    pallas_call x1, Pallas kernels, call_mix_backward(): pl.pallas_call(lambda *refs: mix_backward(rank, len(specs), *refs), grid_...  48.6 us
    ppermute x3, waiting for transfers between devices, seg_parts(): return [a] + [lax.ppermute(a, 'seg', flips[m]) for m in range(1, segs)]  43 us
    ppermute x3, waiting for transfers between devices, reduce_apart(): lax.ppermute(a, 'chan', [(i, (i + k + 1) % chans) for i in range(chans)])  36.7 us
    pallas_call x1, Pallas kernels, call_forward(): pl.pallas_call(lambda *refs: mix_forward(rank, *refs), grid=(count,), in_...  31.6 us
    ppermute x1, waiting for transfers between devices, on_device(): lax.ppermute(grad_out, ALL, [(i * group + j, segs * j + i) for i in range...  27.1 us
    pallas_call x1, Pallas kernels, call_wkv_backward(): pl.pallas_call(wkv_backward, grid_spec=pltpu.PrefetchScalarGridSpec(num_s...  23.3 us
  transfers between devices with their start and end apart: 38, of which 21 were waited for; matrix products, arithmetic and copies ran while one was open for 9% of the time, Pallas kernels for 30%

profile of v5, /device:TPU:1, one launch (start us, length us, event | category | flops | bytes accessed | tf_op | source)
XLA Modules:
  0.0 722.5 jit_solution(6149960822387325502)
XLA Ops:
  15.3 21.1 %collective-permute-done.2.refs_13_.refs_19_ = bf16[512,1024]{1,0:T(8,128)(2,1)S(1)} collective-permute-done((bf16[512,1024]{1,0:T(8,128)(2,1)S(1)}, bf16[512,1024]{1,0:T(8,128)(2,1)S(1)}, u32[]{:S(2)}, u32[]{:S(2)}) %collective-permute-start.2) | collective-permute-done | bytes 1048608 | tf_op jit(solution)/shard_map/ppermute | solution.py:1169
  37.6 22.0 %collective-permute-done.1.refs_12_.refs_18_ = bf16[512,1024]{1,0:T(8,128)(2,1)} collective-permute-done((bf16[512,1024]{1,0:T(8,128)(2,1)S(1)}, bf16[512,1024]{1,0:T(8,128)(2,1)}, u32[]{:S(2)}, u32[]{:S(2)}) %collective-permute-start.1) | collective-permute-done | bytes 1048608 | tf_op jit(solution)/shard_map/ppermute | solution.py:1169
  87.4 31.6 %mix_forward.1 = (bf16[1024,256]{1,0:T(8,128)(2,1)}, bf16[1024,2048]{1,0:T(8,128)(2,1)}, bf16[1024,2048]{1,0:T(8,128)(2,1)}, bf16[1024,2048]{1,0:T(8,128)(2,1)},...) custom-call(bf16[1024,2048]{1,0:T(8,128)(2,1)} %bitcast.137, ...), custom_call_target="tpu_custom_call" | custom-call | tf_op jit(solution)/shard_map/mix_forward/pallas_call | solution.py:489
  119.0 16.1 %all-to-all-done.refs_3_.mine_ref.adj_ref = bf16[4,160,2048]{2,1,0:T(8,128)(2,1)} async-done(((bf16[4,160,2048]{2,1,0:T(8,128)(2,1)}), bf16[4,160,2048]{2,1,0:T(8,128)(2,1)}, u32[]{:S(2)}, u32[]{:S(2)}) %all-to-all-start) | async-done | bytes 2621472 | tf_op jit(solution)/shard_map/all_to_all | solution.py:1205
  135.1 7.7 %out_projection.1 = (bf16[512,2048]{1,0:T(8,128)(2,1)}, bf16[512,2048]{1,0:T(8,128)(2,1)}, bf16[256,2048]{1,0:T(8,128)(2,1)}) custom-call(s32[3]{0:T(128)} %pad_add_fusion.1.place_ref, bf16[1024,256]{1,0:T(8,128)(2,1)} %get-tuple-element.73.gated_ref.refs_10_, bf16[256,2048]{1,0:T(8,128)(2,1)} %copy-done.11, ...), custom_call_target="tpu_custom_call" | custom-call | tf_op jit(solution)/shard_map/out_projection/pallas_call | solution.py:914
  157.3 47.2 %all-to-all-done.1.blocks_ref = bf16[4,128,2048]{2,1,0:T(8,128)(2,1)} async-done(((bf16[4,128,2048]{2,1,0:T(8,128)(2,1)}), bf16[4,128,2048]{2,1,0:T(8,128)(2,1)}, u32[]{:S(2)}, u32[]{:S(2)}) %all-to-all-start.1) | async-done | bytes 2097184 | tf_op jit(solution)/shard_map/all_to_all | solution.py:1064
  208.9 46.2 %all-gather.9.cloned.1.call-done.refs_1_.refs_2_ = bf16[1024,2048]{1,0:T(8,128)(2,1)} async-done(((bf16[128,2048]{1,0:T(8,128)(2,1)}), bf16[1024,2048]{1,0:T(8,128)(2,1)}) %all-gather.9.cloned.1.call-update) | async-done | bytes 4194320 | tf_op jit(solution)/shard_map/all_gather | solution.py:1051
  259.8 19.5 %ffn_forward.1 = (bf16[1024,2048]{1,0:T(8,128)(2,1)}, bf16[1024,2048]{1,0:T(8,128)(2,1)}, f32[1024,896]{1,0:T(8,128)}, bf16[1024,896]{1,0:T(8,128)(2,1)}, bf16[5...) custom-call(s32[2]{0:T(128)} %pad_add_fusion.refs_9_.refs_0_.place_ref, ...), custom_call_target="tpu_custom_call" | custom-call | tf_op jit(solution)/shard_map/ffn_forward/pallas_call | solution.py:580
  291.8 18.8 %all-gather.11.cloned.1.call-done.mine_ref.gate_ref = bf16[2048,1024]{1,0:T(8,128)(2,1)} async-done(((bf16[512,1024]{1,0:T(8,128)(2,1)}), bf16[2048,1024]{1,0:T(8,128)(2,1)}) %all-gather.11.cloned.1.call-update) | async-done | bytes 4194320 | tf_op jit(solution)/shard_map/all_gather | solution.py:1247
  310.6 9.8 %ffn_gate.1.mine_ref.refs_1_ = bf16[1024,1024]{1,0:T(8,128)(2,1)} custom-call(s32[2]{0:T(128)} %pad_add_fusion.refs_9_.refs_0_.place_ref, bf16[1024,2048]{1,0:T(8,128)(2,1)} %get-tuple-element.85.recept_ref.refs_4_, bf16[4,160,2048]{2,1,0:T(8,128)(2,1)} %all-to-all-done.refs_3_.mine_ref.adj_ref, ...), custom_call_target="tpu_custom_call" | custom-call | tf_op jit(solution)/shard_map/ffn_gate/pallas_call | solution.py:631
  325.3 9.3 %grad_halves.1.refs_6_ = bf16[2048,896]{1,0:T(8,128)(2,1)} custom-call(s32[2]{0:T(128)} %pad_add_fusion.refs_9_.refs_0_.place_ref, bf16[1024,1024]{1,0:T(8,128)(2,1)} %ffn_gate.1.mine_ref.refs_1_, bf16[1024,1024]{1,0:T(8,128)(2,1)} %collective-permute-done.10.other_ref.refs_2_, bf16[1024,896]{1,0:T(8,128)(2,1)} %get-tuple-element.87.d_ref), custom_call_target="tpu_custom_call" | custom-call | tf_op jit(solution)/shard_map/grad_halves/pallas_call | solution.py:749
  334.5 5.3 all-to-all-done.2.blocks_ref.refs_5_
  339.9 17.5 %ffn_backward.1 = (bf16[1024,896]{1,0:T(8,128)(2,1)}, bf16[512,2048]{1,0:T(8,128)(2,1)}, bf16[512,2048]{1,0:T(8,128)(2,1)}) custom-call(s32[2]{0:T(128)} %pad_add_fusion.refs_9_.refs_0_.place_ref, bf16[1024,1024]{1,0:T(8,128)(2,1)} %ffn_gate.1.mine_ref.refs_1_, bf16[1024,1024]{1,0:T(8,128)(2,1)} %collective-permute-done.10.other_ref.refs_2_, ...), custom_call_target="tpu_custom_call" | custom-call | tf_op jit(solution)/shard_map/ffn_backward/pallas_call | solution.py:688
  372.3 11.0 %ffn_local.1 = (bf16[128,2048]{1,0:T(8,128)(2,1)}, bf16[8,128,256]{2,1,0:T(8,128)(2,1)}, f32[128,2048]{1,0:T(8,128)}) custom-call(s32[2]{0:T(128)} %pad_add_fusion.refs_9_.refs_0_.place_ref, bf16[128,2048]{1,0:T(8,128)(2,1)} %add_convert_fusion.recept_ref, bf16[4,128,2048]{2,1,0:T(8,128)(2,1)} %all-to-all-done.2.blocks_ref.refs_5_, ...), custom_call_target="tpu_custom_call" | custom-call | tf_op jit(solution)/shard_map/ffn_local/pallas_call | solution.py:875
  383.3 35.0 %all-to-all-done.3 = bf16[4,128,2048]{2,1,0:T(8,128)(2,1)} async-done(((bf16[4,128,2048]{2,1,0:T(8,128)(2,1)}), bf16[4,128,2048]{2,1,0:T(8,128)(2,1)}, u32[]{:S(2)}, u32[]{:S(2)}) %all-to-all-start.3) | async-done | bytes 2097184 | tf_op jit(solution)/shard_map/all_to_all | solution.py:1064
  432.0 8.3 %grad.1.refs_1_ = bf16[2048,896]{1,0:T(8,128)(2,1)} custom-call(bf16[1024,2048]{1,0:T(8,128)(2,1)} %get-tuple-element.92.x_ref, bf16[1024,896]{1,0:T(8,128)(2,1)} %get-tuple-element.93.d_ref, bf16[128,2048]{1,0:T(8,128)(2,1)} %get-tuple-element.177.refs_0_), custom_call_target="tpu_custom_call" | custom-call | tf_op jit(solution)/shard_map/grad/pallas_call | solution.py:715
  443.3 37.9 %all-gather.13.cloned.1.call-done.d_ref.refs_11_ = bf16[1024,2048]{1,0:T(8,128)(2,1)} async-done(((bf16[128,2048]{1,0:T(8,128)(2,1)}), bf16[1024,2048]{1,0:T(8,128)(2,1)}) %all-gather.13.cloned.1.call-update) | async-done | bytes 4194320 | tf_op jit(solution)/shard_map/all_gather | solution.py:1051
  488.3 23.3 %wkv_backward.1 = (f32[32,256]{1,0:T(8,128)}, f32[64,256]{1,0:T(8,128)}, bf16[1024,256]{1,0:T(8,128)(2,1)}, bf16[1024,256]{1,0:T(8,128)(2,1)}, bf16[1024,256]{1,...) custom-call(s32[2]{0:T(128)} %pad_add_fusion.refs_9_.refs_0_.place_ref, ...), custom_call_target="tpu_custom_call" | custom-call | tf_op jit(solution)/shard_map/wkv_backward/pallas_call | solution.py:997
  514.8 16.3 %grads.1.refs_20_ = bf16[4,6,512,256]{3,2,1,0:T(8,128)(2,1)} custom-call(bf16[1024,2048]{1,0:T(8,128)(2,1)} %get-tuple-element.110.refs_0_, bf16[1024,2048]{1,0:T(8,128)(2,1)} %get-tuple-element.111.refs_1_, bf16[1024,2048]{1,0:T(8,128)(2,1)} %get-tuple-element.112.refs_2_, bf16[1024,2048]{1,0:T(8,128)(2,1)} %get-tuple-element.113.refs_3_, ...), custom_call_target="tpu_custom_call" | custom-call | tf_op jit(solution)/shard_map/grads/pallas_call | solution.py:792
  533.8 48.6 %mix_backward.1 = (bf16[480,2048]{1,0:T(8,128)(2,1)}, bf16[512,2048]{1,0:T(8,128)(2,1)}, bf16[512,2048]{1,0:T(8,128)(2,1)}) custom-call(s32[2]{0:T(128)} %pad_add_fusion.refs_9_.refs_0_.place_ref, bf16[1024,2048]{1,0:T(8,128)(2,1)} %bitcast.138, bf16[1024,2048]{1,0:T(8,128)(2,1)} %bitcast.139, f32[24,2048]{1,0:T(8,128)} %copy-done.14, ...), custom_call_target="tpu_custom_call" | custom-call | tf_op jit(solution)/shard_map/mix_backward/pallas_call | solution.py:1031
  587.0 5.5 combine.1
  599.0 8.5 %collective-permute-done.16 = bf16[128,2048]{1,0:T(8,128)(2,1)S(1)} collective-permute-done((bf16[128,2048]{1,0:T(8,128)(2,1)}, bf16[128,2048]{1,0:T(8,128)(2,1)S(1)}, u32[]{:S(2)}, u32[]{:S(2)}) %collective-permute-start.16) | collective-permute-done | bytes 524320 | tf_op jit(solution)/shard_map/ppermute | solution.py:1078
  609.8 28.3 %collective-permute-done.15 = bf16[128,2048]{1,0:T(8,128)(2,1)S(1)} collective-permute-done((bf16[128,2048]{1,0:T(8,128)(2,1)}, bf16[128,2048]{1,0:T(8,128)(2,1)S(1)}, u32[]{:S(2)}, u32[]{:S(2)}) %collective-permute-start.15) | collective-permute-done | bytes 524320 | tf_op jit(solution)/shard_map/ppermute | solution.py:1078
  682.6 27.1 %collective-permute-done.20 = bf16[64,2048]{1,0:T(8,128)(2,1)S(1)} collective-permute-done((bf16[64,2048]{1,0:T(8,128)(2,1)S(1)}, bf16[64,2048]{1,0:T(8,128)(2,1)S(1)}, u32[]{:S(2)}, u32[]{:S(2)}) %collective-permute-start.20) | collective-permute-done | bytes 262176 | tf_op jit(solution)/shard_map/ppermute | solution.py:1326
  (246 shorter events, 178.1 us)
Async XLA Ops:
  7.2 60.2 %all-gather.15.cloned.1.call-start = ((), (), s32[]{:S(2)}) async-start(), calls=%async_computation.17 | async-start | bytes 4718592 | tf_op jit(solution)/shard_map/all_gather | solution.py:1051
  8.0 149.3 %all-gather.7.cloned.1.call-start = ((), (), s32[]{:S(2)}) async-start(), calls=%async_computation.10 | async-start | bytes 9175040 | tf_op jit(solution)/shard_map/all_gather | solution.py:1195
  13.4 46.2 %collective-permute-start.1 = (bf16[512,1024]{1,0:T(8,128)(2,1)S(1)}, bf16[512,1024]{1,0:T(8,128)(2,1)}, u32[]{:S(2)}, u32[]{:S(2)}) collective-permute-start(bf16[512,1024]{1,0:T(8,128)(2,1)S(1)} %pad_maximum_fusion.1.refs_10_.refs_16_), channel_id=1, source_target_pairs={{0,16},{8,24},{16,0},{24,8},{1,17},{9,25},{17,1},{25,9},{2,18},{10... | collective-permute-start | bytes 3145736 | tf_op jit(solution)/shard_map/ppermute | solution.py:1169
  13.6 47.8 %collective-permute-start = (bf16[512,1024]{1,0:T(8,128)(2,1)S(1)}, bf16[512,1024]{1,0:T(8,128)(2,1)}, u32[]{:S(2)}, u32[]{:S(2)}) collective-permute-start(bf16[512,1024]{1,0:T(8,128)(2,1)S(1)} %pad_maximum_fusion.1.refs_10_.refs_16_), channel_id=1, source_target_pairs={{0,8},{8,0},{16,24},{24,16},{1,9},{9,1},{17,25},{25,17},{2,10},{10... | collective-permute-start | bytes 3145736 | tf_op jit(solution)/shard_map/ppermute | solution.py:1169
  71.3 63.8 %all-to-all-start = ((bf16[4,160,2048]{2,1,0:T(8,128)(2,1)}), bf16[4,160,2048]{2,1,0:T(8,128)(2,1)}, u32[]{:S(2)}, u32[]{:S(2)}) async-start(bf16[4,160,2048]{2,1,0:T(8,128)(2,1)} %pad_maximum_fusion), calls=%async_computation | async-start | bytes 5242880 | tf_op jit(solution)/shard_map/all_to_all | solution.py:1205
  78.0 41.0 %collective-permute-start.3 = (bf16[256,2048]{1,0:T(8,128)(2,1)S(1)}, bf16[256,2048]{1,0:T(8,128)(2,1)}, u32[]{:S(2)}, u32[]{:S(2)}) collective-permute-start(bf16[256,2048]{1,0:T(8,128)(2,1)S(1)} %dynamic-slice_add_fusion.1.own_ref), channel_id=1, source_target_pairs={{0,8},{1,9},{10,2},{11,3},{20,28},{21,29},{30,22},{31,23}} | collective-permute-start | bytes 3145736 | tf_op jit(solution)/shard_map/ppermute | solution.py:1191
  79.6 39.4 %collective-permute-start.4 = (bf16[256,2048]{1,0:T(8,128)(2,1)S(1)}, bf16[256,2048]{1,0:T(8,128)(2,1)}, u32[]{:S(2)}, u32[]{:S(2)}) collective-permute-start(bf16[256,2048]{1,0:T(8,128)(2,1)S(1)} %dynamic-slice_add_fusion.1.own_ref), channel_id=1, source_target_pairs={{0,16},{1,17},{10,26},{11,27},{20,4},{21,5},{30,14},{31,15}} | collective-permute-start | bytes 3145736 | tf_op jit(solution)/shard_map/ppermute | solution.py:1191
  80.9 38.1 %collective-permute-start.5 = (bf16[256,2048]{1,0:T(8,128)(2,1)S(1)}, bf16[256,2048]{1,0:T(8,128)(2,1)}, u32[]{:S(2)}, u32[]{:S(2)}) collective-permute-start(bf16[256,2048]{1,0:T(8,128)(2,1)S(1)} %dynamic-slice_add_fusion.1.own_ref), channel_id=1, source_target_pairs={{0,24},{1,25},{10,18},{11,19},{20,12},{21,13},{30,6},{31,7}} | collective-permute-start | bytes 3145736 | tf_op jit(solution)/shard_map/ppermute | solution.py:1191
  151.9 52.7 %all-to-all-start.1 = ((bf16[4,128,2048]{2,1,0:T(8,128)(2,1)}), bf16[4,128,2048]{2,1,0:T(8,128)(2,1)}, u32[]{:S(2)}, u32[]{:S(2)}) async-start(bf16[4,128,2048]{2,1,0:T(8,128)(2,1)} %bitcast.144), calls=%async_computation.1 | async-start | bytes 4194304 | tf_op jit(solution)/shard_map/all_to_all | solution.py:1064
  156.5 98.7 %all-gather.9.cloned.1.call-start = ((), (), s32[]{:S(2)}) async-start(), calls=%async_computation.11 | async-start | bytes 4718592 | tf_op jit(solution)/shard_map/all_gather | solution.py:1051
  208.7 101.9 %all-gather.11.cloned.1.call-start = ((), (), s32[]{:S(2)}) async-start(), calls=%async_computation.12 | async-start | bytes 5242880 | tf_op jit(solution)/shard_map/all_gather | solution.py:1247
  287.3 52.6 %all-to-all-start.2 = ((bf16[4,128,2048]{2,1,0:T(8,128)(2,1)}), bf16[4,128,2048]{2,1,0:T(8,128)(2,1)}, u32[]{:S(2)}, u32[]{:S(2)}) async-start(bf16[4,128,2048]{2,1,0:T(8,128)(2,1)} %bitcast.140), calls=%async_computation.2 | async-start | bytes 4194304 | tf_op jit(solution)/shard_map/all_to_all | solution.py:1064
  291.7 135.6 %reduce-scatter.4.cloned.1.call-start = ((), (), s32[]{:S(2)}) async-start(), calls=%async_computation.13 | async-start | bytes 4587520 | tf_op jit(solution)/shard_map/reduce_scatter | solution.py:1180
  365.6 52.6 %all-to-all-start.3 = ((bf16[4,128,2048]{2,1,0:T(8,128)(2,1)}), bf16[4,128,2048]{2,1,0:T(8,128)(2,1)}, u32[]{:S(2)}, u32[]{:S(2)}) async-start(bf16[4,128,2048]{2,1,0:T(8,128)(2,1)} %bitcast.143), calls=%async_computation.3 | async-start | bytes 4194304 | tf_op jit(solution)/shard_map/all_to_all | solution.py:1064
  370.2 111.0 %all-gather.13.cloned.1.call-start = ((), (), s32[]{:S(2)}) async-start(), calls=%async_computation.14 | async-start | bytes 4718592 | tf_op jit(solution)/shard_map/all_gather | solution.py:1051
  431.9 218.4 %reduce-scatter.8.cloned.1.call-start = ((), (), s32[]{:S(2)}) async-start(), calls=%async_computation.16 | async-start | bytes 4587520 | tf_op jit(solution)/shard_map/reduce_scatter | solution.py:1180
  488.1 168.9 %reduce-scatter.6.cloned.1.call-start = ((), (), s32[]{:S(2)}) async-start(), calls=%async_computation.15 | async-start | bytes 7864320 | tf_op jit(solution)/shard_map/reduce_scatter | solution.py:1180
  592.8 45.4 %collective-permute-start.15 = (bf16[128,2048]{1,0:T(8,128)(2,1)}, bf16[128,2048]{1,0:T(8,128)(2,1)S(1)}, u32[]{:S(2)}, u32[]{:S(2)}) collective-permute-start(bf16[128,2048]{1,0:T(8,128)(2,1)} %get-tuple-element.118), channel_id=1, source_target_pairs={{0,2},{1,3},{2,0},{3,1},{4,6},{5,7},{6,4},{7,5},{8,10},{9,11},{10,... | collective-permute-start | bytes 1572872 | tf_op jit(solution)/shard_map/ppermute | solution.py:1078
  592.8 46.6 %collective-permute-start.14 = (bf16[128,2048]{1,0:T(8,128)(2,1)}, bf16[128,2048]{1,0:T(8,128)(2,1)S(1)}, u32[]{:S(2)}, u32[]{:S(2)}) collective-permute-start(bf16[128,2048]{1,0:T(8,128)(2,1)} %get-tuple-element.117), channel_id=1, source_target_pairs={{0,1},{1,2},{2,3},{3,0},{4,5},{5,6},{6,7},{7,4},{8,9},{9,10},{10,1... | collective-permute-start | bytes 1572872 | tf_op jit(solution)/shard_map/ppermute | solution.py:1078
  596.6 44.0 %collective-permute-start.19 = (bf16[480,512]{1,0:T(8,128)(2,1)}, bf16[480,512]{1,0:T(8,128)(2,1)}, u32[]{:S(2)}, u32[]{:S(2)}) collective-permute-start(bf16[480,512]{1,0:T(8,128)(2,1)} %get-tuple-element.191), channel_id=1, source_target_pairs={{0,24},{8,16},{16,8},{24,0},{1,25},{9,17},{17,9},{25,1},{2,26},{10... | collective-permute-start | bytes 1474568 | tf_op jit(solution)/shard_map/ppermute | solution.py:1177
  598.8 41.8 %collective-permute-start.18 = (bf16[480,512]{1,0:T(8,128)(2,1)}, bf16[480,512]{1,0:T(8,128)(2,1)}, u32[]{:S(2)}, u32[]{:S(2)}) collective-permute-start(bf16[480,512]{1,0:T(8,128)(2,1)} %get-tuple-element.192), channel_id=1, source_target_pairs={{0,16},{8,24},{16,0},{24,8},{1,17},{9,25},{17,1},{25,9},{2,18},{10... | collective-permute-start | bytes 1474568 | tf_op jit(solution)/shard_map/ppermute | solution.py:1177
  607.5 33.1 %collective-permute-start.17 = (bf16[480,512]{1,0:T(8,128)(2,1)}, bf16[480,512]{1,0:T(8,128)(2,1)}, u32[]{:S(2)}, u32[]{:S(2)}) collective-permute-start(bf16[480,512]{1,0:T(8,128)(2,1)} %get-tuple-element.190), channel_id=1, source_target_pairs={{0,8},{8,0},{16,24},{24,16},{1,9},{9,1},{17,25},{25,17},{2,10},{10... | collective-permute-start | bytes 1474568 | tf_op jit(solution)/shard_map/ppermute | solution.py:1177
  662.9 47.7 %all-to-all-start.6 = ((bf16[8,320,256]{2,1,0:T(8,128)(2,1)}), bf16[8,320,256]{2,1,0:T(8,128)(2,1)S(1)}, u32[]{:S(2)}, u32[]{:S(2)}) async-start(bf16[8,320,256]{2,1,0:T(8,128)(2,1)} %bitcast.68), calls=%async_computation.8 | async-start | bytes 2621440 | tf_op jit(solution)/shard_map/all_to_all | solution.py:1332
  675.2 34.5 %collective-permute-start.20 = (bf16[64,2048]{1,0:T(8,128)(2,1)S(1)}, bf16[64,2048]{1,0:T(8,128)(2,1)S(1)}, u32[]{:S(2)}, u32[]{:S(2)}) collective-permute-start(bf16[64,2048]{1,0:T(8,128)(2,1)S(1)} %bitcast.174), channel_id=1, source_target_pairs={{0,0},{1,4},{2,8},{3,12},{4,16},{5,20},{6,24},{7,28},{8,1},{9,5},{... | collective-permute-start | bytes 786440 | tf_op jit(solution)/shard_map/ppermute | solution.py:1326
  (50 other events, 608.9 us)
Sparse Core Ops, SparseCore 0:
  9.7 49.6 all-gather.14
  65.2 91.6 all-gather.6
  208.8 46.2 all-gather.8
  259.6 51.0 all-gather.10
  334.7 48.0 reduce-scatter.3
  432.1 49.1 all-gather.12
  484.2 46.6 reduce-scatter.7
  533.9 72.8 reduce-scatter.5
